TPU v7x, 32 devices: a whole 2x2x4 slice. The times are simulated.
32 devices in a mesh: section: 16 (over z, y, x), dp: 2 (over core).
Axes of the slice: x: 2, y: 2, z: 4, core: 2. Of those that a mesh axis runs over, the one named last changes fastest.
Arguments:
- act_down: bfloat16 [16, 2, 512, 1024], P('section', None, 'dp'), may hold values from -6 to 6
- act_up: bfloat16 [16, 2, 512, 1024], P('section', None, 'dp'), may hold values from -6 to 6
- grad_down: bfloat16 [16, 512, 1024], P('section', 'dp'), may hold values from -1.5 to 1.5
- grad_up: bfloat16 [16, 512, 1024], P('section', 'dp'), may hold values from -1.5 to 1.5
- seed_down: bfloat16 [512, 1024], P('dp'), may hold values from -1.5 to 1.5
- seed_up: bfloat16 [512, 1024], P('dp'), may hold values from -1.5 to 1.5
- gain_down: float32 [16, 1024], P('section'), as said below
- qkv_down: bfloat16 [16, 1024, 768], P('section'), as said below
- outproj_down: bfloat16 [16, 512, 1024], P('section'), as said below
- gain_up: float32 [16, 1024], P('section'), as said below
- qkv_up: bfloat16 [16, 1024, 768], P('section'), as said below
- outproj_up: bfloat16 [16, 512, 1024], P('section'), as said below
- doc_offsets: int32 [2, 16, 2, 2], P(None, 'section', None, 'dp'), may hold values from 1 to 255
- slot_order: int32 [2, 16, 2], P(None, 'section'), may hold values from 0 to 1, each once within a row
Outputs:
- input_grads: bfloat16 [2, 16, 2, 512, 1024], P(None, 'section', None, 'dp')
- grad_gain: float32 [16, 1024], P('section', 'dp')
- grad_qkv: float32 [16, 1024, 768], P('section', 'dp')
- grad_outproj: float32 [16, 512, 1024], P('section', 'dp')
Inputs may be any that keep to these rules, and one draw needn't show every extreme that they name: `gain_down`: the down copy of every layer. `qkv_down`: the down copy of every layer. `outproj_down`: the down copy of every layer. gain_up[s] equals gain_down[15 - s]. qkv_up[s] equals qkv_down[15 - s]. outproj_up[s] equals outproj_down[15 - s]. `doc_offsets`: each sequence holds two documents; the value is the position where the second begins. `slot_order`: each row of a direction and section names 0 and 1 once each.
All inputs are finite; a program needn't handle non-finite values.
Results may differ from a plain program's by a relative error of at most 0.015.
Values may be sent and summed in bfloat16 or wider, within the bound.
No kernel may reach another device: no remote copies, remote signals or barrier semaphores. Data moves between devices by JAX's collectives and lax.ppermute only.
A program may use at most 128 MiB of HBM per device.

v0:
```python
import jax
import jax.numpy as jnp
from jax import lax
from jax.sharding import PartitionSpec as P

HEADS = 8
KV_HEADS = 2


EPSILON = 1e-05


def shifted(value, axis, steps):
    count = lax.axis_size(axis)
    first, last = (max(0, -steps), min(count, count - steps))
    return lax.ppermute(value, axis, [(source, source + steps) for source in range(first, last)])


def swapped(shard, axis, apart):
    return lax.ppermute(shard, axis, [(i, i ^ 1 << apart) for i in range(lax.axis_size(axis))])


def backward_layer(inputs, gain_vec, qkv_weight, out_weight, offset, upstream):
    seq_len = inputs.shape[0]
    query_width = out_weight.shape[0]
    pair_width = (qkv_weight.shape[1] - query_width) // 2
    group_size = HEADS // KV_HEADS
    head_width = query_width // HEADS
    score_scale = head_width ** (-0.5)
    xfloat = inputs.astype(jnp.float32)
    inverse = lax.rsqrt(jnp.mean(xfloat * xfloat, axis=1, keepdims=True) + EPSILON)
    scaled = xfloat * inverse
    normed = (scaled * gain_vec).astype(jnp.bfloat16)
    project = jnp.dot(normed, qkv_weight, preferred_element_type=jnp.float32).astype(jnp.bfloat16)
    queries = project[:, :query_width].reshape(seq_len, KV_HEADS, group_size, head_width)
    keys_all = project[:, query_width : query_width + pair_width].reshape(
        seq_len, KV_HEADS, head_width
    )
    values = project[:, query_width + pair_width :].reshape(seq_len, KV_HEADS, head_width)
    positions = jnp.arange(seq_len, dtype=jnp.int32)
    second_doc = positions >= offset
    allowed = (positions[None, :] <= positions[:, None]) & (
        second_doc[None, :] == second_doc[:, None]
    )
    scores = (
        jnp.einsum("igha,jga->ghij", queries, keys_all, preferred_element_type=jnp.float32)
        * score_scale
    )
    scores = jnp.where(allowed, scores, -1e30)
    row_top = jnp.max(scores, axis=3, keepdims=True)
    raised = jnp.exp(scores - row_top)
    soft_weights = raised / jnp.sum(raised, axis=3, keepdims=True)
    soft_low = soft_weights.astype(jnp.bfloat16)
    attended = jnp.einsum("ghij,jga->igha", soft_low, values, preferred_element_type=jnp.float32)
    attended = attended.reshape(seq_len, query_width).astype(jnp.bfloat16)
    grad_out = jnp.einsum("ia,id->ad", attended, upstream, preferred_element_type=jnp.float32)
    grad_attended = jnp.einsum(
        "id,ad->ia", upstream, out_weight, preferred_element_type=jnp.float32
    ).astype(jnp.bfloat16)
    grad_heads = grad_attended.reshape(seq_len, KV_HEADS, group_size, head_width)
    grad_values = jnp.einsum(
        "ghij,igha->jga", soft_low, grad_heads, preferred_element_type=jnp.float32
    )
    grad_soft = jnp.einsum("igha,jga->ghij", grad_heads, values, preferred_element_type=jnp.float32)
    grad_scores = (
        soft_weights
        * (grad_soft - jnp.sum(soft_weights * grad_soft, axis=3, keepdims=True))
        * score_scale
    ).astype(jnp.bfloat16)
    grad_queries = jnp.einsum(
        "ghij,jga->igha", grad_scores, keys_all, preferred_element_type=jnp.float32
    )
    grad_keys = jnp.einsum(
        "ghij,igha->jga", grad_scores, queries, preferred_element_type=jnp.float32
    )
    grad_project = jnp.concatenate(
        [
            grad_queries.reshape(seq_len, query_width),
            grad_keys.reshape(seq_len, pair_width),
            grad_values.reshape(seq_len, pair_width),
        ],
        axis=1,
    ).astype(jnp.bfloat16)
    grad_qkv = jnp.einsum("id,ik->dk", normed, grad_project, preferred_element_type=jnp.float32)
    grad_normed = jnp.einsum(
        "ik,dk->id", grad_project, qkv_weight, preferred_element_type=jnp.float32
    )
    grad_gain = jnp.sum(grad_normed * scaled, axis=0)
    grad_hat = grad_normed * gain_vec
    grad_inputs = upstream.astype(jnp.float32) + inverse * (
        grad_hat - scaled * jnp.mean(grad_hat * scaled, axis=1, keepdims=True)
    )
    return (grad_inputs.astype(jnp.bfloat16), grad_gain, grad_qkv, grad_out)


def slot_pass(acts, offsets, which, gain_vec, qkv_weight, out_weight, upstream):
    chosen = lax.dynamic_index_in_dim(acts, which, 0, keepdims=False)
    offset = lax.dynamic_index_in_dim(offsets, which, 0, keepdims=False)
    return backward_layer(chosen, gain_vec, qkv_weight, out_weight, offset, upstream)


def partials(first_pass, second_pass):
    gain_part = (first_pass[1] + second_pass[1]).astype(jnp.bfloat16)[None]
    qkv_part = (first_pass[2] + second_pass[2]).astype(jnp.bfloat16)[None]
    out_part = (first_pass[3] + second_pass[3]).astype(jnp.bfloat16)[None]
    return (gain_part, qkv_part, out_part)


def shards(
    act_down,
    act_up,
    grad_down,
    grad_up,
    seed_down,
    seed_up,
    gain_down,
    qkv_down,
    outproj_down,
    gain_up,
    qkv_up,
    outproj_up,
    doc_offsets,
    slot_order,
):
    section_index = lax.axis_index("section")
    section_count = lax.axis_size("section")
    down_offsets = doc_offsets[0, 0, :, 0]
    upper_offsets = doc_offsets[1, 0, :, 0]
    down_one = slot_pass(
        act_down[0],
        down_offsets,
        slot_order[0, 0, 0],
        gain_down[0],
        qkv_down[0],
        outproj_down[0],
        grad_down[0],
    )
    upper_one = slot_pass(
        act_up[0],
        upper_offsets,
        slot_order[1, 0, 0],
        gain_up[0],
        qkv_up[0],
        outproj_up[0],
        grad_up[0],
    )
    from_above = shifted(down_one[0], "section", -1)
    from_below = shifted(upper_one[0], "section", 1)
    down_upstream = jnp.where(section_index == section_count - 1, seed_down, from_above)
    upper_upstream = jnp.where(section_index == 0, seed_up, from_below)
    down_two = slot_pass(
        act_down[0],
        down_offsets,
        slot_order[0, 0, 1],
        gain_down[0],
        qkv_down[0],
        outproj_down[0],
        down_upstream,
    )
    upper_two = slot_pass(
        act_up[0],
        upper_offsets,
        slot_order[1, 0, 1],
        gain_up[0],
        qkv_up[0],
        outproj_up[0],
        upper_upstream,
    )
    down_gain, down_qkv, down_out = partials(down_one, down_two)
    upper_gain, upper_qkv, upper_out = partials(upper_one, upper_two)
    bit_total = section_count.bit_length() - 1
    bit_list = list(range(bit_total))
    sums = (
        lax.psum_scatter(down_gain, "dp", scatter_dimension=1, tiled=True).astype(jnp.float32),
        lax.psum_scatter(down_qkv, "dp", scatter_dimension=1, tiled=True).astype(jnp.float32),
        lax.psum_scatter(down_out, "dp", scatter_dimension=1, tiled=True).astype(jnp.float32),
        lax.psum_scatter(upper_gain, "dp", scatter_dimension=1, tiled=True).astype(jnp.float32),
        lax.psum_scatter(upper_qkv, "dp", scatter_dimension=1, tiled=True).astype(jnp.float32),
        lax.psum_scatter(upper_out, "dp", scatter_dimension=1, tiled=True).astype(jnp.float32),
    )
    mirror_gain, mirror_qkv, mirror_out = (sums[3], sums[4], sums[5])
    for bit_num in bit_list:
        mirror_gain, mirror_qkv, mirror_out = (
            swapped(mirror_gain.astype(jnp.bfloat16), "section", bit_num).astype(mirror_gain.dtype),
            swapped(mirror_qkv.astype(jnp.bfloat16), "section", bit_num).astype(mirror_qkv.dtype),
            swapped(mirror_out.astype(jnp.bfloat16), "section", bit_num).astype(mirror_out.dtype),
        )
    grad_gain = sums[0] + mirror_gain
    grad_qkv = sums[1] + mirror_qkv
    grad_outproj = sums[2] + mirror_out
    down_pair = jnp.stack([down_one[0], down_two[0]], axis=0)
    upper_pair = jnp.stack([upper_one[0], upper_two[0]], axis=0)
    input_grads = jnp.stack([down_pair, upper_pair], axis=0)[:, None]
    return (input_grads, grad_gain, grad_qkv, grad_outproj)


def solution(mesh):
    return jax.shard_map(
        shards,
        mesh=mesh,
        in_specs=(
            P("section", None, "dp", None),
            P("section", None, "dp", None),
            P("section", "dp", None),
            P("section", "dp", None),
            P("dp", None),
            P("dp", None),
            P("section", None),
            P("section", None, None),
            P("section", None, None),
            P("section", None),
            P("section", None, None),
            P("section", None, None),
            P(None, "section", None, "dp"),
            P(None, "section", None),
        ),
        out_specs=(
            P(None, "section", None, "dp", None),
            P("section", "dp"),
            P("section", "dp", None),
            P("section", "dp", None),
        ),
        check_vma=False,
    )
```

profile of v0, /device:TPU:16, one launch (start us, length us, event | category | flops | bytes accessed | tf_op | source)
XLA Modules:
  0.0 289.0 jit_solution(15132474029488953403)
XLA Ops:
  22.1 2.1 fusion.260
  25.3 1.8 fusion.266
  27.1 4.2 %fusion.84 = bf16[2,64,256]{2,1,0:T(8,128)(2,1)S(1)} fusion(bf16[256,2,4,64]{0,3,2,1:T(8,128)(2,1)S(1)} %bitcast.588, f32[2,256,256,4]{2,1,3,0:T(8,128)} %fusion.266, f32[2,4,256,256]{2,3,1,0:T(8,128)} %get-tuple-element.45, f32[2,4,256]{2,1,0:T(4,128)S(1)} %get-tuple-element.44), kind=kOutput, calls=%fused_computation.126 | convolution fusion | flops 70813952 | bytes 4530176 | tf_op jit(solution)/shard_map/ghij,igha->jga/dot_general | solution.py:73
  31.4 4.3 %convolution_convert_fusion.9 = bf16[2,64,4,256]{3,1,2,0:T(8,128)(2,1)S(1)} fusion(bf16[256,2,64,1]{0,2,3,1:T(8,128)(2,1)} %bitcast.626, f32[2,256,256,4]{2,1,3,0:T(8,128)} %fusion.266, f32[2,4,256,256]{2,3,1,0:T(8,128)} %get-tuple-element.45, f32[2,4,256]{2,1,0:T(4,128)S(1)} %get-tuple-element.44), kind=kOutput, calls=%fused_computation.111 | convolution fusion | flops 70912256 | bytes 4530176 | tf_op jit(solution)/shard_map/ghij,jga->igha/dot_general | solution.py:70
  38.4 3.7 %collective-permute-start.1 = (bf16[256,1024]{1,0:T(8,128)(2,1)}, bf16[256,1024]{1,0:T(8,128)(2,1)}, u32[]{:S(2)}, u32[]{:S(2)}) collective-permute-start(bf16[256,1024]{1,0:T(8,128)(2,1)} %fusion.112), channel_id=1, source_target_pairs={{0,2},{2,4},{4,6},{6,8},{8,10},{10,12},{12,14},{14,16},{16,18},{18... | collective-permute-start | bytes 1572872 | tf_op jit(solution)/shard_map/ppermute | solution.py:16
  48.0 3.0 %fusion.262 = (f32[2,4,256]{2,1,0:T(4,128)S(1)}, f32[2,4,256,256]{2,3,1,0:T(8,128)}) fusion(pred[256,256]{0,1:T(8,128)(4,1)} %fusion.197, bf16[256,2,64,1]{0,2,3,1:T(8,128)(2,1)} %bitcast.628, bf16[256,2,4,64]{0,3,2,1:T(8,128)(2,1)S(1)} %bitcast.590), kind=kOutput, calls=%fused_computation.327 | convolution fusion | flops 69206272 | bytes 2498560 | tf_op jit(solution)/shard_map/sub | solution.py:51
  51.0 2.6 fusion.81
  53.6 1.8 fusion.264
  55.4 4.8 %fusion.80 = bf16[2,64,256]{2,1,0:T(8,128)(2,1)} fusion(bf16[256,2,4,64]{0,3,2,1:T(8,128)(2,1)S(1)} %bitcast.592, f32[2,256,256,4]{2,1,3,0:T(8,128)} %fusion.264, f32[2,4,256,256]{2,3,1,0:T(8,128)} %get-tuple-element.51, f32[2,4,256]{2,1,0:T(4,128)S(1)} %get-tuple-element.50), kind=kOutput, calls=%fused_computation.122 | convolution fusion | flops 70813952 | bytes 4530176 | tf_op jit(solution)/shard_map/ghij,igha->jga/dot_general | solution.py:73
  60.2 4.2 %convolution_convert_fusion.11 = bf16[2,64,4,256]{3,1,2,0:T(8,128)(2,1)S(1)} fusion(bf16[256,2,64,1]{0,2,3,1:T(8,128)(2,1)S(1)} %bitcast.630, f32[2,256,256,4]{2,1,3,0:T(8,128)} %fusion.264, f32[2,4,256,256]{2,3,1,0:T(8,128)} %get-tuple-element.51, f32[2,4,256]{2,1,0:T(4,128)S(1)} %get-tuple-element.50), kind=kOutput, calls=%fused_computation.113 | convolution fusion | flops 70912256 | bytes 4530176 | tf_op jit(solution)/shard_map/ghij,jga->igha/dot_general | solution.py:70
  67.9 3.6 %fusion.261 = (f32[2,4,256]{2,1,0:T(4,128)}, f32[2,4,256,256]{2,3,1,0:T(8,128)}) fusion(pred[256,256]{0,1:T(8,128)(4,1)} %fusion.194, bf16[256,2,64,1]{0,2,3,1:T(8,128)(2,1)} %bitcast.632, bf16[256,2,4,64]{0,3,2,1:T(8,128)(2,1)S(1)} %bitcast.594), kind=kOutput, calls=%fused_computation.326 | convolution fusion | flops 69206272 | bytes 2498560 | tf_op jit(solution)/shard_map/sub | solution.py:51
  71.5 4.0 %fusion.93 = (f32[1024]{0:T(1024)}, f32[256]{0:T(256)S(1)}, f32[256]{0:T(256)}, f32[256,1024]{1,0:T(8,128)}) fusion(f32[256]{0:T(256)S(1)} %add_rsqrt_fusion.3, bf16[1,2,256,1024]{3,2,1,0:T(8,128)(2,1)} %param.14, s32[]{:T(128)S(6)} %select_n.45, f32[1024]{0:T(1024)S(1)} %bitcast.649, s32[]{:T(128)S(6)} %select_n.49, bf16[1,1024,768]{2,1,0:T(8,128)(2,1)} %param.21, ...), kind=kOutput, calls=%fused_computation.135 | convolution fusion | flops 406452736 | bytes 4074504 | tf_op jit(solution)/shard_map/ik,dk->id/dot_general | solution.py:85
  76.1 2.4 fusion.154
  81.9 2.7 fusion.87
  84.6 1.8 fusion.267
  86.5 5.0 %fusion.86 = bf16[2,64,256]{2,1,0:T(8,128)(2,1)} fusion(bf16[256,2,4,64]{0,3,2,1:T(8,128)(2,1)} %bitcast.596, f32[2,256,256,4]{2,1,3,0:T(8,128)} %fusion.267, f32[2,4,256,256]{2,3,1,0:T(8,128)} %get-tuple-element.48, f32[2,4,256]{2,1,0:T(4,128)} %get-tuple-element.47), kind=kOutput, calls=%fused_computation.128 | convolution fusion | flops 70813952 | bytes 4530176 | tf_op jit(solution)/shard_map/ghij,igha->jga/dot_general | solution.py:73
  91.4 4.3 %convolution_convert_fusion.8 = bf16[2,64,4,256]{3,1,2,0:T(8,128)(2,1)S(1)} fusion(bf16[256,2,64,1]{0,2,3,1:T(8,128)(2,1)} %bitcast.634, f32[2,256,256,4]{2,1,3,0:T(8,128)} %fusion.267, f32[2,4,256,256]{2,3,1,0:T(8,128)} %get-tuple-element.48, f32[2,4,256]{2,1,0:T(4,128)} %get-tuple-element.47), kind=kOutput, calls=%fused_computation.110 | convolution fusion | flops 70912256 | bytes 4530176 | tf_op jit(solution)/shard_map/ghij,jga->igha/dot_general | solution.py:70
  95.7 3.8 %fusion.41 = bf16[1,1024,768]{2,1,0:T(8,128)(2,1)} fusion(f32[1024,768]{1,0:T(8,128)} %fusion.154, f32[256]{0:T(256)S(1)} %add_rsqrt_fusion, f32[1024]{0:T(1024)S(1)} %bitcast.645, bf16[1,2,256,1024]{3,2,1,0:T(8,128)(2,1)S(1)} %copy-done.1, s32[]{:T(128)S(6)} %select_n.55, bf16[256,128]{0,1:T(8,128)(2,1)S(1)} %bitcast.612, bf16[256,128]{0,1:T(8,128)(2,1)} %bitcast.616, ...), kind=kOutput, calls=%fused_computation.63 | convolution fusion | flops 406454272 | bytes 5641220 | tf_op jit(solution)/shard_map/id,ik->dk/dot_general | solution.py:84
  99.8 2.7 fusion.92
  102.5 4.2 %collective-permute-start = (bf16[256,1024]{1,0:T(8,128)(2,1)}, bf16[256,1024]{1,0:T(8,128)(2,1)}, u32[]{:S(2)}, u32[]{:S(2)}) collective-permute-start(bf16[256,1024]{1,0:T(8,128)(2,1)} %fusion.92), channel_id=1, source_target_pairs={{2,0},{4,2},{6,4},{8,6},{10,8},{12,10},{14,12},{16,14},{18,16},{20... | collective-permute-start | bytes 1572872 | tf_op jit(solution)/shard_map/ppermute | solution.py:16
  106.8 2.1 fusion.71
  110.9 2.8 convolution_convert_fusion.5
  113.8 2.7 convolution_convert_fusion.4
  116.5 2.7 convolution_convert_fusion.7
  119.2 2.1 fusion.263
  121.3 1.8 convolution_convert_fusion.6
  124.6 1.8 fusion.167
  129.0 1.7 convolution_convert_fusion.2
  130.9 3.3 %fusion.123 = (f32[1024]{0:T(1024)S(1)}, f32[256]{0:T(256)}, f32[256,1024]{1,0:T(8,128)}) fusion(f32[256]{0:T(256)S(1)} %add_rsqrt_fusion, bf16[1,2,256,1024]{3,2,1,0:T(8,128)(2,1)} %param.15, s32[]{:T(128)S(6)} %select_n.55, f32[1024]{0:T(1024)S(1)} %bitcast.646, bf16[1,1024,768]{2,1,0:T(8,128)(2,1)S(1)} %copy-done, bf16[256,128]{0,1:T(8,128)(2,1)S(1)} %bitcast.613, ...), kind=kOutput, calls=%fused_computation.165 | convolution fusion | flops 405666560 | bytes 3549188 | tf_op jit(solution)/shard_map/ik,dk->id/dot_general | solution.py:85
  135.2 1.8 fusion.265
  136.9 4.2 %fusion.82 = bf16[2,64,256]{2,1,0:T(8,128)(2,1)S(1)} fusion(bf16[256,2,4,64]{0,3,2,1:T(8,128)(2,1)S(1)} %bitcast.600, f32[2,256,256,4]{2,1,3,0:T(8,128)} %fusion.265, f32[2,4,256,256]{2,3,1,0:T(8,128)} %get-tuple-element.54, f32[2,4,256]{2,1,0:T(4,128)S(1)} %copy-done.78), kind=kOutput, calls=%fused_computation.124 | convolution fusion | flops 70813952 | bytes 4530176 | tf_op jit(solution)/shard_map/ghij,igha->jga/dot_general | solution.py:73
  141.2 4.2 %convolution_convert_fusion.10 = bf16[2,64,4,256]{3,1,2,0:T(8,128)(2,1)S(1)} fusion(bf16[256,2,64,1]{0,2,3,1:T(8,128)(2,1)S(1)} %bitcast.639, f32[2,256,256,4]{2,1,3,0:T(8,128)} %fusion.265, f32[2,4,256,256]{2,3,1,0:T(8,128)} %get-tuple-element.54, f32[2,4,256]{2,1,0:T(4,128)} %copy-done.77), kind=kOutput, calls=%fused_computation.112 | convolution fusion | flops 70912256 | bytes 4530176 | tf_op jit(solution)/shard_map/ghij,jga->igha/dot_general | solution.py:70
  145.4 2.0 fusion.83
  147.6 3.8 %fusion.103 = (f32[1024]{0:T(1024)S(1)}, f32[256]{0:T(256)}, f32[256,1024]{1,0:T(8,128)}) fusion(f32[256]{0:T(256)} %copy-done.62, bf16[1,2,256,1024]{3,2,1,0:T(8,128)(2,1)} %param.14, s32[]{:T(128)S(6)} %select_n.49, f32[1024]{0:T(1024)S(1)} %bitcast.652, bf16[1,1024,768]{2,1,0:T(8,128)(2,1)} %param.21, bf16[256,128]{0,1:T(8,128)(2,1)S(1)} %bitcast.622, ...), kind=kOutput, calls=%fused_computation.145 | convolution fusion | flops 405666560 | bytes 3549188 | tf_op jit(solution)/shard_map/ik,dk->id/dot_general | solution.py:85
  152.7 3.1 %fusion.42 = bf16[1,512,1024]{2,1,0:T(8,128)(2,1)} fusion(f32[512,1024]{1,0:T(8,128)} %fusion.167, bf16[256,512]{0,1:T(8,128)(2,1)S(1)} %bitcast.604, bf16[256,1024]{1,0:T(8,128)(2,1)S(1)} %broadcast_select_fusion.1), kind=kOutput, calls=%fused_computation.64 | convolution fusion | flops 269484032 | bytes 3932160 | tf_op jit(solution)/shard_map/ia,id->ad/dot_general | solution.py:56
  155.9 3.4 %fusion.162 = f32[1024,768]{1,0:T(8,128)} fusion(f32[1024]{0:T(1024)S(1)} %bitcast.653, f32[256]{0:T(256)S(1)} %add_rsqrt_fusion.3, bf16[1,2,256,1024]{3,2,1,0:T(8,128)(2,1)} %param.14, s32[]{:T(128)S(6)} %select_n.45, bf16[256,128]{0,1:T(8,128)(2,1)S(1)} %bitcast.609, bf16[256,128]{0,1:T(8,128)(2,1)S(1)} %bitcast.611, bf16[256,512]{0,1:T(8,128)(2,1)S(1)} %bitcast.571), kind=kOutput, calls=%fused_computation.204 | convolution fusion | flops 404881408 | bytes 4068356 | tf_op jit(solution)/shard_map/id,ik->dk/dot_general | solution.py:84
  159.4 3.9 %fusion.40 = bf16[1,1024,768]{2,1,0:T(8,128)(2,1)} fusion(f32[1024,768]{1,0:T(8,128)} %fusion.162, f32[256]{0:T(256)S(1)} %copy-done.63, f32[1024]{0:T(1024)S(1)} %bitcast.654, bf16[1,2,256,1024]{3,2,1,0:T(8,128)(2,1)} %param.14, s32[]{:T(128)S(6)} %select_n.49, bf16[256,128]{0,1:T(8,128)(2,1)S(1)} %bitcast.623, bf16[256,128]{0,1:T(8,128)(2,1)S(1)} %bitcast.621, ...), kind=kOutput, calls=%fused_computation.62 | convolution fusion | flops 406454272 | bytes 5641220 | tf_op jit(solution)/shard_map/id,ik->dk/dot_general | solution.py:84
  163.4 15.1 %collective-permute-done.6 = bf16[1,512,768]{2,1,0:T(8,128)(2,1)} collective-permute-done((bf16[1,512,768]{2,1,0:T(8,128)(2,1)}, bf16[1,512,768]{2,1,0:T(8,128)(2,1)}, u32[]{:S(2)}, u32[]{:S(2)}) %collective-permute-start.6) | collective-permute-done | bytes 786464 | tf_op jit(solution)/shard_map/ppermute | solution.py:20
  179.8 12.2 %collective-permute-done.10 = bf16[1,256,1024]{2,1,0:T(8,128)(2,1)S(1)} collective-permute-done((bf16[1,256,1024]{2,1,0:T(8,128)(2,1)}, bf16[1,256,1024]{2,1,0:T(8,128)(2,1)S(1)}, u32[]{:S(2)}, u32[]{:S(2)}) %collective-permute-start.10) | collective-permute-done | bytes 524320 | tf_op jit(solution)/shard_map/ppermute | solution.py:20
  192.8 6.5 %collective-permute-done.7 = bf16[1,512,768]{2,1,0:T(8,128)(2,1)} collective-permute-done((bf16[1,512,768]{2,1,0:T(8,128)(2,1)}, bf16[1,512,768]{2,1,0:T(8,128)(2,1)}, u32[]{:S(2)}, u32[]{:S(2)}) %collective-permute-start.7) | collective-permute-done | bytes 786464 | tf_op jit(solution)/shard_map/ppermute | solution.py:20
  200.9 1.7 fusion.151
  202.6 5.5 %collective-permute-done.11 = bf16[1,256,1024]{2,1,0:T(8,128)(2,1)} collective-permute-done((bf16[1,256,1024]{2,1,0:T(8,128)(2,1)S(1)}, bf16[1,256,1024]{2,1,0:T(8,128)(2,1)}, u32[]{:S(2)}, u32[]{:S(2)}) %collective-permute-start.11) | collective-permute-done | bytes 524320 | tf_op jit(solution)/shard_map/ppermute | solution.py:20
  211.0 1.7 fusion.159
  218.3 9.7 %collective-permute-done.12 = bf16[1,256,1024]{2,1,0:T(8,128)(2,1)} collective-permute-done((bf16[1,256,1024]{2,1,0:T(8,128)(2,1)}, bf16[1,256,1024]{2,1,0:T(8,128)(2,1)}, u32[]{:S(2)}, u32[]{:S(2)}) %collective-permute-start.12) | collective-permute-done | bytes 524320 | tf_op jit(solution)/shard_map/ppermute | solution.py:20
  228.4 2.5 collective-permute-start.9
  235.1 41.9 %collective-permute-done.5 = bf16[1,512]{1,0:T(2,128)(2,1)S(1)} collective-permute-done((bf16[1,512]{1,0:T(2,128)(2,1)S(1)}, bf16[1,512]{1,0:T(2,128)(2,1)S(1)}, u32[]{:S(2)}, u32[]{:S(2)}) %collective-permute-start.5) | collective-permute-done | bytes 1056 | tf_op jit(solution)/shard_map/ppermute | solution.py:20
  277.6 2.2 convert_add_fusion.1
  279.8 2.4 convert_add_fusion
  (264 shorter events, 50.2 us)
Async XLA Ops:
  7.2 8.7 %copy-start = (bf16[1,1024,768]{2,1,0:T(8,128)(2,1)S(1)}, bf16[1,1024,768]{2,1,0:T(8,128)(2,1)}, u32[]{:S(2)}) copy-start(bf16[1,1024,768]{2,1,0:T(8,128)(2,1)} %param.24) | copy-start | bytes 4718596
  7.2 152.1 %reduce-scatter.13.cloned.1.call-start = ((), (), s32[]{:S(2)}) async-start(), calls=%async_computation.7 | async-start | bytes 2359296 | tf_op jit(solution)/shard_map/reduce_scatter | solution.py:178
  15.8 21.4 %copy-start.64 = (f32[256]{0:T(256)}, f32[256]{0:T(256)S(1)}, u32[]{:S(2)}) copy-start(f32[256]{0:T(256)S(1)} %add_rsqrt_fusion.1) | copy-start | bytes 3076
  21.9 5.2 %copy-start.24 = (bf16[256,512]{0,1:T(8,128)(2,1)}, bf16[256,512]{0,1:T(8,128)(2,1)S(1)}, u32[]{:S(2)}) copy-start(bf16[256,512]{0,1:T(8,128)(2,1)S(1)} %copy.115) | copy-start | bytes 786436
  24.2 7.2 %copy-start.73 = (f32[2,4,256]{2,1,0:T(4,128)}, f32[2,4,256]{2,1,0:T(4,128)S(1)}, u32[]{:S(2)}) copy-start(f32[2,4,256]{2,1,0:T(4,128)S(1)} %get-tuple-element.44) | copy-start | bytes 24580
  25.3 10.4 %copy-start.43 = (bf16[2,64,256]{2,1,0:T(8,128)(2,1)}, bf16[2,64,256]{2,1,0:T(8,128)(2,1)S(1)}, u32[]{:S(2)}) copy-start(bf16[2,64,256]{2,1,0:T(8,128)(2,1)S(1)} %fusion.85) | copy-start | bytes 196612
  38.4 5.1 %copy-start.2 = (bf16[1,2,256,1024]{3,2,1,0:T(8,128)(2,1)S(1)}, bf16[1,2,256,1024]{3,2,1,0:T(8,128)(2,1)}, u32[]{:S(2)}) copy-start(bf16[1,2,256,1024]{3,2,1,0:T(8,128)(2,1)} %param.14) | copy-start | bytes 3145732
  38.4 40.2 %collective-permute-start.1 = (bf16[256,1024]{1,0:T(8,128)(2,1)}, bf16[256,1024]{1,0:T(8,128)(2,1)}, u32[]{:S(2)}, u32[]{:S(2)}) collective-permute-start(bf16[256,1024]{1,0:T(8,128)(2,1)} %fusion.112), channel_id=1, source_target_pairs={{0,2},{2,4},{4,6},{6,8},{8,10},{10,12},{12,14},{14,16},{16,18},{18... | collective-permute-start | bytes 1572872 | tf_op jit(solution)/shard_map/ppermute | solution.py:16
  47.9 7.5 %copy-start.25 = (bf16[256,512]{0,1:T(8,128)(2,1)}, bf16[256,512]{0,1:T(8,128)(2,1)S(1)}, u32[]{:S(2)}) copy-start(bf16[256,512]{0,1:T(8,128)(2,1)S(1)} %copy.101) | copy-start | bytes 786436
  51.0 9.2 %copy-start.74 = (f32[2,4,256]{2,1,0:T(4,128)}, f32[2,4,256]{2,1,0:T(4,128)S(1)}, u32[]{:S(2)}) copy-start(f32[2,4,256]{2,1,0:T(4,128)S(1)} %get-tuple-element.50) | copy-start | bytes 24580
  60.2 5.7 %copy-start.31 = (bf16[256,128]{1,0:T(8,128)(2,1)S(1)}, bf16[256,128]{1,0:T(8,128)(2,1)}, u32[]{:S(2)}) copy-start(bf16[256,128]{1,0:T(8,128)(2,1)} %get-tuple-element.31) | copy-start | bytes 196612
  60.2 6.4 %slice-start = ((bf16[256,768]{1,0:T(8,128)(2,1)}), bf16[256,512]{1,0:T(8,128)(2,1)S(1)}, s32[]{:S(2)}) async-start(bf16[256,768]{1,0:T(8,128)(2,1)} %copy-done.11), calls=%async_computation.12 | async-start | bytes 524288 | tf_op jit(solution)/shard_map/slice | solution.py:35
  64.5 7.0 %copy-start.14 = (bf16[2,64,4,256]{3,1,2,0:T(8,128)(2,1)}, bf16[2,64,4,256]{3,1,2,0:T(8,128)(2,1)S(1)}, u32[]{:S(2)}) copy-start(bf16[2,64,4,256]{3,1,2,0:T(8,128)(2,1)S(1)} %convolution_convert_fusion.11) | copy-start | bytes 786436
  66.8 8.8 %copy-start.27 = (bf16[256,512]{0,1:T(8,128)(2,1)}, bf16[256,512]{0,1:T(8,128)(2,1)S(1)}, u32[]{:S(2)}) copy-start(bf16[256,512]{0,1:T(8,128)(2,1)S(1)} %copy.122) | copy-start | bytes 786436
  66.8 4.7 %copy-start.37 = (bf16[2,64,256]{2,1,0:T(8,128)(2,1)S(1)}, bf16[2,64,256]{2,1,0:T(8,128)(2,1)}, u32[]{:S(2)}) copy-start(bf16[2,64,256]{2,1,0:T(8,128)(2,1)} %fusion.81) | copy-start | bytes 196612
  66.8 4.7 %copy-start.39 = (bf16[2,64,256]{2,1,0:T(8,128)(2,1)S(1)}, bf16[2,64,256]{2,1,0:T(8,128)(2,1)}, u32[]{:S(2)}) copy-start(bf16[2,64,256]{2,1,0:T(8,128)(2,1)} %fusion.80) | copy-start | bytes 196612
  67.9 16.8 %copy-start.20 = (bf16[256,128]{0,1:T(8,128)(2,1)}, bf16[256,128]{0,1:T(8,128)(2,1)S(1)}, u32[]{:S(2)}) copy-start(bf16[256,128]{0,1:T(8,128)(2,1)S(1)} %copy.123) | copy-start | bytes 196612
  71.5 4.6 %copy-start.17 = (bf16[2,64,4,256]{3,1,2,0:T(8,128)(2,1)S(1)}, bf16[2,64,4,256]{3,1,2,0:T(8,128)(2,1)}, u32[]{:S(2)}) copy-start(bf16[2,64,4,256]{3,1,2,0:T(8,128)(2,1)} %copy-done.16) | copy-start | bytes 786436
  71.5 4.6 %copy-start.44 = (bf16[2,64,256]{2,1,0:T(8,128)(2,1)S(1)}, bf16[2,64,256]{2,1,0:T(8,128)(2,1)}, u32[]{:S(2)}) copy-start(bf16[2,64,256]{2,1,0:T(8,128)(2,1)} %copy-done.43) | copy-start | bytes 196612
  71.5 4.6 %copy-start.47 = (bf16[2,64,256]{2,1,0:T(8,128)(2,1)S(1)}, bf16[2,64,256]{2,1,0:T(8,128)(2,1)}, u32[]{:S(2)}) copy-start(bf16[2,64,256]{2,1,0:T(8,128)(2,1)} %copy-done.46) | copy-start | bytes 196612
  71.5 4.6 %copy-start.65 = (f32[256]{0:T(256)S(1)}, f32[256]{0:T(256)}, u32[]{:S(2)}) copy-start(f32[256]{0:T(256)} %copy-done.64) | copy-start | bytes 3076
  99.5 7.2 %copy-start.71 = (f32[256]{0:T(256)S(1)}, f32[256]{0:T(256)}, u32[]{:S(2)}) copy-start(f32[256]{0:T(256)} %get-tuple-element.24) | copy-start | bytes 3076
  99.5 7.3 %copy-start.3 = (bf16[1,2,256,1024]{3,2,1,0:T(8,128)(2,1)S(1)}, bf16[1,2,256,1024]{3,2,1,0:T(8,128)(2,1)}, u32[]{:S(2)}) copy-start(bf16[1,2,256,1024]{3,2,1,0:T(8,128)(2,1)} %param.14) | copy-start | bytes 3145732
  99.6 79.9 %reduce-scatter.17.cloned.1.call-start = ((), (), s32[]{:S(2)}) async-start(), calls=%async_computation.9 | async-start | bytes 1572864 | tf_op jit(solution)/shard_map/reduce_scatter | solution.py:179
  102.5 25.4 %collective-permute-start = (bf16[256,1024]{1,0:T(8,128)(2,1)}, bf16[256,1024]{1,0:T(8,128)(2,1)}, u32[]{:S(2)}, u32[]{:S(2)}) collective-permute-start(bf16[256,1024]{1,0:T(8,128)(2,1)} %fusion.92), channel_id=1, source_target_pairs={{2,0},{4,2},{6,4},{8,6},{10,8},{12,10},{14,12},{16,14},{18,16},{20... | collective-permute-start | bytes 1572872 | tf_op jit(solution)/shard_map/ppermute | solution.py:16
  109.1 12.2 %copy-start.57 = (bf16[256,128]{0,1:T(8,128)(2,1)}, bf16[256,128]{0,1:T(8,128)(2,1)S(1)}, u32[]{:S(2)}) copy-start(bf16[256,128]{0,1:T(8,128)(2,1)S(1)} %copy.107) | copy-start | bytes 196612
  110.1 11.2 %copy-start.22 = (bf16[256,128]{0,1:T(8,128)(2,1)}, bf16[256,128]{0,1:T(8,128)(2,1)S(1)}, u32[]{:S(2)}) copy-start(bf16[256,128]{0,1:T(8,128)(2,1)S(1)} %copy.109) | copy-start | bytes 196612
  110.8 10.4 %copy-start.59 = (pred[256,256]{0,1:T(8,128)(4,1)}, pred[256,256]{0,1:T(8,128)(4,1)S(1)}, u32[]{:S(2)}) copy-start(pred[256,256]{0,1:T(8,128)(4,1)S(1)} %fusion.196) | copy-start | bytes 196612
  127.9 81.7 %reduce-scatter.21.cloned.1.call-start = ((), (), s32[]{:S(2)}) async-start(), calls=%async_computation.11 | async-start | bytes 393216
  141.2 6.4 %copy-start.48 = (bf16[2,64,256]{2,1,0:T(8,128)(2,1)}, bf16[2,64,256]{2,1,0:T(8,128)(2,1)S(1)}, u32[]{:S(2)}) copy-start(bf16[2,64,256]{2,1,0:T(8,128)(2,1)S(1)} %fusion.82) | copy-start | bytes 196612
  147.5 86.6 %reduce-scatter.19.cloned.1.call-start = ((), (), s32[]{:S(2)}) async-start(), calls=%async_computation.10 | async-start | bytes 393216
  147.5 5.1 %copy-start.35 = (bf16[2,64,4,256]{3,1,2,0:T(8,128)(2,1)S(1)}, bf16[2,64,4,256]{3,1,2,0:T(8,128)(2,1)}, u32[]{:S(2)}) copy-start(bf16[2,64,4,256]{3,1,2,0:T(8,128)(2,1)} %convolution_convert_fusion.6) | copy-start | bytes 786436
  152.3 125.2 %reduce-scatter.15.cloned.1.call-start = ((), (), s32[]{:S(2)}) async-start(), calls=%async_computation.8 | async-start | bytes 1572864 | tf_op jit(solution)/shard_map/reduce_scatter | solution.py:176
  155.8 123.9 %reduce-scatter.11.cloned.1.call-start = ((), (), s32[]{:S(2)}) async-start(), calls=%async_computation.6 | async-start | bytes 2359296 | tf_op jit(solution)/shard_map/reduce_scatter | solution.py:175
  159.3 33.5 %copy-start.69 = (f32[256]{0:T(256)S(1)}, f32[256]{0:T(256)}, u32[]{:S(2)}) copy-start(f32[256]{0:T(256)} %get-tuple-element.21) | copy-start | bytes 3076
  159.3 19.2 %collective-permute-start.6 = (bf16[1,512,768]{2,1,0:T(8,128)(2,1)}, bf16[1,512,768]{2,1,0:T(8,128)(2,1)}, u32[]{:S(2)}, u32[]{:S(2)}) collective-permute-start(bf16[1,512,768]{2,1,0:T(8,128)(2,1)} %reduce-scatter.13.cloned.1.call-done), channel_id=1, source_target_pairs={{0,2},{2,0},{4,6},{6,4},{8,10},{10,8},{12,14},{14,12},{16,18},{18,... | collective-permute-start | bytes 2359304 | tf_op jit(solution)/shard_map/ppermute | solution.py:20
  163.4 46.1 %copy-start.70 = (f32[256]{0:T(256)S(1)}, f32[256]{0:T(256)}, u32[]{:S(2)}) copy-start(f32[256]{0:T(256)} %get-tuple-element.17) | copy-start | bytes 3076
  178.5 20.8 %collective-permute-start.7 = (bf16[1,512,768]{2,1,0:T(8,128)(2,1)}, bf16[1,512,768]{2,1,0:T(8,128)(2,1)}, u32[]{:S(2)}, u32[]{:S(2)}) collective-permute-start(bf16[1,512,768]{2,1,0:T(8,128)(2,1)} %collective-permute-done.6), channel_id=1, source_target_pairs={{0,4},{2,6},{4,0},{6,2},{8,12},{10,14},{12,8},{14,10},{16,20},{18,... | collective-permute-start | bytes 2359304 | tf_op jit(solution)/shard_map/ppermute | solution.py:20
  179.5 12.5 %collective-permute-start.10 = (bf16[1,256,1024]{2,1,0:T(8,128)(2,1)}, bf16[1,256,1024]{2,1,0:T(8,128)(2,1)S(1)}, u32[]{:S(2)}, u32[]{:S(2)}) collective-permute-start(bf16[1,256,1024]{2,1,0:T(8,128)(2,1)} %reduce-scatter.17.cloned.1.call-done), channel_id=1, source_target_pairs={{0,2},{2,0},{4,6},{6,4},{8,10},{10,8},{12,14},{14,12},{16,18},{18,... | collective-permute-start | bytes 1572872 | tf_op jit(solution)/shard_map/ppermute | solution.py:20
  191.9 16.1 %collective-permute-start.11 = (bf16[1,256,1024]{2,1,0:T(8,128)(2,1)S(1)}, bf16[1,256,1024]{2,1,0:T(8,128)(2,1)}, u32[]{:S(2)}, u32[]{:S(2)}) collective-permute-start(bf16[1,256,1024]{2,1,0:T(8,128)(2,1)S(1)} %collective-permute-done.10), channel_id=1, source_target_pairs={{0,4},{2,6},{4,0},{6,2},{8,12},{10,14},{12,8},{14,10},{16,20},{18,... | collective-permute-start | bytes 1572872 | tf_op jit(solution)/shard_map/ppermute | solution.py:20
  199.3 29.1 %collective-permute-start.8 = (bf16[1,512,768]{2,1,0:T(8,128)(2,1)}, bf16[1,512,768]{2,1,0:T(8,128)(2,1)}, u32[]{:S(2)}, u32[]{:S(2)}) collective-permute-start(bf16[1,512,768]{2,1,0:T(8,128)(2,1)} %collective-permute-done.7), channel_id=1, source_target_pairs={{0,8},{2,10},{4,12},{6,14},{8,0},{10,2},{12,4},{14,6},{16,24},{18,... | collective-permute-start | bytes 2359304 | tf_op jit(solution)/shard_map/ppermute | solution.py:20
  208.0 19.9 %collective-permute-start.12 = (bf16[1,256,1024]{2,1,0:T(8,128)(2,1)}, bf16[1,256,1024]{2,1,0:T(8,128)(2,1)}, u32[]{:S(2)}, u32[]{:S(2)}) collective-permute-start(bf16[1,256,1024]{2,1,0:T(8,128)(2,1)} %collective-permute-done.11), channel_id=1, source_target_pairs={{0,8},{2,10},{4,12},{6,14},{8,0},{10,2},{12,4},{14,6},{16,24},{18,... | collective-permute-start | bytes 1572872 | tf_op jit(solution)/shard_map/ppermute | solution.py:20
  210.5 3.6 %collective-permute-start.2 = (bf16[1,512]{1,0:T(2,128)(2,1)S(1)}, bf16[1,512]{1,0:T(2,128)(2,1)S(1)}, u32[]{:S(2)}, u32[]{:S(2)}) collective-permute-start(bf16[1,512]{1,0:T(2,128)(2,1)S(1)} %copy.168), channel_id=1, source_target_pairs={{0,2},{2,0},{4,6},{6,4},{8,10},{10,8},{12,14},{14,12},{16,18},{18,... | collective-permute-start | bytes 3080 | tf_op jit(solution)/shard_map/ppermute | solution.py:20
  214.2 3.6 %collective-permute-start.3 = (bf16[1,512]{1,0:T(2,128)(2,1)S(1)}, bf16[1,512]{1,0:T(2,128)(2,1)S(1)}, u32[]{:S(2)}, u32[]{:S(2)}) collective-permute-start(bf16[1,512]{1,0:T(2,128)(2,1)S(1)} %collective-permute-done.2), channel_id=1, source_target_pairs={{0,4},{2,6},{4,0},{6,2},{8,12},{10,14},{12,8},{14,10},{16,20},{18,... | collective-permute-start | bytes 3080 | tf_op jit(solution)/shard_map/ppermute | solution.py:20
  217.8 14.3 %collective-permute-start.4 = (bf16[1,512]{1,0:T(2,128)(2,1)S(1)}, bf16[1,512]{1,0:T(2,128)(2,1)S(1)}, u32[]{:S(2)}, u32[]{:S(2)}) collective-permute-start(bf16[1,512]{1,0:T(2,128)(2,1)S(1)} %collective-permute-done.3), channel_id=1, source_target_pairs={{0,8},{2,10},{4,12},{6,14},{8,0},{10,2},{12,4},{14,6},{16,24},{18,... | collective-permute-start | bytes 3080 | tf_op jit(solution)/shard_map/ppermute | solution.py:20
  228.0 49.6 %collective-permute-start.13 = (bf16[1,256,1024]{2,1,0:T(8,128)(2,1)}, bf16[1,256,1024]{2,1,0:T(8,128)(2,1)S(1)}, u32[]{:S(2)}, u32[]{:S(2)}) collective-permute-start(bf16[1,256,1024]{2,1,0:T(8,128)(2,1)} %collective-permute-done.12), channel_id=1, source_target_pairs={{0,16},{2,18},{4,20},{6,22},{8,24},{10,26},{12,28},{14,30},{16,0},... | collective-permute-start | bytes 1572872 | tf_op jit(solution)/shard_map/ppermute | solution.py:20
  228.4 51.3 %collective-permute-start.9 = (bf16[1,512,768]{2,1,0:T(8,128)(2,1)}, bf16[1,512,768]{2,1,0:T(8,128)(2,1)S(1)}, u32[]{:S(2)}, u32[]{:S(2)}) collective-permute-start(bf16[1,512,768]{2,1,0:T(8,128)(2,1)} %collective-permute-done.8), channel_id=1, source_target_pairs={{0,16},{2,18},{4,20},{6,22},{8,24},{10,26},{12,28},{14,30},{16,0},... | collective-permute-start | bytes 2359304 | tf_op jit(solution)/shard_map/ppermute | solution.py:20
  232.0 44.9 %collective-permute-start.5 = (bf16[1,512]{1,0:T(2,128)(2,1)S(1)}, bf16[1,512]{1,0:T(2,128)(2,1)S(1)}, u32[]{:S(2)}, u32[]{:S(2)}) collective-permute-start(bf16[1,512]{1,0:T(2,128)(2,1)S(1)} %collective-permute-done.4), channel_id=1, source_target_pairs={{0,16},{2,18},{4,20},{6,22},{8,24},{10,26},{12,28},{14,30},{16,0},... | collective-permute-start | bytes 3080 | tf_op jit(solution)/shard_map/ppermute | solution.py:20
  (52 other events, 146.4 us)
Sparse Core Ops, SparseCore 0:
  99.7 9.4 reduce-scatter.12
  128.0 8.8 reduce-scatter.16
  147.6 7.1 reduce-scatter.20
  157.0 8.8 reduce-scatter.18
  167.9 9.6 reduce-scatter.14
  180.4 10.2 reduce-scatter.10
where the time goes:
time: 295 us; the launch traced here: 289 us
  matrix products  114 us (39%)
  waiting for transfers between devices  93.5 us (32%)
  other arithmetic  24.8 us (8%)
  between operations  23.1 us (8%)
  starting transfers between devices  19.7 us (7%)
  local copies, waits for them, and re-layouts  13.6 us (5%)
    ppermute x12, waiting for transfers between devices, swapped(): lax.ppermute(shard, axis, [(i, i ^ 1 << apart) for i in range(lax.axis_si...  93.4 us
    dot_general x4, matrix products, backward_layer(): jnp.einsum('ghij,igha->jga', grad_scores, queries, preferred_element_type...  18.2 us
    dot_general x4, matrix products, backward_layer(): jnp.einsum('ghij,jga->igha', grad_scores, keys_all, preferred_element_typ...  17.1 us
    dot_general x4, matrix products, backward_layer(): jnp.einsum('id,ik->dk', normed, grad_project, preferred_element_type=jnp....  13.5 us
    dot_general x4, matrix products, backward_layer(): jnp.einsum('ik,dk->id', grad_project, qkv_weight, preferred_element_type=...  12.6 us
    ppermute x12, starting transfers between devices, swapped(): lax.ppermute(shard, axis, [(i, i ^ 1 << apart) for i in range(lax.axis_si...  11.1 us
    sub x4, matrix products, backward_layer(): raised = jnp.exp(scores - row_top)  10.8 us
    dot_general x4, matrix products, backward_layer(): jnp.einsum('ghij,jga->igha', soft_low, values, preferred_element_type=jnp...  10 us
  transfers between devices with their start and end apart: 20, of which 8 were waited for; matrix products, arithmetic and copies ran while one was open for 37% of the time, Pallas kernels for 0%

commit v1 on v0

v1 whole, which is shorter than its diff:
```python
import functools
import jax
import jax.numpy as jnp
from jax import lax
from jax.experimental import pallas as pl
from jax.experimental.pallas import tpu as pltpu
from jax.sharding import PartitionSpec as P

HEADS = 8
KV_HEADS = 2
EPSILON = 1e-05
MASKED = -1e30
PAD = 16
VMEM_LIMIT = 32 * 1024 * 1024
F32 = jnp.float32
BF16 = jnp.bfloat16
NN = (((1,), (0,)), ((), ()))
NT = (((1,), (1,)), ((), ()))
TN = (((0,), (0,)), ((), ()))


def dot(a, b, dims=NN):
    return lax.dot_general(a, b, dims, preferred_element_type=F32)


def doubled(pair, half):
    wide = pair.astype(F32)
    turned = pltpu.roll(wide, half, 1)
    left = lax.broadcasted_iota(jnp.int32, wide.shape, 1) < half
    zero = jnp.zeros_like(wide)
    out = []
    for g in range(KV_HEADS):
        a, b = (wide, turned) if g == 0 else (turned, wide)
        out.append(
            jnp.concatenate([jnp.where(left, a, zero), jnp.where(left, zero, b)], axis=0).astype(BF16)
        )
    return out


def mask_bias(seq, offset):
    row = lax.broadcasted_iota(jnp.int32, (seq, seq), 0)
    col = lax.broadcasted_iota(jnp.int32, (seq, seq), 1)
    start = jnp.where(row >= offset, offset, 0)
    return jnp.where((col <= row) & (col >= start), 0.0, MASKED).astype(F32)


def normalise(x, gain):
    xf = x.astype(F32)
    inverse = lax.rsqrt(jnp.mean(xf * xf, axis=1, keepdims=True) + EPSILON)
    scaled = xf * inverse
    return inverse, scaled, (scaled * gain).astype(BF16)


def forward_heads(project, offset, query_width, soft_ref):
    seq = project.shape[0]
    half = query_width // HEADS
    wide = 2 * half
    keys = doubled(project[:, query_width : query_width + wide], half)
    values = doubled(project[:, query_width + wide :], half)
    bias = mask_bias(seq, offset)
    scale = half ** (-0.5)
    pairs = HEADS // 2
    attended = []
    for p in range(pairs):
        g = p * KV_HEADS // pairs
        queries = project[:, p * wide : (p + 1) * wide] * jnp.asarray(scale, BF16)
        scores = dot(queries, keys[g], NT)
        for t in range(2):
            s = scores[:, t * seq : (t + 1) * seq] + bias
            e = jnp.exp(s - jnp.max(s, axis=1, keepdims=True))
            soft = e * (1.0 / jnp.sum(e, axis=1, keepdims=True))
            soft_ref[p, :, t * seq : (t + 1) * seq] = soft.astype(BF16)
        attended.append(dot(soft_ref[p], values[g]))
    return attended


def backward_heads(project, attended, grad_attended, query_width, soft_ref):
    seq = project.shape[0]
    half = query_width // HEADS
    wide = 2 * half
    keys = doubled(project[:, query_width : query_width + wide], half)
    values = doubled(project[:, query_width + wide :], half)
    scale = half ** (-0.5)
    pairs = HEADS // 2
    left = lax.broadcasted_iota(jnp.int32, (seq, wide), 1) < half
    grad_queries = []
    grad_keys = [None] * KV_HEADS
    grad_values = [None] * KV_HEADS
    for p in range(pairs):
        g = p * KV_HEADS // pairs
        queries = project[:, p * wide : (p + 1) * wide] * jnp.asarray(scale, BF16)
        grad_pair = grad_attended[:, p * wide : (p + 1) * wide]
        grad_soft = dot(grad_pair, values[g], NT)
        both = attended[p].astype(F32) * grad_pair.astype(F32)
        rows = [
            jnp.sum(jnp.where(left, both, 0.0), axis=1, keepdims=True),
            jnp.sum(jnp.where(left, 0.0, both), axis=1, keepdims=True),
        ]
        soft = soft_ref[p]
        grad_scores = jnp.concatenate(
            [
                (
                    soft[:, t * seq : (t + 1) * seq].astype(F32)
                    * (grad_soft[:, t * seq : (t + 1) * seq] - rows[t])
                ).astype(BF16)
                for t in range(2)
            ],
            axis=1,
        )
        grad_queries.append(dot(grad_scores, keys[g]) * scale)
        keys_part = dot(queries, grad_scores, TN)
        values_part = dot(grad_pair, soft, TN)
        keys_sum = keys_part[:half, :seq] + keys_part[half:, seq:]
        values_sum = values_part[:half, :seq] + values_part[half:, seq:]
        grad_keys[g] = keys_sum if grad_keys[g] is None else grad_keys[g] + keys_sum
        grad_values[g] = values_sum if grad_values[g] is None else grad_values[g] + values_sum
    columns = grad_queries + [
        jnp.concatenate(grad_keys, axis=0).T,
        jnp.concatenate(grad_values, axis=0).T,
    ]
    return jnp.concatenate([c.astype(BF16) for c in columns], axis=1)


def input_gradient(grad_project, qkv, gain, scaled, inverse, upstream):
    grad_normed = dot(grad_project, qkv, NT)
    grad_hat = grad_normed * gain
    part = grad_normed * scaled
    grad_gain = jnp.sum(part, axis=0, keepdims=True)
    mean = jnp.mean(part * gain, axis=1, keepdims=True)
    grad_in = upstream.astype(F32) + inverse * (grad_hat - scaled * mean)
    return grad_in.astype(BF16), grad_gain


def first_kernel(
    scalars, act, qkv_hbm, out_hbm, up_hbm, gain_ref,
    grad_ref, normed_ref, attended_ref, project_ref, gain_out,
    x_ref, qkv_ref, out_ref, up_ref, soft_ref, sems,
):
    copies = [
        pltpu.make_async_copy(act.at[scalars[0]], x_ref, sems.at[0]),
        pltpu.make_async_copy(qkv_hbm, qkv_ref, sems.at[1]),
        pltpu.make_async_copy(up_hbm, up_ref, sems.at[2]),
        pltpu.make_async_copy(out_hbm, out_ref, sems.at[3]),
    ]
    for copy in copies:
        copy.start()
    query_width = out_hbm.shape[0]
    gain = gain_ref[...]
    copies[0].wait()
    inverse, scaled, normed = normalise(x_ref[...], gain)
    normed_ref[...] = normed
    copies[1].wait()
    project = dot(normed, qkv_ref[...]).astype(BF16)
    attended = forward_heads(project, scalars[1], query_width, soft_ref)
    attended_ref[...] = jnp.concatenate([a.astype(BF16) for a in attended], axis=1)
    copies[2].wait()
    copies[3].wait()
    grad_attended = dot(up_ref[...], out_ref[...], NT).astype(BF16)
    grad_project = backward_heads(project, attended, grad_attended, query_width, soft_ref)
    project_ref[...] = grad_project
    inverse, scaled, _ = normalise(x_ref[...], gain)
    grad_ref[...], gain_out[...] = input_gradient(
        grad_project, qkv_ref[...], gain, scaled, inverse, up_ref[...]
    )


def whole(memory=pltpu.VMEM):
    return pl.BlockSpec(memory_space=memory)


def first_pass(scalars, act, gain, qkv, out, upstream):
    seq, model = act.shape[1:]
    width = qkv.shape[1]
    query_width = out.shape[0]
    shape = jax.ShapeDtypeStruct
    return pl.pallas_call(
        first_kernel,
        out_shape=(
            shape((seq, model), BF16),
            shape((seq, model), BF16),
            shape((seq, query_width), BF16),
            shape((seq, width), BF16),
            shape((1, model), F32),
        ),
        in_specs=[whole(pltpu.SMEM)] + [whole(pl.ANY)] * 4 + [whole()],
        out_specs=[whole()] * 5,
        scratch_shapes=[
            pltpu.VMEM((seq, model), BF16),
            pltpu.VMEM((model, width), BF16),
            pltpu.VMEM((query_width, model), BF16),
            pltpu.VMEM((seq, model), BF16),
            pltpu.VMEM((HEADS // 2, seq, 2 * seq), BF16),
            pltpu.SemaphoreType.DMA((4,)),
        ],
        compiler_params=pltpu.CompilerParams(vmem_limit_bytes=VMEM_LIMIT),
        cost_estimate=pl.CostEstimate(flops=2 * 10**9, bytes_accessed=6 * 10**6, transcendentals=HEADS * seq * seq),
        name="first_pass",
    )(scalars, act, qkv, out, upstream, gain)


def forward_kernel(
    scalars, act, qkv_hbm, gain_ref, normed_ref, project_ref, attended_ref, soft_ref, x_ref, qkv_ref, sems, *, query_width
):
    copies = [
        pltpu.make_async_copy(act.at[scalars[0]], x_ref, sems.at[0]),
        pltpu.make_async_copy(qkv_hbm, qkv_ref, sems.at[1]),
    ]
    for copy in copies:
        copy.start()
    copies[0].wait()
    _, _, normed = normalise(x_ref[...], gain_ref[...])
    normed_ref[...] = normed
    copies[1].wait()
    project = dot(normed, qkv_ref[...]).astype(BF16)
    project_ref[...] = project
    attended = forward_heads(project, scalars[1], query_width, soft_ref)
    attended_ref[...] = jnp.concatenate([a.astype(BF16) for a in attended], axis=1)


def forward_pass(scalars, act, gain, qkv, query_width):
    seq, model = act.shape[1:]
    width = qkv.shape[1]
    shape = jax.ShapeDtypeStruct
    return pl.pallas_call(
        functools.partial(forward_kernel, query_width=query_width),
        out_shape=(
            shape((seq, model), BF16),
            shape((seq, width), BF16),
            shape((seq, query_width), BF16),
            shape((HEADS // 2, seq, 2 * seq), BF16),
        ),
        in_specs=[whole(pltpu.SMEM)] + [whole(pl.ANY)] * 2 + [whole()],
        out_specs=[whole()] * 4,
        scratch_shapes=[
            pltpu.VMEM((seq, model), BF16),
            pltpu.VMEM((model, width), BF16),
            pltpu.SemaphoreType.DMA((2,)),
        ],
        compiler_params=pltpu.CompilerParams(vmem_limit_bytes=VMEM_LIMIT),
        cost_estimate=pl.CostEstimate(flops=10**9, bytes_accessed=4 * 10**6, transcendentals=HEADS * seq * seq),
        name="forward_pass",
    )(scalars, act, qkv, gain)


def hand_out(blocks, scalars, send_ref, keep_ref):
    parts = blocks.shape[0]
    replica = scalars[3]
    for k in range(parts - 1):
        send_ref[k] = blocks[lax.rem(replica + 1 + k, parts)]
    keep_ref[...] = blocks[replica]


def outproj_kernel(scalars, att1, att2, up1, moved, seed, send_ref, keep_ref, up_ref, blocks):
    seeded = scalars[2] == 1

    @pl.when(seeded)
    def _():
        up_ref[...] = seed[...]

    @pl.when(jnp.logical_not(seeded))
    def _():
        up_ref[...] = moved[...]

    parts, rows, model = blocks.shape
    total = dot(att1[...], up1[...], TN) + dot(att2[...], up_ref[...], TN)
    for q in range(parts):
        blocks[q] = total[q * rows : (q + 1) * rows].astype(BF16)
    hand_out(blocks, scalars, send_ref, keep_ref)


def outproj_pass(scalars, att1, att2, up1, moved, seed, parts):
    seq, model = up1.shape
    rows = att1.shape[1] // parts
    shape = jax.ShapeDtypeStruct
    return pl.pallas_call(
        outproj_kernel,
        out_shape=(shape((parts - 1, rows, model), BF16), shape((rows, model), BF16), shape((seq, model), BF16)),
        in_specs=[whole(pltpu.SMEM)] + [whole()] * 5,
        out_specs=[whole()] * 3,
        scratch_shapes=[pltpu.VMEM((parts, rows, model), BF16)],
        compiler_params=pltpu.CompilerParams(vmem_limit_bytes=VMEM_LIMIT),
        cost_estimate=pl.CostEstimate(flops=10**9, bytes_accessed=4 * 10**6, transcendentals=0),
        name="outproj_pass",
    )(scalars, att1, att2, up1, moved, seed)


def second_kernel(
    scalars, act, project_ref, attended_ref, soft_ref, normed2, normed1, gproj1, gain1, up_ref, qkv_ref, out_ref, gain_ref,
    grad_ref, send_ref, keep_ref,
    x_ref, gproj2, blocks, sem,
):
    copy = pltpu.make_async_copy(act.at[scalars[0]], x_ref, sem)
    copy.start()
    query_width = out_ref.shape[0]
    wide = 2 * query_width // HEADS
    gain = gain_ref[...]
    grad_attended = dot(up_ref[...], out_ref[...], NT).astype(BF16)
    attended = [attended_ref[:, p * wide : (p + 1) * wide] for p in range(HEADS // 2)]
    gproj2[...] = backward_heads(project_ref[...], attended, grad_attended, query_width, soft_ref)
    copy.wait()
    inverse, scaled, _ = normalise(x_ref[...], gain)
    grad_ref[...], grad_gain = input_gradient(gproj2[...], qkv_ref[...], gain, scaled, inverse, up_ref[...])
    grad_gain = grad_gain + gain1[...]
    parts, height, width = blocks.shape
    rows = normed1.shape[1] // parts
    pad = height - rows
    for q in range(parts):
        at = slice(q * rows, (q + 1) * rows)
        total = dot(normed1[:, at], gproj1[...], TN) + dot(normed2[:, at], gproj2[...], TN)
        blocks[q, :rows, :] = total.astype(BF16)
        blocks[q, rows:, :] = jnp.zeros((pad, width), BF16)
        blocks[q, rows:, :rows] = jnp.broadcast_to(grad_gain[:, at], (pad, rows)).astype(BF16)
    hand_out(blocks, scalars, send_ref, keep_ref)


def second_pass(scalars, act, forward, first, upstream, gain, qkv, out, parts):
    seq, model = act.shape[1:]
    width = qkv.shape[1]
    height = model // parts + PAD
    normed2, project2, attended2, soft2 = forward
    shape = jax.ShapeDtypeStruct
    return pl.pallas_call(
        second_kernel,
        out_shape=(
            shape((seq, model), BF16),
            shape((parts - 1, height, width), BF16),
            shape((height, width), BF16),
        ),
        in_specs=[whole(pltpu.SMEM), whole(pl.ANY)] + [whole()] * 11,
        out_specs=[whole()] * 3,
        scratch_shapes=[
            pltpu.VMEM((seq, model), BF16),
            pltpu.VMEM((seq, width), BF16),
            pltpu.VMEM((parts, height, width), BF16),
            pltpu.SemaphoreType.DMA(()),
        ],
        compiler_params=pltpu.CompilerParams(vmem_limit_bytes=VMEM_LIMIT),
        cost_estimate=pl.CostEstimate(flops=2 * 10**9, bytes_accessed=6 * 10**6, transcendentals=0),
        name="second_pass",
    )(scalars, act, project2, attended2, soft2, normed2, first[1], first[3], first[4], upstream, qkv, out, gain)


def shifted(value, axis, steps):
    count = lax.axis_size(axis)
    first, last = (max(0, -steps), min(count, count - steps))
    return lax.ppermute(value, axis, [(source, source + steps) for source in range(first, last)])


def mirrored(value, axis):
    count = lax.axis_size(axis)
    return lax.ppermute(value, axis, [(i, count - 1 - i) for i in range(count)])


def replica_sum(send, keep, axis):
    parts = lax.axis_size(axis)
    total = keep.astype(F32)
    for k in range(parts - 1):
        moved = lax.ppermute(send[k], axis, [(i, (i + 1 + k) % parts) for i in range(parts)])
        total = total + moved.astype(F32)
    return total


def shards(
    act_down, act_up, grad_down, grad_up, seed_down, seed_up, gain_down, qkv_down, outproj_down,
    gain_up, qkv_up, outproj_up, doc_offsets, slot_order,
):
    section = lax.axis_index("section")
    sections = lax.axis_size("section")
    replica = lax.axis_index("dp")
    parts = lax.axis_size("dp")
    query_width = outproj_down.shape[1]
    model = act_down.shape[3]

    def scalars(direction, slot):
        which = slot_order[direction, 0, slot]
        offset = doc_offsets[direction, 0, which, 0]
        edge = section == (sections - 1 if direction == 0 else 0)
        return jnp.stack([which, offset, edge.astype(jnp.int32), replica]).astype(jnp.int32)

    up_one = first_pass(scalars(1, 0), act_up[0], gain_up, qkv_up[0], outproj_up[0], grad_up[0])
    up_moved = shifted(up_one[0], "section", 1)
    down_one = first_pass(scalars(0, 0), act_down[0], gain_down, qkv_down[0], outproj_down[0], grad_down[0])
    down_moved = shifted(down_one[0], "section", -1)
    up_forward = forward_pass(scalars(1, 1), act_up[0], gain_up, qkv_up[0], query_width)
    down_forward = forward_pass(scalars(0, 1), act_down[0], gain_down, qkv_down[0], query_width)
    up_out_send, up_out_keep, up_stream = outproj_pass(
        scalars(1, 1), up_one[2], up_forward[2], grad_up[0], up_moved, seed_up, parts
    )
    up_out = replica_sum(up_out_send, up_out_keep, "dp").astype(BF16)
    mirror_out = mirrored(up_out, "section")
    up_two, up_send, up_keep = second_pass(
        scalars(1, 1), act_up[0], up_forward, up_one, up_stream, gain_up, qkv_up[0], outproj_up[0], parts
    )
    up_qkv = replica_sum(up_send, up_keep, "dp").astype(BF16)
    mirror_qkv = mirrored(up_qkv, "section")
    down_out_send, down_out_keep, down_stream = outproj_pass(
        scalars(0, 1), down_one[2], down_forward[2], grad_down[0], down_moved, seed_down, parts
    )
    down_two, down_send, down_keep = second_pass(
        scalars(0, 1), act_down[0], down_forward, down_one, down_stream, gain_down, qkv_down[0], outproj_down[0], parts
    )
    down_out = replica_sum(down_out_send, down_out_keep, "dp")
    down_qkv = replica_sum(down_send, down_keep, "dp")
    rows = model // parts
    grad_outproj = down_out + mirror_out.astype(F32)
    grad_qkv = down_qkv[:rows] + mirror_qkv[:rows].astype(F32)
    grad_gain = down_qkv[rows, :rows] + mirror_qkv[rows, :rows].astype(F32)
    input_grads = jnp.stack(
        [jnp.stack([down_one[0], down_two], axis=0), jnp.stack([up_one[0], up_two], axis=0)], axis=0
    )[:, None]
    return (input_grads, grad_gain[None], grad_qkv[None], grad_outproj[None])


def solution(mesh):
    return jax.shard_map(
        shards,
        mesh=mesh,
        in_specs=(
            P("section", None, "dp", None),
            P("section", None, "dp", None),
            P("section", "dp", None),
            P("section", "dp", None),
            P("dp", None),
            P("dp", None),
            P("section", None),
            P("section", None, None),
            P("section", None, None),
            P("section", None),
            P("section", None, None),
            P("section", None, None),
            P(None, "section", None, "dp"),
            P(None, "section", None),
        ),
        out_specs=(
            P(None, "section", None, "dp", None),
            P("section", "dp"),
            P("section", "dp", None),
            P("section", "dp", None),
        ),
        check_vma=False,
    )
```

time: 295 us -> 127 us (0.43); the launches traced: 289 us -> 126 us
  matrix products: 114 us -> 0 us
  waiting for transfers between devices: 93.5 us -> 54.6 us
  Pallas kernels: 0 us -> 31.1 us
  between operations: 23.1 us -> 8.7 us
  other arithmetic: 24.8 us -> 10.7 us
  starting transfers between devices: 19.7 us -> 12.7 us
  local copies, waits for them, and re-layouts: 13.6 us -> 8.37 us
    dot_general x40 -> x0, matrix products: 104 us -> none  [the longest x4 18.2 us: backward_layer(): jnp.einsum('ghij,igha->jga', grad_scores, queries, preferred_element_type...]
    ppermute x12 -> x6, waiting for transfers between devices: 93.4 us -> 54.6 us  [the longest x2 54.6 us: mirrored(): return lax.ppermute(value, axis, [(i, count - 1 - i) for i in range(count)])]
    pallas_call x0 -> x8, Pallas kernels: none -> 31.1 us  [the longest x2 12.2 us: first_pass(): pl.pallas_call(first_kernel, out_shape=(shape((seq, model), BF16), shape(...]
    sub x4 -> x0, matrix products: 10.8 us -> none  [backward_layer(): raised = jnp.exp(scores - row_top)]
    ppermute x12 -> x6, starting transfers between devices: 11.1 us -> 5.07 us  [the longest x2 3.95 us: mirrored(): return lax.ppermute(value, axis, [(i, count - 1 - i) for i in range(count)])]
    slice x23 -> x1, local copies, waits for them, and re-layouts: 7.21 us -> 1.32 us  [scalars(): which = slot_order[direction, 0, slot]]
    add x3 -> x2, other arithmetic: 5.2 us -> 0.74 us  [the longest x1 0.58 us: shards(): grad_gain = down_qkv[rows, :rows] + mirror_qkv[rows, :rows].astype(F32)]
    convert_element_type x4 -> x2, other arithmetic: 3.87 us -> 0.42 us  [the longest x1 0.23 us: shards(): up_qkv = replica_sum(up_send, up_keep, 'dp').astype(BF16)]
  transfers between devices with their start and end apart: 20 -> 8, of which waited for: 8 -> 2; matrix products, arithmetic and copies ran while one was open for 37% -> 5% of each run, Pallas kernels for 0% -> 20%
where the time goes in v1:
time: 127 us; the launch traced here: 126 us
  waiting for transfers between devices  54.6 us (43%)
  Pallas kernels  31.1 us (24%)
  starting transfers between devices  12.7 us (10%)
  other arithmetic  10.7 us (8%)
  between operations  8.7 us (7%)
  local copies, waits for them, and re-layouts  8.37 us (7%)
    ppermute x2, waiting for transfers between devices, mirrored(): return lax.ppermute(value, axis, [(i, count - 1 - i) for i in range(count)])  54.6 us
    pallas_call x2, Pallas kernels, first_pass(): pl.pallas_call(first_kernel, out_shape=(shape((seq, model), BF16), shape(...  12.2 us
    pallas_call x2, Pallas kernels, second_pass(): pl.pallas_call(second_kernel, out_shape=(shape((seq, model), BF16), shape...  8.58 us
    ppermute x2, starting transfers between devices, shifted(): lax.ppermute(value, axis, [(source, source + steps) for source in range(f...  7.64 us
    pallas_call x2, Pallas kernels, forward_pass(): pl.pallas_call(functools.partial(forward_kernel, query_width=query_width)...  7.17 us
    unnamed x34, local copies, waits for them, and re-layouts  5.65 us
    another operation x3, other arithmetic, scalars(): jnp.stack([which, offset, edge.astype(jnp.int32), replica])  5.36 us
    ppermute x2, starting transfers between devices, mirrored(): return lax.ppermute(value, axis, [(i, count - 1 - i) for i in range(count)])  3.95 us
  transfers between devices with their start and end apart: 8, of which 2 were waited for; matrix products, arithmetic and copies ran while one was open for 5% of the time, Pallas kernels for 20%

profile of v1, /device:TPU:16, one launch (start us, length us, event | category | flops | bytes accessed | tf_op | source)
XLA Modules:
  0.0 126.2 jit_solution(1194111004407935803)
XLA Ops:
  0.6 1.3 %fusion.2 = (s32[1,1,1]{2,1,0:T(1,128)}, s32[1,1,1]{2,1,0:T(1,128)}, s32[1,1,1]{2,1,0:T(1,128)}, s32[1,1,1]{2,1,0:T(1,128)}) fusion(s32[2,1,2]{2,1,0:T(1,128)} %param.27), kind=kLoop, calls=%fused_computation.19 | loop fusion | bytes 32 | tf_op jit(solution)/shard_map/slice | solution.py:375
  9.7 1.4 %constant_dynamic-slice_fusion.3 = (s32[1,1,1,1]{2,3,1,0:T(1,128)}, s32[1,1,1,1]{2,3,1,0:T(1,128)}, s32[1,1,1,1]{2,3,1,0:T(1,128)}, s32[1,1,1,1]{2,3,1,0:T(1,128)}) fusion(s32[2,1,2,1]{2,3,1,0:T(1,128)} %param.26, s32[]{:T(128)S(6)} %select_n.16, s32[]{:T(128)S(6)} %select_n.17, s32[]{:T(128)S(6)} %select_n.19, s32[]{:T(128)S(6)} %select_n.18), kind=kLoop, calls=%fused_computation.14 | loop fusion | bytes 48 | tf_op jit(solution)/shard_map/dynamic_slice | solution.py:376
  11.1 2.6 %add_add_fusion = (s32[4]{0:T(128)S(1)}, s32[4]{0:T(128)S(1)}) fusion(s32[1]{0:T(128)} %bitcast.2, s32[1]{0:T(128)} %bitcast, s32[1]{0:T(128)} %bitcast.3, s32[1]{0:T(128)} %bitcast.4, s32[1]{0:T(128)} %bitcast.18, s32[1]{0:T(128)} %bitcast.17, s32[1]{0:T(128)} %bitcast.15), kind=kLoop, calls=%fused_computation.15 | loop fusion | flops 24 | bytes 60 | tf_op jit(solution)/shard_map/stack | solution.py:378
  13.8 1.4 %copy-done = bf16[1,1024,768]{2,1,0:T(8,128)(2,1)S(1)} copy-done((bf16[1,1024,768]{2,1,0:T(8,128)(2,1)S(1)}, bf16[1,1024,768]{2,1,0:T(8,128)(2,1)}, u32[]{:S(2)}) %copy-start) | copy-done | bytes 1572888
  15.2 1.2 copy-done.3
  16.4 1.2 copy-done.5
  17.6 1.0 copy-done.9
  18.7 0.7 copy-done.14
  19.4 0.0 copy-start.16
  19.4 6.1 %first_pass.3 = (bf16[256,1024]{1,0:T(8,128)(2,1)S(1)}, bf16[256,1024]{1,0:T(8,128)(2,1)S(1)}, bf16[256,512]{1,0:T(8,128)(2,1)S(1)}, bf16[256,768]{1,0:T(8,128)(2,1)S(1)}, f32[1,1024]{1,0:T(1,128)S(1)}) custom-call(s32[4]{0:T(128)S(1)} %get-tuple-element.77.scalars, bf16[2,256,1024]{2,1,0:T(8,128)(2,1)S(1)} %bitcast.53, bf16[1024,768]{1,0:T(8,128)(2,1)S(1)} %bitcast.47, ...), custom_call_target="tpu_custom_call" | custom-call | flops 2000000000 | bytes 6000000 | tf_op jit(solution)/shard_map/first_pass/pallas_call | solution.py:176
  25.5 3.4 %collective-permute-start.1 = (bf16[256,1024]{1,0:T(8,128)(2,1)S(1)}, bf16[256,1024]{1,0:T(8,128)(2,1)S(1)}, u32[]{:S(2)}, u32[]{:S(2)}) collective-permute-start(bf16[256,1024]{1,0:T(8,128)(2,1)S(1)} %get-tuple-element.45), channel_id=1, source_target_pairs={{0,2},{2,4},{4,6},{6,8},{8,10},{10,12},{12,14},{14,16},{16,18},{18... | collective-permute-start | bytes 1572872 | tf_op jit(solution)/shard_map/ppermute | solution.py:346
  28.9 0.0 copy-start.1
  28.9 0.0 copy-start.4
  29.0 0.0 copy-start.15
  29.0 6.1 %first_pass.2 = (bf16[256,1024]{1,0:T(8,128)(2,1)S(1)}, bf16[256,1024]{1,0:T(8,128)(2,1)S(1)}, bf16[256,512]{1,0:T(8,128)(2,1)S(1)}, bf16[256,768]{1,0:T(8,128)(2,1)S(1)}, f32[1,1024]{1,0:T(1,128)S(1)}) custom-call(s32[4]{0:T(128)S(1)} %get-tuple-element.76.scalars, bf16[2,256,1024]{2,1,0:T(8,128)(2,1)S(1)} %bitcast.58, bf16[1024,768]{1,0:T(8,128)(2,1)S(1)} %bitcast.50, ...), custom_call_target="tpu_custom_call" | custom-call | flops 2000000000 | bytes 6000000 | tf_op jit(solution)/shard_map/first_pass/pallas_call | solution.py:176
  35.1 4.3 %collective-permute-start = (bf16[256,1024]{1,0:T(8,128)(2,1)S(1)}, bf16[256,1024]{1,0:T(8,128)(2,1)S(1)}, u32[]{:S(2)}, u32[]{:S(2)}) collective-permute-start(bf16[256,1024]{1,0:T(8,128)(2,1)S(1)} %get-tuple-element.34), channel_id=1, source_target_pairs={{2,0},{4,2},{6,4},{8,6},{10,8},{12,10},{14,12},{16,14},{18,16},{20... | collective-permute-start | bytes 1572872 | tf_op jit(solution)/shard_map/ppermute | solution.py:346
  39.3 1.3 %add_add_fusion.3.scalars = s32[4]{0:T(128)S(1)} fusion(s32[1]{0:T(128)} %bitcast.26, s32[1]{0:T(128)} %bitcast.24, s32[1]{0:T(128)} %bitcast.18, s32[1]{0:T(128)} %bitcast.4), kind=kLoop, calls=%fused_computation.18 | loop fusion | flops 12 | bytes 32 | tf_op jit(solution)/shard_map/stack | solution.py:378
  40.7 0.0 copy-start.10
  40.7 0.0 copy-start.11
  40.7 3.6 %forward_pass.3 = (bf16[256,1024]{1,0:T(8,128)(2,1)S(1)}, bf16[256,768]{1,0:T(8,128)(2,1)S(1)}, bf16[256,512]{1,0:T(8,128)(2,1)S(1)}, bf16[4,256,512]{2,1,0:T(8,128)(2,1)S(1)}) custom-call(s32[4]{0:T(128)S(1)} %add_add_fusion.3.scalars, bf16[2,256,1024]{2,1,0:T(8,128)(2,1)S(1)} %bitcast.54, bf16[1024,768]{1,0:T(8,128)(2,1)S(1)} %bitcast.48, ...), custom_call_target="tpu_custom_call" | custom-call | flops 1000000000 | bytes 4000000 | tf_op jit(solution)/shard_map/forward_pass/pallas_call | solution.py:224
  44.3 0.0 collective-permute-done.1.moved
  44.3 0.0 copy-start.6
  44.3 1.6 %outproj_pass.3 = (bf16[1,256,1024]{2,1,0:T(8,128)(2,1)S(1)}, bf16[256,1024]{1,0:T(8,128)(2,1)S(1)}, bf16[256,1024]{1,0:T(8,128)(2,1)S(1)}) custom-call(s32[4]{0:T(128)S(1)} %add_add_fusion.3.scalars, bf16[256,512]{1,0:T(8,128)(2,1)S(1)} %get-tuple-element.53.att1, bf16[256,512]{1,0:T(8,128)(2,1)S(1)} %get-tuple-element.47.att2.attended_ref, ...), custom_call_target="tpu_custom_call" | custom-call | flops 1000000000 | bytes 4000000 | tf_op jit(solution)/shard_map/outproj_pass/pallas_call | solution.py:275
  46.0 0.1 collective-permute-start.6
  46.1 4.3 %second_pass.3 = (bf16[256,1024]{1,0:T(8,128)(2,1)S(1)}, bf16[1,528,768]{2,1,0:T(8,128)(2,1)S(1)}, bf16[528,768]{1,0:T(8,128)(2,1)S(1)}) custom-call(s32[4]{0:T(128)S(1)} %add_add_fusion.3.scalars, bf16[2,256,1024]{2,1,0:T(8,128)(2,1)S(1)} %bitcast.55, bf16[256,768]{1,0:T(8,128)(2,1)S(1)} %get-tuple-element.46.project_ref, ...), custom_call_target="tpu_custom_call" | custom-call | flops 2000000000 | bytes 6000000 | tf_op jit(solution)/shard_map/second_pass/pallas_call | solution.py:322
  50.4 0.5 collective-permute-start.3
  50.9 1.4 %add_add_fusion.1.scalars = s32[4]{0:T(128)S(1)} fusion(s32[1]{0:T(128)} %bitcast.12, s32[1]{0:T(128)} %bitcast.10, s32[1]{0:T(128)} %bitcast.3, s32[1]{0:T(128)} %bitcast.4), kind=kLoop, calls=%fused_computation.16 | loop fusion | flops 12 | bytes 32 | tf_op jit(solution)/shard_map/stack | solution.py:378
  52.3 3.6 %forward_pass.2 = (bf16[256,1024]{1,0:T(8,128)(2,1)S(1)}, bf16[256,768]{1,0:T(8,128)(2,1)S(1)}, bf16[256,512]{1,0:T(8,128)(2,1)S(1)}, bf16[4,256,512]{2,1,0:T(8,128)(2,1)S(1)}) custom-call(s32[4]{0:T(128)S(1)} %add_add_fusion.1.scalars, bf16[2,256,1024]{2,1,0:T(8,128)(2,1)S(1)} %bitcast.59, bf16[1024,768]{1,0:T(8,128)(2,1)S(1)} %bitcast.51, ...), custom_call_target="tpu_custom_call" | custom-call | flops 1000000000 | bytes 4000000 | tf_op jit(solution)/shard_map/forward_pass/pallas_call | solution.py:224
  55.9 0.0 collective-permute-done.moved
  55.9 1.5 %outproj_pass.2 = (bf16[1,256,1024]{2,1,0:T(8,128)(2,1)S(1)}, bf16[256,1024]{1,0:T(8,128)(2,1)S(1)}, bf16[256,1024]{1,0:T(8,128)(2,1)S(1)}) custom-call(s32[4]{0:T(128)S(1)} %add_add_fusion.1.scalars, bf16[256,512]{1,0:T(8,128)(2,1)S(1)} %get-tuple-element.42.att1, bf16[256,512]{1,0:T(8,128)(2,1)S(1)} %get-tuple-element.36.att2.attended_ref, ...), custom_call_target="tpu_custom_call" | custom-call | flops 1000000000 | bytes 4000000 | tf_op jit(solution)/shard_map/outproj_pass/pallas_call | solution.py:275
  57.4 0.1 collective-permute-start.5
  57.5 4.3 %second_pass.2 = (bf16[256,1024]{1,0:T(8,128)(2,1)S(1)}, bf16[1,528,768]{2,1,0:T(8,128)(2,1)S(1)}, bf16[528,768]{1,0:T(8,128)(2,1)S(1)}) custom-call(s32[4]{0:T(128)S(1)} %add_add_fusion.1.scalars, bf16[2,256,1024]{2,1,0:T(8,128)(2,1)S(1)} %bitcast.60, bf16[256,768]{1,0:T(8,128)(2,1)S(1)} %get-tuple-element.35.project_ref, ...), custom_call_target="tpu_custom_call" | custom-call | flops 2000000000 | bytes 6000000 | tf_op jit(solution)/shard_map/second_pass/pallas_call | solution.py:322
  61.8 0.4 collective-permute-start.2
  62.2 0.1 maximum_bitcast_fusion.1
  62.3 0.0 collective-permute-done.6
  62.3 0.2 add_convert_fusion.1
  62.5 0.6 collective-permute-start.7
  63.1 0.0 collective-permute-done.3
  63.1 0.2 add_convert_fusion
  63.4 3.4 %collective-permute-start.4 = (bf16[528,768]{1,0:T(8,128)(2,1)S(1)}, bf16[528,768]{1,0:T(8,128)(2,1)S(1)}, u32[]{:S(2)}, u32[]{:S(2)}) collective-permute-start(bf16[528,768]{1,0:T(8,128)(2,1)S(1)} %add_convert_fusion), channel_id=1, source_target_pairs={{0,30},{2,28},{4,26},{6,24},{8,22},{10,20},{12,18},{14,16},{16,14}... | collective-permute-start | bytes 2433032 | tf_op jit(solution)/shard_map/ppermute | solution.py:351
  66.7 0.1 maximum_bitcast_fusion.2
  66.8 1.5 %maximum_bitcast_fusion = bf16[2,1,2,256,1024]{4,3,2,1,0:T(8,128)(2,1)} fusion(bf16[1,2,256,1024]{3,2,1,0:T(8,128)(2,1)S(1)} %maximum_bitcast_fusion.2, bf16[1,2,256,1024]{3,2,1,0:T(8,128)(2,1)S(1)} %maximum_bitcast_fusion.1), kind=kLoop, calls=%fused_computation | loop fusion | flops 1048576 | bytes 4194304
  68.3 0.2 convert_add_fusion
  68.5 39.3 %collective-permute-done.7 = bf16[256,1024]{1,0:T(8,128)(2,1)S(1)} collective-permute-done((bf16[256,1024]{1,0:T(8,128)(2,1)S(1)}, bf16[256,1024]{1,0:T(8,128)(2,1)S(1)}, u32[]{:S(2)}, u32[]{:S(2)}) %collective-permute-start.7) | collective-permute-done | bytes 524320 | tf_op jit(solution)/shard_map/ppermute | solution.py:351
  107.8 1.2 add_bitcast_fusion
  109.0 15.3 %collective-permute-done.4 = bf16[528,768]{1,0:T(8,128)(2,1)S(1)} collective-permute-done((bf16[528,768]{1,0:T(8,128)(2,1)S(1)}, bf16[528,768]{1,0:T(8,128)(2,1)S(1)}, u32[]{:S(2)}, u32[]{:S(2)}) %collective-permute-start.4) | collective-permute-done | bytes 811040 | tf_op jit(solution)/shard_map/ppermute | solution.py:351
  124.3 0.6 fusion.1
  124.9 1.3 %fusion = f32[1,512,768]{2,1,0:T(8,128)} fusion(f32[528,768]{1,0:T(8,128)S(1)} %convert_add_fusion, bf16[528,768]{1,0:T(8,128)(2,1)S(1)} %collective-permute-done.4), kind=kLoop, calls=%fused_computation.4 | loop fusion | flops 786432 | bytes 3932160 | tf_op jit(solution)/shard_map/broadcast_in_dim | solution.py:411
  (24 shorter events, 0.0 us)
Async XLA Ops:
  13.8 1.4 %copy-start = (bf16[1,1024,768]{2,1,0:T(8,128)(2,1)S(1)}, bf16[1,1024,768]{2,1,0:T(8,128)(2,1)}, u32[]{:S(2)}) copy-start(bf16[1,1024,768]{2,1,0:T(8,128)(2,1)} %param.24) | copy-start | bytes 4718596
  15.2 1.2 copy-start.3
  16.4 1.2 copy-start.5
  17.6 1.0 copy-start.9
  18.7 0.7 copy-start.14
  19.3 9.5 %copy-start.2 = (bf16[1,1024,768]{2,1,0:T(8,128)(2,1)S(1)}, bf16[1,1024,768]{2,1,0:T(8,128)(2,1)}, u32[]{:S(2)}) copy-start(bf16[1,1024,768]{2,1,0:T(8,128)(2,1)} %param.21) | copy-start | bytes 4718596
  19.3 9.6 %copy-start.7 = (bf16[1,2,256,1024]{3,2,1,0:T(8,128)(2,1)S(1)}, bf16[1,2,256,1024]{3,2,1,0:T(8,128)(2,1)}, u32[]{:S(2)}) copy-start(bf16[1,2,256,1024]{3,2,1,0:T(8,128)(2,1)} %param.14) | copy-start | bytes 3145732
  19.3 9.6 %copy-start.8 = (bf16[1,512,1024]{2,1,0:T(8,128)(2,1)S(1)}, bf16[1,512,1024]{2,1,0:T(8,128)(2,1)}, u32[]{:S(2)}) copy-start(bf16[1,512,1024]{2,1,0:T(8,128)(2,1)} %param.22) | copy-start | bytes 3145732
  19.3 9.6 %copy-start.12 = (bf16[1,256,1024]{2,1,0:T(8,128)(2,1)S(1)}, bf16[1,256,1024]{2,1,0:T(8,128)(2,1)}, u32[]{:S(2)}) copy-start(bf16[1,256,1024]{2,1,0:T(8,128)(2,1)} %param.16) | copy-start | bytes 1572868
  19.4 9.6 %copy-start.16 = (f32[1,1024]{1,0:T(1,128)S(1)}, f32[1,1024]{1,0:T(1,128)}, u32[]{:S(2)}) copy-start(f32[1,1024]{1,0:T(1,128)} %gain_ref.8) | copy-start | bytes 12292
  25.5 18.8 %collective-permute-start.1 = (bf16[256,1024]{1,0:T(8,128)(2,1)S(1)}, bf16[256,1024]{1,0:T(8,128)(2,1)S(1)}, u32[]{:S(2)}, u32[]{:S(2)}) collective-permute-start(bf16[256,1024]{1,0:T(8,128)(2,1)S(1)} %get-tuple-element.45), channel_id=1, source_target_pairs={{0,2},{2,4},{4,6},{6,8},{8,10},{10,12},{12,14},{14,16},{16,18},{18... | collective-permute-start | bytes 1572872 | tf_op jit(solution)/shard_map/ppermute | solution.py:346
  28.9 11.8 %copy-start.1 = (bf16[1,1024,768]{2,1,0:T(8,128)(2,1)S(1)}, bf16[1,1024,768]{2,1,0:T(8,128)(2,1)}, u32[]{:S(2)}) copy-start(bf16[1,1024,768]{2,1,0:T(8,128)(2,1)} %param.24) | copy-start | bytes 4718596
  28.9 11.7 %copy-start.4 = (bf16[1,2,256,1024]{3,2,1,0:T(8,128)(2,1)S(1)}, bf16[1,2,256,1024]{3,2,1,0:T(8,128)(2,1)}, u32[]{:S(2)}) copy-start(bf16[1,2,256,1024]{3,2,1,0:T(8,128)(2,1)} %param.15) | copy-start | bytes 3145732
  29.0 11.7 %copy-start.15 = (f32[1,1024]{1,0:T(1,128)S(1)}, f32[1,1024]{1,0:T(1,128)}, u32[]{:S(2)}) copy-start(f32[1,1024]{1,0:T(1,128)} %gain_ref.11) | copy-start | bytes 12292
  35.1 20.8 %collective-permute-start = (bf16[256,1024]{1,0:T(8,128)(2,1)S(1)}, bf16[256,1024]{1,0:T(8,128)(2,1)S(1)}, u32[]{:S(2)}, u32[]{:S(2)}) collective-permute-start(bf16[256,1024]{1,0:T(8,128)(2,1)S(1)} %get-tuple-element.34), channel_id=1, source_target_pairs={{2,0},{4,2},{6,4},{8,6},{10,8},{12,10},{14,12},{16,14},{18,16},{20... | collective-permute-start | bytes 1572872 | tf_op jit(solution)/shard_map/ppermute | solution.py:346
  40.7 3.6 %copy-start.10 = (bf16[1,256,1024]{2,1,0:T(8,128)(2,1)S(1)}, bf16[1,256,1024]{2,1,0:T(8,128)(2,1)}, u32[]{:S(2)}) copy-start(bf16[1,256,1024]{2,1,0:T(8,128)(2,1)} %param.17) | copy-start | bytes 1572868
  40.7 3.6 %copy-start.11 = (bf16[256,1024]{1,0:T(8,128)(2,1)S(1)}, bf16[256,1024]{1,0:T(8,128)(2,1)}, u32[]{:S(2)}) copy-start(bf16[256,1024]{1,0:T(8,128)(2,1)} %seed.3) | copy-start | bytes 1572868
  44.3 1.7 %copy-start.6 = (bf16[1,512,1024]{2,1,0:T(8,128)(2,1)S(1)}, bf16[1,512,1024]{2,1,0:T(8,128)(2,1)}, u32[]{:S(2)}) copy-start(bf16[1,512,1024]{2,1,0:T(8,128)(2,1)} %param.25) | copy-start | bytes 3145732
  46.0 16.3 %collective-permute-start.6 = (bf16[256,1024]{1,0:T(8,128)(2,1)S(1)}, bf16[256,1024]{1,0:T(8,128)(2,1)S(1)}, u32[]{:S(2)}, u32[]{:S(2)}) collective-permute-start(bf16[256,1024]{1,0:T(8,128)(2,1)S(1)} %bitcast.69), channel_id=1, source_target_pairs={{0,1},{1,0},{2,3},{3,2},{4,5},{5,4},{6,7},{7,6},{8,9},{9,8},{10,11... | collective-permute-start | bytes 1572872 | tf_op jit(solution)/shard_map/ppermute | solution.py:358
  50.4 12.7 %collective-permute-start.3 = (bf16[528,768]{1,0:T(8,128)(2,1)S(1)}, bf16[528,768]{1,0:T(8,128)(2,1)S(1)}, u32[]{:S(2)}, u32[]{:S(2)}) collective-permute-start(bf16[528,768]{1,0:T(8,128)(2,1)S(1)} %bitcast.63), channel_id=1, source_target_pairs={{0,1},{1,0},{2,3},{3,2},{4,5},{5,4},{6,7},{7,6},{8,9},{9,8},{10,11... | collective-permute-start | bytes 2433032 | tf_op jit(solution)/shard_map/ppermute | solution.py:358
  52.3 3.6 %copy-start.13 = (bf16[256,1024]{1,0:T(8,128)(2,1)S(1)}, bf16[256,1024]{1,0:T(8,128)(2,1)}, u32[]{:S(2)}) copy-start(bf16[256,1024]{1,0:T(8,128)(2,1)} %seed.2) | copy-start | bytes 1572868
  57.4 11.1 %collective-permute-start.5 = (bf16[256,1024]{1,0:T(8,128)(2,1)S(1)}, bf16[256,1024]{1,0:T(8,128)(2,1)S(1)}, u32[]{:S(2)}, u32[]{:S(2)}) collective-permute-start(bf16[256,1024]{1,0:T(8,128)(2,1)S(1)} %bitcast.70), channel_id=1, source_target_pairs={{0,1},{1,0},{2,3},{3,2},{4,5},{5,4},{6,7},{7,6},{8,9},{9,8},{10,11... | collective-permute-start | bytes 1572872 | tf_op jit(solution)/shard_map/ppermute | solution.py:358
  61.8 6.5 %collective-permute-start.2 = (bf16[528,768]{1,0:T(8,128)(2,1)S(1)}, bf16[528,768]{1,0:T(8,128)(2,1)S(1)}, u32[]{:S(2)}, u32[]{:S(2)}) collective-permute-start(bf16[528,768]{1,0:T(8,128)(2,1)S(1)} %bitcast.64), channel_id=1, source_target_pairs={{0,1},{1,0},{2,3},{3,2},{4,5},{5,4},{6,7},{7,6},{8,9},{9,8},{10,11... | collective-permute-start | bytes 2433032 | tf_op jit(solution)/shard_map/ppermute | solution.py:358
  62.5 45.2 %collective-permute-start.7 = (bf16[256,1024]{1,0:T(8,128)(2,1)S(1)}, bf16[256,1024]{1,0:T(8,128)(2,1)S(1)}, u32[]{:S(2)}, u32[]{:S(2)}) collective-permute-start(bf16[256,1024]{1,0:T(8,128)(2,1)S(1)} %add_convert_fusion.1), channel_id=1, source_target_pairs={{0,30},{2,28},{4,26},{6,24},{8,22},{10,20},{12,18},{14,16},{16,14}... | collective-permute-start | bytes 1572872 | tf_op jit(solution)/shard_map/ppermute | solution.py:351
  63.4 61.0 %collective-permute-start.4 = (bf16[528,768]{1,0:T(8,128)(2,1)S(1)}, bf16[528,768]{1,0:T(8,128)(2,1)S(1)}, u32[]{:S(2)}, u32[]{:S(2)}) collective-permute-start(bf16[528,768]{1,0:T(8,128)(2,1)S(1)} %add_convert_fusion), channel_id=1, source_target_pairs={{0,30},{2,28},{4,26},{6,24},{8,22},{10,20},{12,18},{14,16},{16,14}... | collective-permute-start | bytes 2433032 | tf_op jit(solution)/shard_map/ppermute | solution.py:351

commit v2 on v1

v2 whole, which is shorter than its diff:
```python
import functools
import math
import jax
import jax.numpy as jnp
from jax import lax
from jax.experimental import pallas as pl
from jax.experimental.pallas import tpu as pltpu
from jax.sharding import PartitionSpec as P

HEADS = 8
KV_HEADS = 2
EPSILON = 1e-05
MASKED = -1e30
PAD = 16
PACKED_PAD = 32
PIECES = 2
PIECES_OUT = 2
PIECES_QKV = 3
VMEM_LIMIT = 24 * 1024 * 1024
FIRST_LIMIT = 60 * 1024 * 1024
F32 = jnp.float32
BF16 = jnp.bfloat16
NN = (((1,), (0,)), ((), ()))
NT = (((1,), (1,)), ((), ()))
TN = (((0,), (0,)), ((), ()))


def dot(a, b, dims=NN):
    return lax.dot_general(a, b, dims, preferred_element_type=F32)


def doubled(pair, half):
    wide = pair.astype(F32)
    turned = pltpu.roll(wide, half, 1)
    left = lax.broadcasted_iota(jnp.int32, wide.shape, 1) < half
    zero = jnp.zeros_like(wide)
    out = []
    for g in range(KV_HEADS):
        a, b = (wide, turned) if g == 0 else (turned, wide)
        out.append(
            jnp.concatenate([jnp.where(left, a, zero), jnp.where(left, zero, b)], axis=0).astype(BF16)
        )
    return out


def mask_bias(seq, offset):
    row = lax.broadcasted_iota(jnp.int32, (seq, seq), 0)
    col = lax.broadcasted_iota(jnp.int32, (seq, seq), 1)
    start = jnp.where(row >= offset, offset, 0)
    return jnp.where((col <= row) & (col >= start), 0.0, MASKED).astype(F32)


def normalise(x, gain):
    xf = x.astype(F32)
    inverse = lax.rsqrt(jnp.mean(xf * xf, axis=1, keepdims=True) + EPSILON)
    scaled = xf * inverse
    return inverse, scaled, (scaled * gain).astype(BF16)


def forward_heads(project, offset, query_width, soft_ref):
    seq = project.shape[0]
    half = query_width // HEADS
    wide = 2 * half
    keys = doubled(project[:, query_width : query_width + wide], half)
    values = doubled(project[:, query_width + wide :], half)
    bias = mask_bias(seq, offset)
    scale = half ** (-0.5)
    pairs = HEADS // 2
    attended = []
    for p in range(pairs):
        g = p * KV_HEADS // pairs
        queries = project[:, p * wide : (p + 1) * wide] * jnp.asarray(scale, BF16)
        scores = dot(queries, keys[g], NT)
        for t in range(2):
            s = scores[:, t * seq : (t + 1) * seq] + bias
            e = jnp.exp(s - jnp.max(s, axis=1, keepdims=True))
            soft = e * (1.0 / jnp.sum(e, axis=1, keepdims=True))
            soft_ref[p, :, t * seq : (t + 1) * seq] = soft.astype(BF16)
        attended.append(dot(soft_ref[p], values[g]))
    return attended


def backward_heads(project, attended, grad_attended, query_width, soft_ref):
    seq = project.shape[0]
    half = query_width // HEADS
    wide = 2 * half
    keys = doubled(project[:, query_width : query_width + wide], half)
    values = doubled(project[:, query_width + wide :], half)
    scale = half ** (-0.5)
    pairs = HEADS // 2
    left = lax.broadcasted_iota(jnp.int32, (seq, wide), 1) < half
    grad_queries = []
    grad_keys = [None] * KV_HEADS
    grad_values = [None] * KV_HEADS
    for p in range(pairs):
        g = p * KV_HEADS // pairs
        queries = project[:, p * wide : (p + 1) * wide] * jnp.asarray(scale, BF16)
        grad_pair = grad_attended[:, p * wide : (p + 1) * wide]
        grad_soft = dot(grad_pair, values[g], NT)
        both = attended[p].astype(F32) * grad_pair.astype(F32)
        rows = [
            jnp.sum(jnp.where(left, both, 0.0), axis=1, keepdims=True),
            jnp.sum(jnp.where(left, 0.0, both), axis=1, keepdims=True),
        ]
        soft = soft_ref[p]
        grad_scores = jnp.concatenate(
            [
                (
                    soft[:, t * seq : (t + 1) * seq].astype(F32)
                    * (grad_soft[:, t * seq : (t + 1) * seq] - rows[t])
                ).astype(BF16)
                for t in range(2)
            ],
            axis=1,
        )
        grad_queries.append(dot(grad_scores, keys[g]) * scale)
        keys_part = dot(queries, grad_scores, TN)
        values_part = dot(grad_pair, soft, TN)
        keys_sum = keys_part[:half, :seq] + keys_part[half:, seq:]
        values_sum = values_part[:half, :seq] + values_part[half:, seq:]
        grad_keys[g] = keys_sum if grad_keys[g] is None else grad_keys[g] + keys_sum
        grad_values[g] = values_sum if grad_values[g] is None else grad_values[g] + values_sum
    columns = grad_queries + [
        jnp.concatenate(grad_keys, axis=0).T,
        jnp.concatenate(grad_values, axis=0).T,
    ]
    return jnp.concatenate([c.astype(BF16) for c in columns], axis=1)


def input_gradient(grad_project, qkv, gain, scaled, inverse, upstream):
    grad_normed = dot(grad_project, qkv, NT)
    grad_hat = grad_normed * gain
    part = grad_normed * scaled
    grad_gain = jnp.sum(part, axis=0, keepdims=True)
    mean = jnp.mean(part * gain, axis=1, keepdims=True)
    grad_in = upstream.astype(F32) + inverse * (grad_hat - scaled * mean)
    return grad_in.astype(BF16), grad_gain


def whole(memory=pltpu.VMEM):
    return pl.BlockSpec(memory_space=memory)


def call(kernel, name, inputs, outputs, scratch, after=(), aliases=None, limit=VMEM_LIMIT):
    count = len(inputs)

    def ordered(*refs):
        kernel(*refs[:count], *refs[count + len(after) :])

    return pl.pallas_call(
        ordered,
        out_shape=tuple(jax.ShapeDtypeStruct(shape, dtype) for shape, dtype, _ in outputs),
        in_specs=[whole(space) for _, space in inputs] + [whole(pl.ANY)] * len(after),
        out_specs=tuple(whole(space) for _, _, space in outputs),
        scratch_shapes=scratch,
        input_output_aliases=aliases or {},
        compiler_params=pltpu.CompilerParams(vmem_limit_bytes=limit),
        cost_estimate=pl.CostEstimate(flops=1, bytes_accessed=1, transcendentals=0),
        name=name,
    )(*(array for array, _ in inputs), *after)


def start_all(sources, targets, sems):
    copies = [pltpu.make_async_copy(a, b, sems.at[i]) for i, (a, b) in enumerate(zip(sources, targets))]
    for copy in copies:
        copy.start()
    return copies


def first_kernel(order, offsets, act, qkv_hbm, out_hbm, up_hbm, gain_hbm, *refs, direction):
    grad_ref, normed_ref, attended_ref, project_ref, gain_out = refs[:5]
    order_ref, offsets_ref, x_ref, qkv_ref, out_ref, up_ref, gain_ref, soft_ref, sems = refs[5:]
    copies = start_all(
        (order, offsets, act, gain_hbm, qkv_hbm, up_hbm, out_hbm),
        (order_ref, offsets_ref, x_ref, gain_ref, qkv_ref, up_ref, out_ref),
        sems,
    )
    query_width = out_hbm.shape[0]
    for copy in copies[:4]:
        copy.wait()
    which = order_ref[direction, 0, 0]
    offset = offsets_ref[direction, 0, which]
    gain = gain_ref[...]
    _, _, normed = normalise(x_ref[which], gain)
    normed_ref[...] = normed
    copies[4].wait()
    project = dot(normed, qkv_ref[...]).astype(BF16)
    attended = forward_heads(project, offset, query_width, soft_ref)
    attended_ref[...] = jnp.concatenate([a.astype(BF16) for a in attended], axis=1)
    copies[5].wait()
    copies[6].wait()
    grad_attended = dot(up_ref[...], out_ref[...], NT).astype(BF16)
    grad_project = backward_heads(project, attended, grad_attended, query_width, soft_ref)
    project_ref[...] = grad_project
    inverse, scaled, _ = normalise(x_ref[which], gain)
    grad_ref[...], gain_out[...] = input_gradient(grad_project, qkv_ref[...], gain, scaled, inverse, up_ref[...])


def first_pass(direction, ints, act, gain, qkv, out, upstream, after=(), limit=VMEM_LIMIT):
    seq, model = act.shape[1:]
    width = qkv.shape[1]
    query_width = out.shape[0]
    hbm, vmem = pltpu.HBM, pltpu.VMEM
    return call(
        functools.partial(first_kernel, direction=direction),
        "first_pass",
        [(a, hbm) for a in (*ints, act, qkv, out, upstream, gain)],
        [
            ((seq, model), BF16, vmem),
            ((seq, model), BF16, vmem),
            ((seq, query_width), BF16, vmem),
            ((seq, width), BF16, vmem),
            ((1, model), F32, vmem),
        ],
        [pltpu.SMEM(a.shape, jnp.int32) for a in ints]
        + [
            pltpu.VMEM(act.shape, BF16),
            pltpu.VMEM((model, width), BF16),
            pltpu.VMEM((query_width, model), BF16),
            pltpu.VMEM((seq, model), BF16),
            pltpu.VMEM((1, model), F32),
            pltpu.VMEM((HEADS // 2, seq, 2 * seq), BF16),
            pltpu.SemaphoreType.DMA((7,)),
        ],
        after,
        limit=limit,
    )


def forward_kernel(order, offsets, act, qkv_hbm, gain_hbm, *refs, direction, query_width):
    normed_ref, project_ref, attended_ref, soft_ref = refs[:4]
    order_ref, offsets_ref, x_ref, qkv_ref, gain_ref, sems = refs[4:]
    copies = start_all(
        (order, offsets, act, gain_hbm, qkv_hbm), (order_ref, offsets_ref, x_ref, gain_ref, qkv_ref), sems
    )
    for copy in copies[:4]:
        copy.wait()
    which = order_ref[direction, 0, 1]
    offset = offsets_ref[direction, 0, which]
    _, _, normed = normalise(x_ref[which], gain_ref[...])
    normed_ref[...] = normed
    copies[4].wait()
    project = dot(normed, qkv_ref[...]).astype(BF16)
    project_ref[...] = project
    attended = forward_heads(project, offset, query_width, soft_ref)
    attended_ref[...] = jnp.concatenate([a.astype(BF16) for a in attended], axis=1)


def forward_pass(direction, ints, act, gain, qkv, query_width, after=()):
    seq, model = act.shape[1:]
    width = qkv.shape[1]
    hbm, vmem = pltpu.HBM, pltpu.VMEM
    return call(
        functools.partial(forward_kernel, direction=direction, query_width=query_width),
        "forward_pass",
        [(a, hbm) for a in (*ints, act, qkv, gain)],
        [
            ((seq, model), BF16, vmem),
            ((seq, width), BF16, vmem),
            ((seq, query_width), BF16, vmem),
            ((HEADS // 2, seq, 2 * seq), BF16, vmem),
        ],
        [pltpu.SMEM(a.shape, jnp.int32) for a in ints]
        + [
            pltpu.VMEM(act.shape, BF16),
            pltpu.VMEM((model, width), BF16),
            pltpu.VMEM((1, model), F32),
            pltpu.SemaphoreType.DMA((5,)),
        ],
        after,
    )


def choose_upstream(direction, moved, seed_hbm, up_ref, sem):
    seeded = lax.axis_index("section") == (lax.axis_size("section") - 1 if direction == 0 else 0)

    @pl.when(seeded)
    def _():
        copy = pltpu.make_async_copy(seed_hbm, up_ref, sem)
        copy.start()
        copy.wait()

    @pl.when(jnp.logical_not(seeded))
    def _():
        up_ref[...] = moved[...]


def backward_kernel(
    order, act, qkv_hbm, out_hbm, gain_hbm, seed_hbm, project_ref, attended_ref, soft_ref, gain1, moved, own,
    *refs, direction, kept,
):
    up_ref, gproj_ref, gain_out, grads_hbm = refs[kept : kept + 4]
    order_ref, x_ref, qkv_ref, out_ref, gain_ref, grad_ref, sems = refs[kept + 4 :]
    copies = start_all(
        (order, act, gain_hbm, out_hbm, qkv_hbm), (order_ref, x_ref, gain_ref, out_ref, qkv_ref), sems
    )
    choose_upstream(direction, moved, seed_hbm, up_ref, sems.at[5])
    copies[3].wait()
    query_width = out_ref.shape[0]
    wide = 2 * query_width // HEADS
    grad_attended = dot(up_ref[...], out_ref[...], NT).astype(BF16)
    attended = [attended_ref[:, p * wide : (p + 1) * wide] for p in range(HEADS // 2)]
    gproj_ref[...] = backward_heads(project_ref[...], attended, grad_attended, query_width, soft_ref)
    for at in (0, 1, 2, 4):
        copies[at].wait()
    gain = gain_ref[...]
    inverse, scaled, _ = normalise(x_ref[order_ref[direction, 0, 1]], gain)
    grad_ref[0] = own[...]
    grad_ref[1], grad_gain = input_gradient(gproj_ref[...], qkv_ref[...], gain, scaled, inverse, up_ref[...])
    gain_out[...] = gain1[...] + grad_gain
    written = pltpu.make_async_copy(grad_ref, grads_hbm.at[direction], sems.at[6])
    written.start()
    written.wait()


def backward_pass(direction, order, act, gain, qkv, out, seed, forward, gain1, moved, own, grads=None, after=()):
    seq, model = act.shape[1:]
    width = qkv.shape[1]
    query_width = out.shape[0]
    hbm, vmem = pltpu.HBM, pltpu.VMEM
    _, project, attended, soft = forward
    inputs = [(a, hbm) for a in (order, act, qkv, out, gain, seed)]
    inputs += [(a, vmem) for a in (project, attended, soft, gain1, moved, own)]
    aliases = {}
    if grads is not None:
        aliases = {len(inputs): 3}
        inputs += [(grads, hbm)]
    return call(
        functools.partial(backward_kernel, direction=direction, kept=len(aliases)),
        "backward_pass",
        inputs,
        [
            ((seq, model), BF16, vmem),
            ((seq, width), BF16, vmem),
            ((1, model), F32, vmem),
            ((2, 2, seq, model), BF16, hbm),
        ],
        [
            pltpu.SMEM(order.shape, jnp.int32),
            pltpu.VMEM(act.shape, BF16),
            pltpu.VMEM((model, width), BF16),
            pltpu.VMEM((query_width, model), BF16),
            pltpu.VMEM((1, model), F32),
            pltpu.VMEM((2, seq, model), BF16),
            pltpu.SemaphoreType.DMA((7,)),
        ],
        after,
        aliases,
    )


def cut(rows, pieces):
    return max(p for p in range(1, pieces + 1) if rows % (16 * p) == 0)


def hand_out(blocks, sends, keep_ref):
    parts = blocks.shape[0]
    replica = lax.axis_index("dp")
    for k in range(parts - 1):
        at = lax.rem(replica + 1 + k, parts)
        for p, ref in enumerate(sends):
            rows = ref.shape[1]
            ref[k] = blocks[at, p * rows : (p + 1) * rows, :]
    keep_ref[...] = blocks[replica]


def outproj_kernel(up_hbm, seed_hbm, att1, att2, moved, *refs, direction):
    *sends, keep_ref, up1_ref, up2_ref, blocks, sems = refs
    copy = pltpu.make_async_copy(up_hbm, up1_ref, sems.at[0])
    copy.start()
    choose_upstream(direction, moved, seed_hbm, up2_ref, sems.at[1])
    parts, rows, _ = blocks.shape
    copy.wait()
    total = dot(att1[...], up1_ref[...], TN) + dot(att2[...], up2_ref[...], TN)
    for q in range(parts):
        blocks[q] = total[q * rows : (q + 1) * rows].astype(BF16)
    hand_out(blocks, sends, keep_ref)


def outproj_pass(direction, att1, att2, upstream, moved, seed, parts, after=()):
    seq, model = moved.shape
    rows = att1.shape[1] // parts
    pieces = cut(rows, PIECES_OUT)
    hbm, vmem = pltpu.HBM, pltpu.VMEM
    *sends, keep = call(
        functools.partial(outproj_kernel, direction=direction),
        "outproj_pass",
        [(upstream, hbm), (seed, hbm), (att1, vmem), (att2, vmem), (moved, vmem)],
        [((parts - 1, rows // pieces, model), BF16, vmem)] * pieces + [((rows, model), BF16, vmem)],
        [
            pltpu.VMEM((seq, model), BF16),
            pltpu.VMEM((seq, model), BF16),
            pltpu.VMEM((parts, rows, model), BF16),
            pltpu.SemaphoreType.DMA((2,)),
        ],
        after,
    )
    return sends, keep


def qkv_kernel(normed1, gproj1, normed2, gproj2, gain, *refs):
    *sends, keep_ref, blocks = refs
    parts, height, width = blocks.shape
    rows = normed1.shape[1] // parts
    for q in range(parts):
        at = slice(q * rows, (q + 1) * rows)
        total = dot(normed1[:, at], gproj1[...], TN) + dot(normed2[:, at], gproj2[...], TN)
        blocks[q, :rows, :] = total.astype(BF16)
        blocks[q, rows:, :] = jnp.zeros((height - rows, width), BF16)
        blocks[q, rows:, :rows] = jnp.broadcast_to(gain[:, at], (height - rows, rows)).astype(BF16)
    hand_out(blocks, sends, keep_ref)


def qkv_pass(normed1, gproj1, normed2, gproj2, gain, parts, after=()):
    rows, width = normed1.shape[1] // parts + PAD, gproj1.shape[1]
    pieces = cut(rows, PIECES_QKV)
    vmem = pltpu.VMEM
    *sends, keep = call(
        qkv_kernel,
        "qkv_pass",
        [(a, vmem) for a in (normed1, gproj1, normed2, gproj2, gain)],
        [((parts - 1, rows // pieces, width), BF16, vmem)] * pieces + [((rows, width), BF16, vmem)],
        [pltpu.VMEM((parts, rows, width), BF16)],
        after,
    )
    return sends, keep


def layout(parts, query_width, model, width):
    unit = math.gcd(model, width)
    out_rows, qkv_rows = query_width // parts, model // parts
    start = out_rows * (model // unit)
    gain_at = start + qkv_rows * (width // unit)
    return unit, out_rows, qkv_rows, start, gain_at, gain_at + PACKED_PAD


def packed_kernel(normed1, gproj1, att1, up1_hbm, normed2, gproj2, att2, up2, gain, *refs):
    *sends, keep_ref, blocks, up1, sem = refs
    copy = pltpu.make_async_copy(up1_hbm, up1, sem)
    copy.start()
    parts = blocks.shape[0]
    model, width = normed1.shape[1], gproj1.shape[1]
    unit, out_rows, qkv_rows, start, gain_at, _ = layout(parts, att1.shape[1], model, width)
    row = lax.broadcasted_iota(jnp.int32, (PACKED_PAD, unit), 0)
    for q in range(parts):
        at = slice(q * qkv_rows, (q + 1) * qkv_rows)
        qkv = dot(normed1[:, at], gproj1[...], TN) + dot(normed2[:, at], gproj2[...], TN)
        for c in range(width // unit):
            first = start + c * qkv_rows
            blocks[q, first : first + qkv_rows, :] = qkv[:, c * unit : (c + 1) * unit].astype(BF16)
        lines = jnp.zeros((PACKED_PAD, unit), F32)
        for i in range(pl.cdiv(qkv_rows, unit)):
            line = gain[:, q * qkv_rows + i * unit : q * qkv_rows + min((i + 1) * unit, qkv_rows)]
            if line.shape[1] < unit:
                line = jnp.concatenate([line, jnp.zeros((1, unit - line.shape[1]), F32)], axis=1)
            lines = jnp.where(row == i, line, lines)
        blocks[q, gain_at:, :] = lines.astype(BF16)
    copy.wait()
    out = dot(att1[...], up1[...], TN) + dot(att2[...], up2[...], TN)
    for q in range(parts):
        for c in range(model // unit):
            blocks[q, c * out_rows : (c + 1) * out_rows, :] = out[
                q * out_rows : (q + 1) * out_rows, c * unit : (c + 1) * unit
            ].astype(BF16)
    hand_out(blocks, sends, keep_ref)


def packed_pass(normed1, gproj1, att1, up1, normed2, gproj2, att2, up2, gain, parts, after=()):
    seq, model = normed1.shape
    unit, _, _, _, _, rows = layout(parts, att1.shape[1], model, gproj1.shape[1])
    pieces = cut(rows, PIECES)
    hbm, vmem = pltpu.HBM, pltpu.VMEM
    *sends, keep = call(
        packed_kernel,
        "packed_pass",
        [(normed1, vmem), (gproj1, vmem), (att1, vmem), (up1, hbm)]
        + [(a, vmem) for a in (normed2, gproj2, att2, up2, gain)],
        [((parts - 1, rows // pieces, unit), BF16, vmem)] * pieces + [((rows, unit), BF16, vmem)],
        [
            pltpu.VMEM((parts, rows, unit), BF16),
            pltpu.VMEM((seq, model), BF16),
            pltpu.SemaphoreType.DMA(()),
        ],
        after,
    )
    return sends, keep


def final_kernel(keep, mirror_out, mirror_qkv, *refs, parts, pieces):
    moved, refs = refs[: (parts - 1) * pieces], refs[(parts - 1) * pieces :]
    gain_hbm, qkv_hbm, out_hbm, gain_ref, qkv_ref, out_ref, sems = refs
    model, width = out_ref.shape[1], qkv_ref.shape[1]
    unit, out_rows, qkv_rows, start, gain_at, rows = layout(parts, out_ref.shape[0] * parts, model, width)
    each = rows // pieces

    def total(first, count):
        result = keep[first : first + count, :].astype(F32)
        for k in range(parts - 1):
            taken, at = [], first
            while at < first + count:
                p = at // each
                until = min(first + count, (p + 1) * each)
                taken.append(moved[k * pieces + p][at - p * each : until - p * each, :].astype(F32))
                at = until
            result = result + (taken[0] if len(taken) == 1 else jnp.concatenate(taken, axis=0))
        return result

    for c in range(width // unit):
        columns = slice(c * unit, (c + 1) * unit)
        qkv_ref[:, columns] = total(start + c * qkv_rows, qkv_rows) + mirror_qkv[:qkv_rows, columns].astype(F32)
    copies = [pltpu.make_async_copy(qkv_ref, qkv_hbm, sems.at[0])]
    copies[0].start()
    for c in range(model // unit):
        columns = slice(c * unit, (c + 1) * unit)
        out_ref[:, columns] = total(c * out_rows, out_rows) + mirror_out[:, columns].astype(F32)
    copies.append(pltpu.make_async_copy(out_ref, out_hbm, sems.at[1]))
    copies[1].start()
    lines = total(gain_at, PACKED_PAD)
    other = mirror_qkv[qkv_rows:, :].astype(F32)
    for i in range(pl.cdiv(qkv_rows, unit)):
        until = min((i + 1) * unit, qkv_rows)
        gain_ref[:, i * unit : until] = lines[i : i + 1, : until - i * unit] + other[:1, i * unit : until]
    copies.append(pltpu.make_async_copy(gain_ref, gain_hbm, sems.at[2]))
    copies[2].start()
    for copy in copies:
        copy.wait()


def final_pass(keep, mirror_out, mirror_qkv, moved, parts, query_width, model, width):
    hbm, vmem = pltpu.HBM, pltpu.VMEM
    shapes = ((1, model // parts), (model // parts, width), (query_width // parts, model))
    return call(
        functools.partial(final_kernel, parts=parts, pieces=len(moved[0])),
        "final_pass",
        [(keep, vmem), (mirror_out, vmem), (mirror_qkv, vmem)] + [(m, vmem) for per in moved for m in per],
        [(shape, F32, hbm) for shape in shapes],
        [pltpu.VMEM(shape, F32) for shape in shapes] + [pltpu.SemaphoreType.DMA((3,))],
    )


def sum_kernel(keep, *refs):
    *moved, sum_ref = refs
    pieces = len(moved)
    at = 0
    for p in range(pieces):
        rows = moved[p].shape[1]
        total = keep[at : at + rows, :].astype(F32)
        for k in range(moved[p].shape[0]):
            total = total + moved[p][k].astype(F32)
        sum_ref[at : at + rows, :] = total.astype(BF16)
        at += rows


def sum_pass(keep, moved, after=()):
    vmem = pltpu.VMEM
    pieces = [jnp.stack([per[p] for per in moved]) if len(moved) > 1 else moved[0][p][None] for p in range(len(moved[0]))]
    (total,) = call(
        sum_kernel, "sum_pass", [(keep, vmem)] + [(p, vmem) for p in pieces], [(keep.shape, BF16, vmem)], [], after
    )
    return total


def shifted(value, axis, steps):
    count = lax.axis_size(axis)
    first, last = (max(0, -steps), min(count, count - steps))
    return lax.ppermute(value, axis, [(source, source + steps) for source in range(first, last)])


def mirrored(value, axis):
    count = lax.axis_size(axis)
    return lax.ppermute(value, axis, [(i, count - 1 - i) for i in range(count)])


def exchanged(sends, axis):
    parts = lax.axis_size(axis)
    return [
        [lax.ppermute(send[k], axis, [(i, (i + 1 + k) % parts) for i in range(parts)]) for send in sends]
        for k in range(parts - 1)
    ]


def shards(
    act_down, act_up, grad_down, grad_up, seed_down, seed_up, gain_down, qkv_down, outproj_down,
    gain_up, qkv_up, outproj_up, doc_offsets, slot_order,
):
    parts = lax.axis_size("dp")
    query_width, model = outproj_down.shape[1:]
    width = qkv_down.shape[2]
    ints = (slot_order, doc_offsets.reshape(slot_order.shape))
    down = (gain_down, qkv_down[0], outproj_down[0])
    up = (gain_up, qkv_up[0], outproj_up[0])

    up_one = first_pass(1, ints, act_up[0], *up, grad_up[0], limit=FIRST_LIMIT)
    up_moved = shifted(up_one[0], "section", 1)
    down_one = first_pass(0, ints, act_down[0], *down, grad_down[0], after=(up_one[3],))
    down_moved = shifted(down_one[0], "section", -1)
    up_forward = forward_pass(1, ints, act_up[0], gain_up, qkv_up[0], query_width, after=(down_one[3],))
    sends, keep = outproj_pass(1, up_one[2], up_forward[2], grad_up[0], up_moved, seed_up, parts)
    up_out = sum_pass(keep, exchanged(sends, "dp"))
    mirror_out = mirrored(up_out, "section")
    up_two = backward_pass(
        1, slot_order, act_up[0], *up, seed_up, up_forward, up_one[4], up_moved, up_one[0], after=(up_out,)
    )
    sends, keep = qkv_pass(up_one[1], up_one[3], up_forward[0], up_two[1], up_two[2], parts, after=(down_moved,))
    up_qkv = sum_pass(keep, exchanged(sends, "dp"), after=(mirror_out,))
    mirror_qkv = mirrored(up_qkv, "section")
    down_forward = forward_pass(0, ints, act_down[0], gain_down, qkv_down[0], query_width, after=(keep,))
    down_two = backward_pass(
        0, slot_order, act_down[0], *down, seed_down, down_forward, down_one[4], down_moved, down_one[0],
        grads=up_two[3], after=(up_qkv,),
    )
    sends, keep = packed_pass(
        down_one[1], down_one[3], down_one[2], grad_down[0],
        down_forward[0], down_two[1], down_forward[2], down_two[0], down_two[2], parts,
    )
    grad_gain, grad_qkv, grad_outproj = final_pass(
        keep, mirror_out, mirror_qkv, exchanged(sends, "dp"), parts, query_width, model, width
    )
    return (down_two[3][:, None], grad_gain, grad_qkv[None], grad_outproj[None])


def solution(mesh):
    return jax.shard_map(
        shards,
        mesh=mesh,
        in_specs=(
            P("section", None, "dp", None),
            P("section", None, "dp", None),
            P("section", "dp", None),
            P("section", "dp", None),
            P("dp", None),
            P("dp", None),
            P("section", None),
            P("section", None, None),
            P("section", None, None),
            P("section", None),
            P("section", None, None),
            P("section", None, None),
            P(None, "section", None, "dp"),
            P(None, "section", None),
        ),
        out_specs=(
            P(None, "section", None, "dp", None),
            P("section", "dp"),
            P("section", "dp", None),
            P("section", "dp", None),
        ),
        check_vma=False,
    )
```

time: 127 us -> 99.9 us (0.79)
  other arithmetic: 10.7 us -> 0 us
  waiting for transfers between devices: 54.6 us -> 45.4 us
  between operations: 8.7 us -> 1.19 us
  local copies, waits for them, and re-layouts: 8.37 us -> 2.13 us
  Pallas kernels: 31.1 us -> 36.3 us
    ppermute x2, waiting for transfers between devices: 54.6 us -> 38 us  [mirrored(): return lax.ppermute(value, axis, [(i, count - 1 - i) for i in range(count)])]
    ppermute x4 -> x7, waiting for transfers between devices: 0.01 us -> 5.68 us  [exchanged(): lax.ppermute(send[k], axis, [(i, (i + 1 + k) % parts) for i in range(part...]
    another operation x5 -> x0, other arithmetic: 5.56 us -> none  [the longest x3 5.36 us: scalars(): jnp.stack([which, offset, edge.astype(jnp.int32), replica])]
    pallas_call x8 -> x12, Pallas kernels: 31.1 us -> 36.3 us  [call(): pl.pallas_call(ordered, out_shape=tuple((jax.ShapeDtypeStruct(shape, dtyp...]
    unnamed x34 -> x42, local copies, waits for them, and re-layouts: 5.65 us -> 2.13 us
    broadcast_in_dim x2 -> x0, other arithmetic: 2.52 us -> none  [shards(): return (input_grads, grad_gain[None], grad_qkv[None], grad_outproj[None])]
    ppermute x2, waiting for transfers between devices: 0.01 us -> 1.74 us  [shifted(): lax.ppermute(value, axis, [(source, source + steps) for source in range(f...]
    unnamed x1 -> x0, other arithmetic: 1.5 us -> none
  transfers between devices with their start and end apart: 8 -> 11, of which waited for: 2 -> 10; matrix products, arithmetic and copies ran while one was open for 5% -> 0% of each run, Pallas kernels for 20% -> 27%
where the time goes in v2:
time: 99.9 us; the launch traced here: 99 us
  waiting for transfers between devices  45.4 us (45%)
  Pallas kernels  36.3 us (36%)
  starting transfers between devices  13.9 us (14%)
  local copies, waits for them, and re-layouts  2.13 us (2%)
  between operations  1.19 us (1%)
    ppermute x2, waiting for transfers between devices, mirrored(): return lax.ppermute(value, axis, [(i, count - 1 - i) for i in range(count)])  38 us
    pallas_call x12, Pallas kernels, call(): pl.pallas_call(ordered, out_shape=tuple((jax.ShapeDtypeStruct(shape, dtyp...  36.3 us
    ppermute x2, starting transfers between devices, shifted(): lax.ppermute(value, axis, [(source, source + steps) for source in range(f...  7.77 us
    ppermute x7, waiting for transfers between devices, exchanged(): lax.ppermute(send[k], axis, [(i, (i + 1 + k) % parts) for i in range(part...  5.68 us
    ppermute x2, starting transfers between devices, mirrored(): return lax.ppermute(value, axis, [(i, count - 1 - i) for i in range(count)])  4.39 us
    unnamed x42, local copies, waits for them, and re-layouts  2.13 us
  transfers between devices with their start and end apart: 11, of which 10 were waited for; matrix products, arithmetic and copies ran while one was open for 0% of the time, Pallas kernels for 27%

profile of v2, /device:TPU:16, one launch (start us, length us, event | category | flops | bytes accessed | tf_op | source)
XLA Modules:
  0.0 99.0 jit_solution(6972991278340091912)
XLA Ops:
  0.7 7.8 %first_pass.2 = (bf16[256,1024]{1,0:T(8,128)(2,1)}, bf16[256,1024]{1,0:T(8,128)(2,1)}, bf16[256,512]{1,0:T(8,128)(2,1)}, bf16[256,768]{1,0:T(8,128)(2,1)}, f32[1,1024]{1,0:T(1,128)}) custom-call(s32[2,1,2]{2,1,0:T(1,128)} %refs_0_.11, s32[2,1,2]{2,1,0:T(1,128)} %bitcast.53, bf16[2,256,1024]{2,1,0:T(8,128)(2,1)} %bitcast.34, bf16[1024,768]{1,0:T(8,128)(2,1)} %bitcast.31, ...), custom_call_target="tpu_custom_call" | custom-call | flops 1 | bytes 1 | tf_op jit(solution)/shard_map/first_pass/pallas_call | solution.py:150
  8.5 3.4 %collective-permute-start = (bf16[256,1024]{1,0:T(8,128)(2,1)}, bf16[256,1024]{1,0:T(8,128)(2,1)S(1)}, u32[]{:S(2)}, u32[]{:S(2)}) collective-permute-start(bf16[256,1024]{1,0:T(8,128)(2,1)} %get-tuple-element.50.refs_11_), channel_id=1, source_target_pairs={{0,2},{2,4},{4,6},{6,8},{8,10},{10,12},{12,14},{14,16},{16,18},{18... | collective-permute-start | bytes 1572872 | tf_op jit(solution)/shard_map/ppermute | solution.py:566
  12.0 0.0 copy-start.8
  12.0 1.0 %copy-done.8 = bf16[1,256,1024]{2,1,0:T(8,128)(2,1)S(1)} copy-done((bf16[1,256,1024]{2,1,0:T(8,128)(2,1)S(1)}, bf16[1,256,1024]{2,1,0:T(8,128)(2,1)}, u32[]{:S(2)}) %copy-start.8) | copy-done | bytes 524312
  13.0 1.0 %copy-done.10 = bf16[256,768]{1,0:T(8,128)(2,1)S(1)} copy-done((bf16[256,768]{1,0:T(8,128)(2,1)S(1)}, bf16[256,768]{1,0:T(8,128)(2,1)}, u32[]{:S(2)}) %copy-start.10) | copy-done | bytes 393240
  14.0 5.9 %first_pass.3 = (bf16[256,1024]{1,0:T(8,128)(2,1)S(1)}, bf16[256,1024]{1,0:T(8,128)(2,1)S(1)}, bf16[256,512]{1,0:T(8,128)(2,1)S(1)}, bf16[256,768]{1,0:T(8,128)(2,1)S(1)}, f32[1,1024]{1,0:T(1,128)S(1)}) custom-call(s32[2,1,2]{2,1,0:T(1,128)S(1)} %copy-done.17, s32[2,1,2]{2,1,0:T(1,128)S(1)} %bitcast.54, bf16[2,256,1024]{2,1,0:T(8,128)(2,1)S(1)} %bitcast.37, ...), custom_call_target="tpu_custom_call" | custom-call | flops 1 | bytes 1 | tf_op jit(solution)/shard_map/first_pass/pallas_call | solution.py:150
  19.9 0.0 copy-start.6
  19.9 0.0 copy-start.7
  20.0 0.0 copy-start.15
  20.0 4.4 %collective-permute-start.3 = (bf16[256,1024]{1,0:T(8,128)(2,1)S(1)}, bf16[256,1024]{1,0:T(8,128)(2,1)S(1)}, u32[]{:S(2)}, u32[]{:S(2)}) collective-permute-start(bf16[256,1024]{1,0:T(8,128)(2,1)S(1)} %get-tuple-element.57.refs_11_), channel_id=1, source_target_pairs={{2,0},{4,2},{6,4},{8,6},{10,8},{12,10},{14,12},{16,14},{18,16},{20... | collective-permute-start | bytes 1572872 | tf_op jit(solution)/shard_map/ppermute | solution.py:566
  24.3 0.0 copy-done.1
  24.4 0.0 copy-done.2
  24.4 0.0 copy-done.18
  24.4 3.5 %forward_pass.2 = (bf16[256,1024]{1,0:T(8,128)(2,1)S(1)}, bf16[256,768]{1,0:T(8,128)(2,1)S(1)}, bf16[256,512]{1,0:T(8,128)(2,1)S(1)}, bf16[4,256,512]{2,1,0:T(8,128)(2,1)S(1)}) custom-call(s32[2,1,2]{2,1,0:T(1,128)S(1)} %copy-done.17, s32[2,1,2]{2,1,0:T(1,128)S(1)} %bitcast.55, bf16[2,256,1024]{2,1,0:T(8,128)(2,1)S(1)} %bitcast.35, ...), custom_call_target="tpu_custom_call" | custom-call | flops 1 | bytes 1 | tf_op jit(solution)/shard_map/forward_pass/pallas_call | solution.py:150
  27.9 0.0 collective-permute-done.refs_4_.refs_10_
  27.9 0.0 copy-start.4
  27.9 0.0 copy-start.13
  27.9 1.1 %outproj_pass.1 = (bf16[1,128,1024]{2,1,0:T(8,128)(2,1)S(1)}, bf16[1,128,1024]{2,1,0:T(8,128)(2,1)S(1)}, bf16[256,1024]{1,0:T(8,128)(2,1)S(1)}) custom-call(bf16[256,1024]{1,0:T(8,128)(2,1)S(1)} %bitcast.45, bf16[256,1024]{1,0:T(8,128)(2,1)S(1)} %copy-done.7, bf16[256,512]{1,0:T(8,128)(2,1)S(1)} %copy-done.15, ...), custom_call_target="tpu_custom_call" | custom-call | flops 1 | bytes 1 | tf_op jit(solution)/shard_map/outproj_pass/pallas_call | solution.py:150
  29.1 0.1 collective-permute-start.1
  29.1 0.5 collective-permute-start.2
  29.6 1.0 %collective-permute-done.1 = bf16[128,1024]{1,0:T(8,128)(2,1)S(1)} collective-permute-done((bf16[128,1024]{1,0:T(8,128)(2,1)S(1)}, bf16[128,1024]{1,0:T(8,128)(2,1)S(1)}, u32[]{:S(2)}, u32[]{:S(2)}) %collective-permute-start.1) | collective-permute-done | bytes 262176 | tf_op jit(solution)/shard_map/ppermute | solution.py:577
  30.7 0.4 collective-permute-done.2
  31.0 0.1 sum_pass.2.refs_12_
  31.2 0.6 collective-permute-start.7
  31.8 0.0 copy-start.14
  31.8 4.8 %backward_pass.2 = (bf16[256,1024]{1,0:T(8,128)(2,1)}, bf16[256,768]{1,0:T(8,128)(2,1)S(1)}, f32[1,1024]{1,0:T(1,128)S(1)}, bf16[2,2,256,1024]{3,2,1,0:T(8,128)(2,1)}) custom-call(s32[2,1,2]{2,1,0:T(1,128)S(1)} %copy-done.17, bf16[2,256,1024]{2,1,0:T(8,128)(2,1)S(1)} %bitcast.36, bf16[1024,768]{1,0:T(8,128)(2,1)S(1)} %bitcast.33, ...), custom_call_target="tpu_custom_call" | custom-call | flops 1 | bytes 1 | tf_op jit(solution)/shard_map/backward_pass/pallas_call | solution.py:150
  36.7 1.7 %collective-permute-done.3.refs_5_.refs_10_ = bf16[256,1024]{1,0:T(8,128)(2,1)S(1)} collective-permute-done((bf16[256,1024]{1,0:T(8,128)(2,1)S(1)}, bf16[256,1024]{1,0:T(8,128)(2,1)S(1)}, u32[]{:S(2)}, u32[]{:S(2)}) %collective-permute-start.3) | collective-permute-done | bytes 524320 | tf_op jit(solution)/shard_map/ppermute | solution.py:566
  38.4 1.3 %qkv_pass.1 = (bf16[1,176,768]{2,1,0:T(8,128)(2,1)S(1)}, bf16[1,176,768]{2,1,0:T(8,128)(2,1)S(1)}, bf16[1,176,768]{2,1,0:T(8,128)(2,1)S(1)}, bf16[528,768]{1,0:T(8,128)(2,1)S(1)}) custom-call(bf16[256,1024]{1,0:T(8,128)(2,1)S(1)} %copy-done.14, bf16[256,768]{1,0:T(8,128)(2,1)S(1)} %copy-done.11, bf16[256,1024]{1,0:T(8,128)(2,1)S(1)} %get-tuple-element.45.refs_2_, ...), custom_call_target="tpu_custom_call" | custom-call | flops 1 | bytes 1 | tf_op jit(solution)/shard_map/qkv_pass/pallas_call | solution.py:150
  39.7 0.1 collective-permute-start.4
  39.8 0.5 collective-permute-start.5
  40.3 0.1 collective-permute-start.6
  40.3 1.0 collective-permute-done.4
  41.3 0.4 collective-permute-done.5
  41.7 0.4 collective-permute-done.6
  42.1 33.6 %collective-permute-done.7.refs_4_.refs_1_ = bf16[256,1024]{1,0:T(8,128)(2,1)S(1)} collective-permute-done((bf16[256,1024]{1,0:T(8,128)(2,1)S(1)}, bf16[256,1024]{1,0:T(8,128)(2,1)S(1)}, u32[]{:S(2)}, u32[]{:S(2)}) %collective-permute-start.7) | collective-permute-done | bytes 524320 | tf_op jit(solution)/shard_map/ppermute | solution.py:571
  75.7 0.2 sum_pass.3.refs_13_
  75.8 0.0 copy-start.12
  75.9 3.8 %collective-permute-start.8 = (bf16[528,768]{1,0:T(8,128)(2,1)S(1)}, bf16[528,768]{1,0:T(8,128)(2,1)S(1)}, u32[]{:S(2)}, u32[]{:S(2)}) collective-permute-start(bf16[528,768]{1,0:T(8,128)(2,1)S(1)} %sum_pass.3.refs_13_), channel_id=1, source_target_pairs={{0,30},{2,28},{4,26},{6,24},{8,22},{10,20},{12,18},{14,16},{16,14}... | collective-permute-start | bytes 2433032 | tf_op jit(solution)/shard_map/ppermute | solution.py:571
  79.6 3.5 %forward_pass.3 = (bf16[256,1024]{1,0:T(8,128)(2,1)S(1)}, bf16[256,768]{1,0:T(8,128)(2,1)S(1)}, bf16[256,512]{1,0:T(8,128)(2,1)S(1)}, bf16[4,256,512]{2,1,0:T(8,128)(2,1)S(1)}) custom-call(s32[2,1,2]{2,1,0:T(1,128)S(1)} %copy-done.17, s32[2,1,2]{2,1,0:T(1,128)S(1)} %bitcast.56, bf16[2,256,1024]{2,1,0:T(8,128)(2,1)S(1)} %bitcast.38, ...), custom_call_target="tpu_custom_call" | custom-call | flops 1 | bytes 1 | tf_op jit(solution)/shard_map/forward_pass/pallas_call | solution.py:150
  83.1 0.0 copy-start.9
  83.1 4.3 %backward_pass.3 = (bf16[256,1024]{1,0:T(8,128)(2,1)S(1)}, bf16[256,768]{1,0:T(8,128)(2,1)S(1)}, f32[1,1024]{1,0:T(1,128)S(1)}, bf16[2,2,256,1024]{3,2,1,0:T(8,128)(2,1)}) custom-call(s32[2,1,2]{2,1,0:T(1,128)S(1)} %copy-done.17, bf16[2,256,1024]{2,1,0:T(8,128)(2,1)S(1)} %bitcast.39, ...), custom_call_target="tpu_custom_call", output_to_operand_aliasing={{3}: (12, {})} | custom-call | flops 1 | bytes 1 | tf_op jit(solution)/shard_map/backward_pass/pallas_call | solution.py:150
  87.4 2.0 %packed_pass.1 = (bf16[1,1296,256]{2,1,0:T(8,128)(2,1)S(1)}, bf16[1,1296,256]{2,1,0:T(8,128)(2,1)S(1)}, bf16[2592,256]{1,0:T(8,128)(2,1)S(1)}) custom-call(bf16[256,1024]{1,0:T(8,128)(2,1)S(1)} %get-tuple-element.68.refs_0_, bf16[256,768]{1,0:T(8,128)(2,1)S(1)} %get-tuple-element.44.refs_5_.refs_1_, bf16[256,512]{1,0:T(8,128)(2,1)S(1)} %get-tuple-element.69.refs_2_, ...), custom_call_target="tpu_custom_call" | custom-call | flops 1 | bytes 1 | tf_op jit(solution)/shard_map/packed_pass/pallas_call | solution.py:150
  89.4 0.1 collective-permute-start.10
  89.5 0.5 collective-permute-start.9
  90.0 1.6 %collective-permute-done.10.refs_4_ = bf16[1296,256]{1,0:T(8,128)(2,1)S(1)} collective-permute-done((bf16[1296,256]{1,0:T(8,128)(2,1)S(1)}, bf16[1296,256]{1,0:T(8,128)(2,1)S(1)}, u32[]{:S(2)}, u32[]{:S(2)}) %collective-permute-start.10) | collective-permute-done | bytes 663584 | tf_op jit(solution)/shard_map/ppermute | solution.py:577
  91.6 0.9 collective-permute-done.9.refs_3_
  92.6 4.4 %collective-permute-done.8.refs_2_ = bf16[528,768]{1,0:T(8,128)(2,1)S(1)} collective-permute-done((bf16[528,768]{1,0:T(8,128)(2,1)S(1)}, bf16[528,768]{1,0:T(8,128)(2,1)S(1)}, u32[]{:S(2)}, u32[]{:S(2)}) %collective-permute-start.8) | collective-permute-done | bytes 811040 | tf_op jit(solution)/shard_map/ppermute | solution.py:571
  97.0 1.8 %final_pass.1 = (f32[1,512]{1,0:T(1,128)}, f32[512,768]{1,0:T(8,128)}, f32[256,1024]{1,0:T(8,128)}) custom-call(bf16[2592,256]{1,0:T(8,128)(2,1)S(1)} %get-tuple-element.74.refs_0_, bf16[256,1024]{1,0:T(8,128)(2,1)S(1)} %collective-permute-done.7.refs_4_.refs_1_, bf16[528,768]{1,0:T(8,128)(2,1)S(1)} %collective-permute-done.8.refs_2_, ...), custom_call_target="tpu_custom_call" | custom-call | flops 1 | bytes 1 | tf_op jit(solution)/shard_map/final_pass/pallas_call | solution.py:150
  (28 shorter events, 0.1 us)
Async XLA Ops:
  0.6 11.3 %copy-start = (bf16[1,1024,768]{2,1,0:T(8,128)(2,1)S(1)}, bf16[1,1024,768]{2,1,0:T(8,128)(2,1)}, u32[]{:S(2)}) copy-start(bf16[1,1024,768]{2,1,0:T(8,128)(2,1)} %param.21) | copy-start | bytes 4718596
  0.6 11.3 %copy-start.3 = (bf16[1,2,256,1024]{3,2,1,0:T(8,128)(2,1)S(1)}, bf16[1,2,256,1024]{3,2,1,0:T(8,128)(2,1)}, u32[]{:S(2)}) copy-start(bf16[1,2,256,1024]{3,2,1,0:T(8,128)(2,1)} %param.14) | copy-start | bytes 3145732
  0.7 11.3 %copy-start.5 = (bf16[1,512,1024]{2,1,0:T(8,128)(2,1)S(1)}, bf16[1,512,1024]{2,1,0:T(8,128)(2,1)}, u32[]{:S(2)}) copy-start(bf16[1,512,1024]{2,1,0:T(8,128)(2,1)} %param.22) | copy-start | bytes 3145732
  0.7 11.3 %copy-start.16 = (f32[1,1024]{1,0:T(1,128)S(1)}, f32[1,1024]{1,0:T(1,128)}, u32[]{:S(2)}) copy-start(f32[1,1024]{1,0:T(1,128)} %refs_4_.7) | copy-start | bytes 12292
  0.7 11.3 %copy-start.17 = (s32[2,1,2]{2,1,0:T(1,128)S(1)}, s32[2,1,2]{2,1,0:T(1,128)}, u32[]{:S(2)}) copy-start(s32[2,1,2]{2,1,0:T(1,128)} %refs_0_.11) | copy-start | bytes 52
  0.7 11.3 %copy-start.19 = (s32[2,1,2,1]{2,3,1,0:T(1,128)S(1)}, s32[2,1,2,1]{2,3,1,0:T(1,128)}, u32[]{:S(2)}) copy-start(s32[2,1,2,1]{2,3,1,0:T(1,128)} %param.26) | copy-start | bytes 52
  8.5 19.4 %collective-permute-start = (bf16[256,1024]{1,0:T(8,128)(2,1)}, bf16[256,1024]{1,0:T(8,128)(2,1)S(1)}, u32[]{:S(2)}, u32[]{:S(2)}) collective-permute-start(bf16[256,1024]{1,0:T(8,128)(2,1)} %get-tuple-element.50.refs_11_), channel_id=1, source_target_pairs={{0,2},{2,4},{4,6},{6,8},{8,10},{10,12},{12,14},{14,16},{16,18},{18... | collective-permute-start | bytes 1572872 | tf_op jit(solution)/shard_map/ppermute | solution.py:566
  12.0 1.0 %copy-start.8 = (bf16[1,256,1024]{2,1,0:T(8,128)(2,1)S(1)}, bf16[1,256,1024]{2,1,0:T(8,128)(2,1)}, u32[]{:S(2)}) copy-start(bf16[1,256,1024]{2,1,0:T(8,128)(2,1)} %param.16) | copy-start | bytes 1572868
  13.0 1.0 %copy-start.10 = (bf16[256,768]{1,0:T(8,128)(2,1)S(1)}, bf16[256,768]{1,0:T(8,128)(2,1)}, u32[]{:S(2)}) copy-start(bf16[256,768]{1,0:T(8,128)(2,1)} %get-tuple-element.43.refs_7_.refs_1_) | copy-start | bytes 1179652
  14.0 10.3 %copy-start.1 = (bf16[1,1024,768]{2,1,0:T(8,128)(2,1)S(1)}, bf16[1,1024,768]{2,1,0:T(8,128)(2,1)}, u32[]{:S(2)}) copy-start(bf16[1,1024,768]{2,1,0:T(8,128)(2,1)} %param.24) | copy-start | bytes 4718596
  14.0 10.4 %copy-start.2 = (bf16[1,2,256,1024]{3,2,1,0:T(8,128)(2,1)S(1)}, bf16[1,2,256,1024]{3,2,1,0:T(8,128)(2,1)}, u32[]{:S(2)}) copy-start(bf16[1,2,256,1024]{3,2,1,0:T(8,128)(2,1)} %param.15) | copy-start | bytes 3145732
  14.0 10.4 %copy-start.18 = (f32[1,1024]{1,0:T(1,128)S(1)}, f32[1,1024]{1,0:T(1,128)}, u32[]{:S(2)}) copy-start(f32[1,1024]{1,0:T(1,128)} %refs_4_.5) | copy-start | bytes 12292
  19.9 8.0 %copy-start.6 = (bf16[1,256,1024]{2,1,0:T(8,128)(2,1)S(1)}, bf16[1,256,1024]{2,1,0:T(8,128)(2,1)}, u32[]{:S(2)}) copy-start(bf16[1,256,1024]{2,1,0:T(8,128)(2,1)} %param.17) | copy-start | bytes 1572868
  19.9 8.0 %copy-start.7 = (bf16[256,1024]{1,0:T(8,128)(2,1)S(1)}, bf16[256,1024]{1,0:T(8,128)(2,1)}, u32[]{:S(2)}) copy-start(bf16[256,1024]{1,0:T(8,128)(2,1)} %refs_5_.2) | copy-start | bytes 1572868
  20.0 7.9 %copy-start.15 = (bf16[256,512]{1,0:T(8,128)(2,1)S(1)}, bf16[256,512]{1,0:T(8,128)(2,1)}, u32[]{:S(2)}) copy-start(bf16[256,512]{1,0:T(8,128)(2,1)} %get-tuple-element.51.refs_2_) | copy-start | bytes 786436
  20.0 18.5 %collective-permute-start.3 = (bf16[256,1024]{1,0:T(8,128)(2,1)S(1)}, bf16[256,1024]{1,0:T(8,128)(2,1)S(1)}, u32[]{:S(2)}, u32[]{:S(2)}) collective-permute-start(bf16[256,1024]{1,0:T(8,128)(2,1)S(1)} %get-tuple-element.57.refs_11_), channel_id=1, source_target_pairs={{2,0},{4,2},{6,4},{8,6},{10,8},{12,10},{14,12},{16,14},{18,16},{20... | collective-permute-start | bytes 1572872 | tf_op jit(solution)/shard_map/ppermute | solution.py:566
  27.9 3.9 %copy-start.4 = (bf16[1,512,1024]{2,1,0:T(8,128)(2,1)S(1)}, bf16[1,512,1024]{2,1,0:T(8,128)(2,1)}, u32[]{:S(2)}) copy-start(bf16[1,512,1024]{2,1,0:T(8,128)(2,1)} %param.25) | copy-start | bytes 3145732
  27.9 3.9 %copy-start.13 = (bf16[256,1024]{1,0:T(8,128)(2,1)S(1)}, bf16[256,1024]{1,0:T(8,128)(2,1)}, u32[]{:S(2)}) copy-start(bf16[256,1024]{1,0:T(8,128)(2,1)} %get-tuple-element.50.refs_11_) | copy-start | bytes 1572868
  27.9 3.9 %copy-start.20 = (f32[1,1024]{1,0:T(1,128)S(1)}, f32[1,1024]{1,0:T(1,128)}, u32[]{:S(2)}) copy-start(f32[1,1024]{1,0:T(1,128)} %get-tuple-element.49.refs_9_) | copy-start | bytes 12292
  29.1 1.6 %collective-permute-start.1 = (bf16[128,1024]{1,0:T(8,128)(2,1)S(1)}, bf16[128,1024]{1,0:T(8,128)(2,1)S(1)}, u32[]{:S(2)}, u32[]{:S(2)}) collective-permute-start(bf16[128,1024]{1,0:T(8,128)(2,1)S(1)} %bitcast.63), channel_id=1, source_target_pairs={{0,1},{1,0},{2,3},{3,2},{4,5},{5,4},{6,7},{7,6},{8,9},{9,8},{10,11... | collective-permute-start | bytes 786440 | tf_op jit(solution)/shard_map/ppermute | solution.py:577
  29.1 1.9 %collective-permute-start.2 = (bf16[128,1024]{1,0:T(8,128)(2,1)S(1)}, bf16[128,1024]{1,0:T(8,128)(2,1)S(1)}, u32[]{:S(2)}, u32[]{:S(2)}) collective-permute-start(bf16[128,1024]{1,0:T(8,128)(2,1)S(1)} %bitcast.62), channel_id=1, source_target_pairs={{0,1},{1,0},{2,3},{3,2},{4,5},{5,4},{6,7},{7,6},{8,9},{9,8},{10,11... | collective-permute-start | bytes 786440 | tf_op jit(solution)/shard_map/ppermute | solution.py:577
  31.2 44.5 %collective-permute-start.7 = (bf16[256,1024]{1,0:T(8,128)(2,1)S(1)}, bf16[256,1024]{1,0:T(8,128)(2,1)S(1)}, u32[]{:S(2)}, u32[]{:S(2)}) collective-permute-start(bf16[256,1024]{1,0:T(8,128)(2,1)S(1)} %sum_pass.2.refs_12_), channel_id=1, source_target_pairs={{0,30},{2,28},{4,26},{6,24},{8,22},{10,20},{12,18},{14,16},{16,14}... | collective-permute-start | bytes 1572872 | tf_op jit(solution)/shard_map/ppermute | solution.py:571
  31.8 6.6 %copy-start.11 = (bf16[256,768]{1,0:T(8,128)(2,1)S(1)}, bf16[256,768]{1,0:T(8,128)(2,1)}, u32[]{:S(2)}) copy-start(bf16[256,768]{1,0:T(8,128)(2,1)} %get-tuple-element.43.refs_7_.refs_1_) | copy-start | bytes 1179652
  31.8 6.6 %copy-start.14 = (bf16[256,1024]{1,0:T(8,128)(2,1)S(1)}, bf16[256,1024]{1,0:T(8,128)(2,1)}, u32[]{:S(2)}) copy-start(bf16[256,1024]{1,0:T(8,128)(2,1)} %get-tuple-element.42.refs_0_) | copy-start | bytes 1572868
  39.7 1.6 %collective-permute-start.4 = (bf16[176,768]{1,0:T(8,128)(2,1)S(1)}, bf16[176,768]{1,0:T(8,128)(2,1)S(1)}, u32[]{:S(2)}, u32[]{:S(2)}) collective-permute-start(bf16[176,768]{1,0:T(8,128)(2,1)S(1)} %bitcast.61), channel_id=1, source_target_pairs={{0,1},{1,0},{2,3},{3,2},{4,5},{5,4},{6,7},{7,6},{8,9},{9,8},{10,11... | collective-permute-start | bytes 811016 | tf_op jit(solution)/shard_map/ppermute | solution.py:577
  39.8 1.9 %collective-permute-start.5 = (bf16[176,768]{1,0:T(8,128)(2,1)S(1)}, bf16[176,768]{1,0:T(8,128)(2,1)S(1)}, u32[]{:S(2)}, u32[]{:S(2)}) collective-permute-start(bf16[176,768]{1,0:T(8,128)(2,1)S(1)} %bitcast.60), channel_id=1, source_target_pairs={{0,1},{1,0},{2,3},{3,2},{4,5},{5,4},{6,7},{7,6},{8,9},{9,8},{10,11... | collective-permute-start | bytes 811016 | tf_op jit(solution)/shard_map/ppermute | solution.py:577
  40.3 1.8 %collective-permute-start.6 = (bf16[176,768]{1,0:T(8,128)(2,1)S(1)}, bf16[176,768]{1,0:T(8,128)(2,1)S(1)}, u32[]{:S(2)}, u32[]{:S(2)}) collective-permute-start(bf16[176,768]{1,0:T(8,128)(2,1)S(1)} %bitcast.59), channel_id=1, source_target_pairs={{0,1},{1,0},{2,3},{3,2},{4,5},{5,4},{6,7},{7,6},{8,9},{9,8},{10,11... | collective-permute-start | bytes 811016 | tf_op jit(solution)/shard_map/ppermute | solution.py:577
  75.8 7.3 %copy-start.12 = (bf16[256,1024]{1,0:T(8,128)(2,1)S(1)}, bf16[256,1024]{1,0:T(8,128)(2,1)}, u32[]{:S(2)}) copy-start(bf16[256,1024]{1,0:T(8,128)(2,1)} %refs_5_.3) | copy-start | bytes 1572868
  75.9 21.1 %collective-permute-start.8 = (bf16[528,768]{1,0:T(8,128)(2,1)S(1)}, bf16[528,768]{1,0:T(8,128)(2,1)S(1)}, u32[]{:S(2)}, u32[]{:S(2)}) collective-permute-start(bf16[528,768]{1,0:T(8,128)(2,1)S(1)} %sum_pass.3.refs_13_), channel_id=1, source_target_pairs={{0,30},{2,28},{4,26},{6,24},{8,22},{10,20},{12,18},{14,16},{16,14}... | collective-permute-start | bytes 2433032 | tf_op jit(solution)/shard_map/ppermute | solution.py:571
  83.1 4.3 %copy-start.9 = (bf16[1,256,1024]{2,1,0:T(8,128)(2,1)S(1)}, bf16[1,256,1024]{2,1,0:T(8,128)(2,1)}, u32[]{:S(2)}) copy-start(bf16[1,256,1024]{2,1,0:T(8,128)(2,1)} %param.16) | copy-start | bytes 1572868
  89.4 2.2 %collective-permute-start.10 = (bf16[1296,256]{1,0:T(8,128)(2,1)S(1)}, bf16[1296,256]{1,0:T(8,128)(2,1)S(1)}, u32[]{:S(2)}, u32[]{:S(2)}) collective-permute-start(bf16[1296,256]{1,0:T(8,128)(2,1)S(1)} %bitcast.58), channel_id=1, source_target_pairs={{0,1},{1,0},{2,3},{3,2},{4,5},{5,4},{6,7},{7,6},{8,9},{9,8},{10,11... | collective-permute-start | bytes 1990664 | tf_op jit(solution)/shard_map/ppermute | solution.py:577
  89.5 3.0 %collective-permute-start.9 = (bf16[1296,256]{1,0:T(8,128)(2,1)S(1)}, bf16[1296,256]{1,0:T(8,128)(2,1)S(1)}, u32[]{:S(2)}, u32[]{:S(2)}) collective-permute-start(bf16[1296,256]{1,0:T(8,128)(2,1)S(1)} %bitcast.57), channel_id=1, source_target_pairs={{0,1},{1,0},{2,3},{3,2},{4,5},{5,4},{6,7},{7,6},{8,9},{9,8},{10,11... | collective-permute-start | bytes 1990664 | tf_op jit(solution)/shard_map/ppermute | solution.py:577

commit v3 on v2

--- a/solution.py
+++ b/solution.py
@@ -57,6 +57,16 @@
     return inverse, scaled, (scaled * gain).astype(BF16)
 
 
+def softmax(scores):
+    e = jnp.exp(scores - jnp.max(scores, axis=1, keepdims=True))
+    return (e * (1.0 / jnp.sum(e, axis=1, keepdims=True))).astype(BF16)
+
+
+def pair_columns(array, query_width):
+    wide = 2 * (query_width // HEADS)
+    return [array[:, p * wide : (p + 1) * wide] for p in range(HEADS // 2)]
+
+
 def forward_heads(project, offset, query_width, soft_ref):
     seq = project.shape[0]
     half = query_width // HEADS
@@ -64,20 +74,16 @@
     keys = doubled(project[:, query_width : query_width + wide], half)
     values = doubled(project[:, query_width + wide :], half)
     bias = mask_bias(seq, offset)
-    scale = half ** (-0.5)
+    scale = jnp.asarray(half ** (-0.5), BF16)
     pairs = HEADS // 2
-    attended = []
+    group = [p * KV_HEADS // pairs for p in range(pairs)]
+    queries = pair_columns(project, query_width)
+    scores = [dot(queries[p] * scale, keys[group[p]], NT) for p in range(pairs)]
     for p in range(pairs):
-        g = p * KV_HEADS // pairs
-        queries = project[:, p * wide : (p + 1) * wide] * jnp.asarray(scale, BF16)
-        scores = dot(queries, keys[g], NT)
         for t in range(2):
-            s = scores[:, t * seq : (t + 1) * seq] + bias
-            e = jnp.exp(s - jnp.max(s, axis=1, keepdims=True))
-            soft = e * (1.0 / jnp.sum(e, axis=1, keepdims=True))
-            soft_ref[p, :, t * seq : (t + 1) * seq] = soft.astype(BF16)
-        attended.append(dot(soft_ref[p], values[g]))
-    return attended
+            at = slice(t * seq, (t + 1) * seq)
+            soft_ref[p, :, at] = softmax(scores[p][:, at] + bias)
+    return [dot(soft_ref[p], values[group[p]]) for p in range(pairs)]
 
 
 def backward_heads(project, attended, grad_attended, query_width, soft_ref):
@@ -88,42 +94,40 @@
     values = doubled(project[:, query_width + wide :], half)
     scale = half ** (-0.5)
     pairs = HEADS // 2
+    group = [p * KV_HEADS // pairs for p in range(pairs)]
     left = lax.broadcasted_iota(jnp.int32, (seq, wide), 1) < half
-    grad_queries = []
-    grad_keys = [None] * KV_HEADS
-    grad_values = [None] * KV_HEADS
+    queries = [q * jnp.asarray(scale, BF16) for q in pair_columns(project, query_width)]
+    grads = pair_columns(grad_attended, query_width)
+    grad_soft = [dot(grads[p], values[group[p]], NT) for p in range(pairs)]
+    values_parts = [dot(grads[p], soft_ref[p], TN) for p in range(pairs)]
+    grad_scores = []
     for p in range(pairs):
-        g = p * KV_HEADS // pairs
-        queries = project[:, p * wide : (p + 1) * wide] * jnp.asarray(scale, BF16)
-        grad_pair = grad_attended[:, p * wide : (p + 1) * wide]
-        grad_soft = dot(grad_pair, values[g], NT)
-        both = attended[p].astype(F32) * grad_pair.astype(F32)
+        both = attended[p].astype(F32) * grads[p].astype(F32)
         rows = [
             jnp.sum(jnp.where(left, both, 0.0), axis=1, keepdims=True),
             jnp.sum(jnp.where(left, 0.0, both), axis=1, keepdims=True),
         ]
-        soft = soft_ref[p]
-        grad_scores = jnp.concatenate(
-            [
-                (
-                    soft[:, t * seq : (t + 1) * seq].astype(F32)
-                    * (grad_soft[:, t * seq : (t + 1) * seq] - rows[t])
-                ).astype(BF16)
-                for t in range(2)
-            ],
-            axis=1,
+        columns = [slice(t * seq, (t + 1) * seq) for t in range(2)]
+        grad_scores.append(
+            jnp.concatenate(
+                [
+                    (soft_ref[p, :, at].astype(F32) * (grad_soft[p][:, at] - row)).astype(BF16)
+                    for at, row in zip(columns, rows)
+                ],
+                axis=1,
+            )
         )
-        grad_queries.append(dot(grad_scores, keys[g]) * scale)
-        keys_part = dot(queries, grad_scores, TN)
-        values_part = dot(grad_pair, soft, TN)
-        keys_sum = keys_part[:half, :seq] + keys_part[half:, seq:]
-        values_sum = values_part[:half, :seq] + values_part[half:, seq:]
-        grad_keys[g] = keys_sum if grad_keys[g] is None else grad_keys[g] + keys_sum
-        grad_values[g] = values_sum if grad_values[g] is None else grad_values[g] + values_sum
-    columns = grad_queries + [
-        jnp.concatenate(grad_keys, axis=0).T,
-        jnp.concatenate(grad_values, axis=0).T,
-    ]
+    grad_queries = [dot(grad_scores[p], keys[group[p]]) * scale for p in range(pairs)]
+    keys_parts = [dot(queries[p], grad_scores[p], TN) for p in range(pairs)]
+
+    def joined(parts):
+        sums = []
+        for g in range(KV_HEADS):
+            part = sum(parts[p] for p in range(pairs) if group[p] == g)
+            sums.append(part[:half, :seq] + part[half:, seq:])
+        return jnp.concatenate(sums, axis=0).T
+
+    columns = [*grad_queries, joined(keys_parts), joined(values_parts)]
     return jnp.concatenate([c.astype(BF16) for c in columns], axis=1)
 
 
@@ -170,14 +174,16 @@
 def first_kernel(order, offsets, act, qkv_hbm, out_hbm, up_hbm, gain_hbm, *refs, direction):
     grad_ref, normed_ref, attended_ref, project_ref, gain_out = refs[:5]
     order_ref, offsets_ref, x_ref, qkv_ref, out_ref, up_ref, gain_ref, soft_ref, sems = refs[5:]
-    copies = start_all(
-        (order, offsets, act, gain_hbm, qkv_hbm, up_hbm, out_hbm),
-        (order_ref, offsets_ref, x_ref, gain_ref, qkv_ref, up_ref, out_ref),
-        sems,
-    )
+    sources = (order, offsets, gain_hbm, act, qkv_hbm, up_hbm, out_hbm)
+    targets = (order_ref, offsets_ref, gain_ref, x_ref, qkv_ref, up_ref, out_ref)
+    copies = [pltpu.make_async_copy(a, b, sems.at[i]) for i, (a, b) in enumerate(zip(sources, targets))]
+    for copy in copies[:5]:
+        copy.start()
     query_width = out_hbm.shape[0]
     for copy in copies[:4]:
         copy.wait()
+    for copy in copies[5:]:
+        copy.start()
     which = order_ref[direction, 0, 0]
     offset = offsets_ref[direction, 0, which]
     gain = gain_ref[...]
@@ -486,7 +492,7 @@
     return sends, keep
 
 
-def final_kernel(keep, mirror_out, mirror_qkv, *refs, parts, pieces):
+def final_kernel(keep, outer_out, inner_out, mirror_qkv, *refs, parts, pieces):
     moved, refs = refs[: (parts - 1) * pieces], refs[(parts - 1) * pieces :]
     gain_hbm, qkv_hbm, out_hbm, gain_ref, qkv_ref, out_ref, sems = refs
     model, width = out_ref.shape[1], qkv_ref.shape[1]
@@ -512,7 +518,7 @@
     copies[0].start()
     for c in range(model // unit):
         columns = slice(c * unit, (c + 1) * unit)
-        out_ref[:, columns] = total(c * out_rows, out_rows) + mirror_out[:, columns].astype(F32)
+        out_ref[:, columns] = total(c * out_rows, out_rows) + (outer_out[:, columns] + inner_out[:, columns]).astype(F32)
     copies.append(pltpu.make_async_copy(out_ref, out_hbm, sems.at[1]))
     copies[1].start()
     lines = total(gain_at, PACKED_PAD)
@@ -526,13 +532,13 @@
         copy.wait()
 
 
-def final_pass(keep, mirror_out, mirror_qkv, moved, parts, query_width, model, width):
+def final_pass(keep, outer_out, inner_out, mirror_qkv, moved, parts, query_width, model, width):
     hbm, vmem = pltpu.HBM, pltpu.VMEM
     shapes = ((1, model // parts), (model // parts, width), (query_width // parts, model))
     return call(
         functools.partial(final_kernel, parts=parts, pieces=len(moved[0])),
         "final_pass",
-        [(keep, vmem), (mirror_out, vmem), (mirror_qkv, vmem)] + [(m, vmem) for per in moved for m in per],
+        [(keep, vmem), (outer_out, vmem), (inner_out, vmem), (mirror_qkv, vmem)] + [(m, vmem) for per in moved for m in per],
         [(shape, F32, hbm) for shape in shapes],
         [pltpu.VMEM(shape, F32) for shape in shapes] + [pltpu.SemaphoreType.DMA((3,))],
     )
@@ -566,9 +572,9 @@
     return lax.ppermute(value, axis, [(source, source + steps) for source in range(first, last)])
 
 
-def mirrored(value, axis):
+def mirrored(value, axis, sections=None):
     count = lax.axis_size(axis)
-    return lax.ppermute(value, axis, [(i, count - 1 - i) for i in range(count)])
+    return lax.ppermute(value, axis, [(i, count - 1 - i) for i in (range(count) if sections is None else sections)])
 
 
 def exchanged(sends, axis):
@@ -590,31 +596,37 @@
     down = (gain_down, qkv_down[0], outproj_down[0])
     up = (gain_up, qkv_up[0], outproj_up[0])
 
+    sections = lax.axis_size("section")
+    edge = sections // 4
+    outer = [*range(edge), *range(sections - edge, sections)]
+    inner = range(edge, sections - edge)
+
     up_one = first_pass(1, ints, act_up[0], *up, grad_up[0], limit=FIRST_LIMIT)
     up_moved = shifted(up_one[0], "section", 1)
-    down_one = first_pass(0, ints, act_down[0], *down, grad_down[0], after=(up_one[3],))
+    down_one = first_pass(0, ints, act_down[0], *down, grad_down[0], limit=60 * 1024 * 1024, after=(up_one[4],))
     down_moved = shifted(down_one[0], "section", -1)
     up_forward = forward_pass(1, ints, act_up[0], gain_up, qkv_up[0], query_width, after=(down_one[3],))
     sends, keep = outproj_pass(1, up_one[2], up_forward[2], grad_up[0], up_moved, seed_up, parts)
     up_out = sum_pass(keep, exchanged(sends, "dp"))
-    mirror_out = mirrored(up_out, "section")
+    outer_out = mirrored(up_out, "section", outer)
+    inner_out = mirrored(up_out, "section", inner)
     up_two = backward_pass(
         1, slot_order, act_up[0], *up, seed_up, up_forward, up_one[4], up_moved, up_one[0], after=(up_out,)
     )
     sends, keep = qkv_pass(up_one[1], up_one[3], up_forward[0], up_two[1], up_two[2], parts, after=(down_moved,))
-    up_qkv = sum_pass(keep, exchanged(sends, "dp"), after=(mirror_out,))
+    down_forward = forward_pass(0, ints, act_down[0], gain_down, qkv_down[0], query_width, after=(keep,))
+    up_qkv = sum_pass(keep, exchanged(sends, "dp"), after=(outer_out, down_forward[2]))
     mirror_qkv = mirrored(up_qkv, "section")
-    down_forward = forward_pass(0, ints, act_down[0], gain_down, qkv_down[0], query_width, after=(keep,))
     down_two = backward_pass(
         0, slot_order, act_down[0], *down, seed_down, down_forward, down_one[4], down_moved, down_one[0],
-        grads=up_two[3], after=(up_qkv,),
+        grads=up_two[3], after=(up_qkv, inner_out),
     )
     sends, keep = packed_pass(
         down_one[1], down_one[3], down_one[2], grad_down[0],
         down_forward[0], down_two[1], down_forward[2], down_two[0], down_two[2], parts,
     )
     grad_gain, grad_qkv, grad_outproj = final_pass(
-        keep, mirror_out, mirror_qkv, exchanged(sends, "dp"), parts, query_width, model, width
+        keep, outer_out, inner_out, mirror_qkv, exchanged(sends, "dp"), parts, query_width, model, width
     )
     return (down_two[3][:, None], grad_gain, grad_qkv[None], grad_outproj[None])
 

time: 99.9 us -> 95.2 us (0.953)
  waiting for transfers between devices: 45.4 us -> 42.6 us
  Pallas kernels: 36.3 us -> 33.7 us
  starting transfers between devices: 13.9 us -> 16.1 us
  local copies, waits for them, and re-layouts: 2.13 us -> 1.13 us
    pallas_call x12, Pallas kernels: 36.3 us -> 33.7 us  [call(): pl.pallas_call(ordered, out_shape=tuple((jax.ShapeDtypeStruct(shape, dtyp...]
    ppermute x2 -> x3, starting transfers between devices: 4.39 us -> 6.5 us  [mirrored(): lax.ppermute(value, axis, [(i, count - 1 - i) for i in (range(count) if s...]
    ppermute x2, waiting for transfers between devices: 1.74 us -> 0.01 us  [shifted(): lax.ppermute(value, axis, [(source, source + steps) for source in range(f...]
    ppermute x7, waiting for transfers between devices: 5.68 us -> 3.95 us  [exchanged(): lax.ppermute(send[k], axis, [(i, (i + 1 + k) % parts) for i in range(part...]
    unnamed x42 -> x50, local copies, waits for them, and re-layouts: 2.13 us -> 1.13 us
    ppermute x2 -> x3, waiting for transfers between devices: 38 us -> 38.7 us  [mirrored(): lax.ppermute(value, axis, [(i, count - 1 - i) for i in (range(count) if s...]
  transfers between devices with their start and end apart: 11 -> 12, of which waited for: 10 -> 6; matrix products, arithmetic and copies ran while one was open for 0% -> 0% of each run, Pallas kernels for 27% -> 27%
where the time goes in v3:
time: 95.2 us; the launch traced here: 94.9 us
  waiting for transfers between devices  42.6 us (45%)
  Pallas kernels  33.7 us (35%)
  starting transfers between devices  16.1 us (17%)
  between operations  1.32 us (1%)
  local copies, waits for them, and re-layouts  1.13 us (1%)
    ppermute x3, waiting for transfers between devices, mirrored(): lax.ppermute(value, axis, [(i, count - 1 - i) for i in (range(count) if s...  38.7 us
    pallas_call x12, Pallas kernels, call(): pl.pallas_call(ordered, out_shape=tuple((jax.ShapeDtypeStruct(shape, dtyp...  33.7 us
    ppermute x2, starting transfers between devices, shifted(): lax.ppermute(value, axis, [(source, source + steps) for source in range(f...  7.78 us
    ppermute x3, starting transfers between devices, mirrored(): lax.ppermute(value, axis, [(i, count - 1 - i) for i in (range(count) if s...  6.5 us
    ppermute x7, waiting for transfers between devices, exchanged(): lax.ppermute(send[k], axis, [(i, (i + 1 + k) % parts) for i in range(part...  3.95 us
  transfers between devices with their start and end apart: 12, of which 6 were waited for; matrix products, arithmetic and copies ran while one was open for 0% of the time, Pallas kernels for 27%

profile of v3, /device:TPU:16, one launch (start us, length us, event | category | flops | bytes accessed | tf_op | source)
XLA Modules:
  0.0 94.9 jit_solution(7648822378597005680)
XLA Ops:
  0.6 6.5 %first_pass.2 = (bf16[256,1024]{1,0:T(8,128)(2,1)}, bf16[256,1024]{1,0:T(8,128)(2,1)}, bf16[256,512]{1,0:T(8,128)(2,1)}, bf16[256,768]{1,0:T(8,128)(2,1)}, f32[1,1024]{1,0:T(1,128)}) custom-call(s32[2,1,2]{2,1,0:T(1,128)} %refs_0_.11, s32[2,1,2]{2,1,0:T(1,128)} %bitcast.53, bf16[2,256,1024]{2,1,0:T(8,128)(2,1)} %bitcast.34, bf16[1024,768]{1,0:T(8,128)(2,1)} %bitcast.28, ...), custom_call_target="tpu_custom_call" | custom-call | flops 1 | bytes 1 | tf_op jit(solution)/shard_map/first_pass/pallas_call | solution.py:154
  7.2 3.4 %collective-permute-start = (bf16[256,1024]{1,0:T(8,128)(2,1)}, bf16[256,1024]{1,0:T(8,128)(2,1)S(1)}, u32[]{:S(2)}, u32[]{:S(2)}) collective-permute-start(bf16[256,1024]{1,0:T(8,128)(2,1)} %get-tuple-element.50.refs_11_), channel_id=1, source_target_pairs={{0,2},{2,4},{4,6},{6,8},{8,10},{10,12},{12,14},{14,16},{16,18},{18... | collective-permute-start | bytes 1572872 | tf_op jit(solution)/shard_map/ppermute | solution.py:572
  10.6 0.0 copy-start
  10.6 0.0 copy-start.2
  10.6 0.0 copy-start.19
  10.6 0.0 copy-start.21
  10.6 0.0 copy-start.23
  10.6 0.0 copy-start.18
  10.7 6.7 %first_pass.3 = (bf16[256,1024]{1,0:T(8,128)(2,1)}, bf16[256,1024]{1,0:T(8,128)(2,1)}, bf16[256,512]{1,0:T(8,128)(2,1)}, bf16[256,768]{1,0:T(8,128)(2,1)}, f32[1,1024]{1,0:T(1,128)}) custom-call(s32[2,1,2]{2,1,0:T(1,128)} %refs_0_.11, s32[2,1,2]{2,1,0:T(1,128)} %bitcast.54, bf16[2,256,1024]{2,1,0:T(8,128)(2,1)} %bitcast.37, bf16[1024,768]{1,0:T(8,128)(2,1)} %bitcast.31, ...), custom_call_target="tpu_custom_call" | custom-call | flops 1 | bytes 1 | tf_op jit(solution)/shard_map/first_pass/pallas_call | solution.py:154
  17.3 0.0 copy-start.6
  17.4 0.0 copy-start.7
  17.4 4.4 %collective-permute-start.3 = (bf16[256,1024]{1,0:T(8,128)(2,1)}, bf16[256,1024]{1,0:T(8,128)(2,1)S(1)}, u32[]{:S(2)}, u32[]{:S(2)}) collective-permute-start(bf16[256,1024]{1,0:T(8,128)(2,1)} %get-tuple-element.57.refs_11_), channel_id=1, source_target_pairs={{2,0},{4,2},{6,4},{8,6},{10,8},{12,10},{14,12},{16,14},{18,16},{20... | collective-permute-start | bytes 1572872 | tf_op jit(solution)/shard_map/ppermute | solution.py:572
  21.8 1.0 %copy-done.9 = bf16[256,768]{1,0:T(8,128)(2,1)S(1)} copy-done((bf16[256,768]{1,0:T(8,128)(2,1)S(1)}, bf16[256,768]{1,0:T(8,128)(2,1)}, u32[]{:S(2)}) %copy-start.9) | copy-done | bytes 393240
  22.8 2.6 %forward_pass.2 = (bf16[256,1024]{1,0:T(8,128)(2,1)S(1)}, bf16[256,768]{1,0:T(8,128)(2,1)S(1)}, bf16[256,512]{1,0:T(8,128)(2,1)S(1)}, bf16[4,256,512]{2,1,0:T(8,128)(2,1)S(1)}) custom-call(s32[2,1,2]{2,1,0:T(1,128)S(1)} %copy-done.21, s32[2,1,2]{2,1,0:T(1,128)S(1)} %bitcast.55, bf16[2,256,1024]{2,1,0:T(8,128)(2,1)S(1)} %bitcast.35, ...), custom_call_target="tpu_custom_call" | custom-call | flops 1 | bytes 1 | tf_op jit(solution)/shard_map/forward_pass/pallas_call | solution.py:154
  25.4 0.0 copy-start.4
  25.4 0.0 copy-start.11
  25.5 0.9 outproj_pass.1
  26.4 0.1 collective-permute-start.1
  26.5 0.5 collective-permute-start.2
  27.0 1.0 %collective-permute-done.1 = bf16[128,1024]{1,0:T(8,128)(2,1)S(1)} collective-permute-done((bf16[128,1024]{1,0:T(8,128)(2,1)S(1)}, bf16[128,1024]{1,0:T(8,128)(2,1)S(1)}, u32[]{:S(2)}, u32[]{:S(2)}) %collective-permute-start.1) | collective-permute-done | bytes 262176 | tf_op jit(solution)/shard_map/ppermute | solution.py:583
  28.0 0.4 collective-permute-done.2
  28.4 0.1 sum_pass.2.refs_12_
  28.5 0.7 collective-permute-start.7
  29.2 2.9 %collective-permute-start.8 = (bf16[256,1024]{1,0:T(8,128)(2,1)S(1)}, bf16[256,1024]{1,0:T(8,128)(2,1)S(1)}, u32[]{:S(2)}, u32[]{:S(2)}) collective-permute-start(bf16[256,1024]{1,0:T(8,128)(2,1)S(1)} %sum_pass.2.refs_12_), channel_id=1, source_target_pairs={{8,22},{10,20},{12,18},{14,16},{16,14},{18,12},{20,10},{22,8},{9,2... | collective-permute-start | bytes 1572872 | tf_op jit(solution)/shard_map/ppermute | solution.py:577
  32.2 0.0 copy-start.13
  32.2 0.0 copy-start.3
  32.2 4.9 %backward_pass.2 = (bf16[256,1024]{1,0:T(8,128)(2,1)}, bf16[256,768]{1,0:T(8,128)(2,1)S(1)}, f32[1,1024]{1,0:T(1,128)S(1)}, bf16[2,2,256,1024]{3,2,1,0:T(8,128)(2,1)}) custom-call(s32[2,1,2]{2,1,0:T(1,128)S(1)} %copy-done.21, bf16[2,256,1024]{2,1,0:T(8,128)(2,1)S(1)} %bitcast.36, bf16[1024,768]{1,0:T(8,128)(2,1)S(1)} %bitcast.30, ...), custom_call_target="tpu_custom_call" | custom-call | flops 1 | bytes 1 | tf_op jit(solution)/shard_map/backward_pass/pallas_call | solution.py:154
  37.1 0.0 copy-start.1
  37.1 0.0 copy-start.20
  37.2 1.3 %qkv_pass.1 = (bf16[1,176,768]{2,1,0:T(8,128)(2,1)S(1)}, bf16[1,176,768]{2,1,0:T(8,128)(2,1)S(1)}, bf16[1,176,768]{2,1,0:T(8,128)(2,1)S(1)}, bf16[528,768]{1,0:T(8,128)(2,1)S(1)}) custom-call(bf16[256,1024]{1,0:T(8,128)(2,1)S(1)} %copy-done.13, bf16[256,768]{1,0:T(8,128)(2,1)S(1)} %copy-done.16, bf16[256,1024]{1,0:T(8,128)(2,1)S(1)} %get-tuple-element.46.refs_2_, ...), custom_call_target="tpu_custom_call" | custom-call | flops 1 | bytes 1 | tf_op jit(solution)/shard_map/qkv_pass/pallas_call | solution.py:154
  38.5 0.1 collective-permute-start.5
  38.5 0.5 collective-permute-start.4
  39.0 0.1 collective-permute-start.6
  39.1 2.6 %forward_pass.3 = (bf16[256,1024]{1,0:T(8,128)(2,1)S(1)}, bf16[256,768]{1,0:T(8,128)(2,1)S(1)}, bf16[256,512]{1,0:T(8,128)(2,1)S(1)}, bf16[4,256,512]{2,1,0:T(8,128)(2,1)S(1)}) custom-call(s32[2,1,2]{2,1,0:T(1,128)S(1)} %copy-done.21, s32[2,1,2]{2,1,0:T(1,128)S(1)} %bitcast.56, bf16[2,256,1024]{2,1,0:T(8,128)(2,1)S(1)} %bitcast.38, ...), custom_call_target="tpu_custom_call" | custom-call | flops 1 | bytes 1 | tf_op jit(solution)/shard_map/forward_pass/pallas_call | solution.py:154
  41.8 0.0 copy-start.5
  41.8 0.0 copy-start.14
  41.8 0.2 sum_pass.3.refs_13_
  42.0 2.9 %collective-permute-start.9 = (bf16[528,768]{1,0:T(8,128)(2,1)S(1)}, bf16[528,768]{1,0:T(8,128)(2,1)S(1)}, u32[]{:S(2)}, u32[]{:S(2)}) collective-permute-start(bf16[528,768]{1,0:T(8,128)(2,1)S(1)} %sum_pass.3.refs_13_), channel_id=1, source_target_pairs={{0,30},{2,28},{4,26},{6,24},{8,22},{10,20},{12,18},{14,16},{16,14}... | collective-permute-start | bytes 2433032 | tf_op jit(solution)/shard_map/ppermute | solution.py:577
  44.9 31.4 %collective-permute-done.8.refs_14_.refs_2_ = bf16[256,1024]{1,0:T(8,128)(2,1)S(1)} collective-permute-done((bf16[256,1024]{1,0:T(8,128)(2,1)S(1)}, bf16[256,1024]{1,0:T(8,128)(2,1)S(1)}, u32[]{:S(2)}, u32[]{:S(2)}) %collective-permute-start.8) | collective-permute-done | bytes 524320 | tf_op jit(solution)/shard_map/ppermute | solution.py:577
  76.4 0.0 copy-start.8
  76.4 4.0 %backward_pass.3 = (bf16[256,1024]{1,0:T(8,128)(2,1)S(1)}, bf16[256,768]{1,0:T(8,128)(2,1)S(1)}, f32[1,1024]{1,0:T(1,128)S(1)}, bf16[2,2,256,1024]{3,2,1,0:T(8,128)(2,1)}) custom-call(s32[2,1,2]{2,1,0:T(1,128)S(1)} %copy-done.21, bf16[2,256,1024]{2,1,0:T(8,128)(2,1)S(1)} %bitcast.39, ...), custom_call_target="tpu_custom_call", output_to_operand_aliasing={{3}: (12, {})} | custom-call | flops 1 | bytes 1 | tf_op jit(solution)/shard_map/backward_pass/pallas_call | solution.py:154
  80.5 2.0 %packed_pass.1 = (bf16[1,1296,256]{2,1,0:T(8,128)(2,1)S(1)}, bf16[1,1296,256]{2,1,0:T(8,128)(2,1)S(1)}, bf16[2592,256]{1,0:T(8,128)(2,1)S(1)}) custom-call(bf16[256,1024]{1,0:T(8,128)(2,1)S(1)} %copy-done.12, bf16[256,768]{1,0:T(8,128)(2,1)S(1)} %copy-done.10, bf16[256,512]{1,0:T(8,128)(2,1)S(1)} %copy-done.17, bf16[256,1024]{1,0:T(8,128)(2,1)S(1)} %bitcast.47, ...), custom_call_target="tpu_custom_call" | custom-call | flops 1 | bytes 1 | tf_op jit(solution)/shard_map/packed_pass/pallas_call | solution.py:154
  82.5 0.1 collective-permute-start.10
  82.6 0.5 collective-permute-start.11
  83.1 1.6 %collective-permute-done.10.refs_4_ = bf16[1296,256]{1,0:T(8,128)(2,1)S(1)} collective-permute-done((bf16[1296,256]{1,0:T(8,128)(2,1)S(1)}, bf16[1296,256]{1,0:T(8,128)(2,1)S(1)}, u32[]{:S(2)}, u32[]{:S(2)}) %collective-permute-start.10) | collective-permute-done | bytes 663584 | tf_op jit(solution)/shard_map/ppermute | solution.py:583
  84.7 0.9 collective-permute-done.11.refs_5_
  85.7 7.3 %collective-permute-done.9.refs_3_ = bf16[528,768]{1,0:T(8,128)(2,1)S(1)} collective-permute-done((bf16[528,768]{1,0:T(8,128)(2,1)S(1)}, bf16[528,768]{1,0:T(8,128)(2,1)S(1)}, u32[]{:S(2)}, u32[]{:S(2)}) %collective-permute-start.9) | collective-permute-done | bytes 811040 | tf_op jit(solution)/shard_map/ppermute | solution.py:577
  92.9 1.8 %final_pass.1 = (f32[1,512]{1,0:T(1,128)}, f32[512,768]{1,0:T(8,128)}, f32[256,1024]{1,0:T(8,128)}) custom-call(bf16[2592,256]{1,0:T(8,128)(2,1)S(1)} %get-tuple-element.74.refs_0_, bf16[256,1024]{1,0:T(8,128)(2,1)S(1)} %collective-permute-done.7.refs_4_.refs_1_, bf16[256,1024]{1,0:T(8,128)(2,1)S(1)} %collective-permute-done.8.refs_14_.refs_2_, ...), custom_call_target="tpu_custom_call" | custom-call | flops 1 | bytes 1 | tf_op jit(solution)/shard_map/final_pass/pallas_call | solution.py:154
  (38 shorter events, 0.1 us)
Async XLA Ops:
  7.2 18.2 %collective-permute-start = (bf16[256,1024]{1,0:T(8,128)(2,1)}, bf16[256,1024]{1,0:T(8,128)(2,1)S(1)}, u32[]{:S(2)}, u32[]{:S(2)}) collective-permute-start(bf16[256,1024]{1,0:T(8,128)(2,1)} %get-tuple-element.50.refs_11_), channel_id=1, source_target_pairs={{0,2},{2,4},{4,6},{6,8},{8,10},{10,12},{12,14},{14,16},{16,18},{18... | collective-permute-start | bytes 1572872 | tf_op jit(solution)/shard_map/ppermute | solution.py:572
  10.6 11.2 %copy-start = (bf16[1,1024,768]{2,1,0:T(8,128)(2,1)S(1)}, bf16[1,1024,768]{2,1,0:T(8,128)(2,1)}, u32[]{:S(2)}) copy-start(bf16[1,1024,768]{2,1,0:T(8,128)(2,1)} %param.24) | copy-start | bytes 4718596
  10.6 11.2 %copy-start.2 = (bf16[1,2,256,1024]{3,2,1,0:T(8,128)(2,1)S(1)}, bf16[1,2,256,1024]{3,2,1,0:T(8,128)(2,1)}, u32[]{:S(2)}) copy-start(bf16[1,2,256,1024]{3,2,1,0:T(8,128)(2,1)} %param.15) | copy-start | bytes 3145732
  10.6 11.2 %copy-start.19 = (f32[1,1024]{1,0:T(1,128)S(1)}, f32[1,1024]{1,0:T(1,128)}, u32[]{:S(2)}) copy-start(f32[1,1024]{1,0:T(1,128)} %refs_4_.5) | copy-start | bytes 12292
  10.6 11.2 %copy-start.21 = (s32[2,1,2]{2,1,0:T(1,128)S(1)}, s32[2,1,2]{2,1,0:T(1,128)}, u32[]{:S(2)}) copy-start(s32[2,1,2]{2,1,0:T(1,128)} %refs_0_.11) | copy-start | bytes 52
  10.6 11.2 %copy-start.23 = (s32[2,1,2,1]{2,3,1,0:T(1,128)S(1)}, s32[2,1,2,1]{2,3,1,0:T(1,128)}, u32[]{:S(2)}) copy-start(s32[2,1,2,1]{2,3,1,0:T(1,128)} %param.26) | copy-start | bytes 52
  10.6 14.8 %copy-start.18 = (bf16[256,512]{1,0:T(8,128)(2,1)S(1)}, bf16[256,512]{1,0:T(8,128)(2,1)}, u32[]{:S(2)}) copy-start(bf16[256,512]{1,0:T(8,128)(2,1)} %get-tuple-element.51.refs_2_) | copy-start | bytes 786436
  17.3 8.1 %copy-start.6 = (bf16[1,256,1024]{2,1,0:T(8,128)(2,1)S(1)}, bf16[1,256,1024]{2,1,0:T(8,128)(2,1)}, u32[]{:S(2)}) copy-start(bf16[1,256,1024]{2,1,0:T(8,128)(2,1)} %param.17) | copy-start | bytes 1572868
  17.4 8.1 %copy-start.7 = (bf16[256,1024]{1,0:T(8,128)(2,1)S(1)}, bf16[256,1024]{1,0:T(8,128)(2,1)}, u32[]{:S(2)}) copy-start(bf16[256,1024]{1,0:T(8,128)(2,1)} %refs_5_.2) | copy-start | bytes 1572868
  17.4 19.8 %collective-permute-start.3 = (bf16[256,1024]{1,0:T(8,128)(2,1)}, bf16[256,1024]{1,0:T(8,128)(2,1)S(1)}, u32[]{:S(2)}, u32[]{:S(2)}) collective-permute-start(bf16[256,1024]{1,0:T(8,128)(2,1)} %get-tuple-element.57.refs_11_), channel_id=1, source_target_pairs={{2,0},{4,2},{6,4},{8,6},{10,8},{12,10},{14,12},{16,14},{18,16},{20... | collective-permute-start | bytes 1572872 | tf_op jit(solution)/shard_map/ppermute | solution.py:572
  21.8 1.0 %copy-start.9 = (bf16[256,768]{1,0:T(8,128)(2,1)S(1)}, bf16[256,768]{1,0:T(8,128)(2,1)}, u32[]{:S(2)}) copy-start(bf16[256,768]{1,0:T(8,128)(2,1)} %get-tuple-element.45.refs_5_.refs_1_) | copy-start | bytes 1179652
  25.4 6.7 %copy-start.4 = (bf16[1,512,1024]{2,1,0:T(8,128)(2,1)S(1)}, bf16[1,512,1024]{2,1,0:T(8,128)(2,1)}, u32[]{:S(2)}) copy-start(bf16[1,512,1024]{2,1,0:T(8,128)(2,1)} %param.25) | copy-start | bytes 3145732
  25.4 6.7 %copy-start.11 = (bf16[256,1024]{1,0:T(8,128)(2,1)S(1)}, bf16[256,1024]{1,0:T(8,128)(2,1)}, u32[]{:S(2)}) copy-start(bf16[256,1024]{1,0:T(8,128)(2,1)} %get-tuple-element.50.refs_11_) | copy-start | bytes 1572868
  25.5 6.7 %copy-start.22 = (f32[1,1024]{1,0:T(1,128)S(1)}, f32[1,1024]{1,0:T(1,128)}, u32[]{:S(2)}) copy-start(f32[1,1024]{1,0:T(1,128)} %get-tuple-element.44.refs_7_.refs_9_) | copy-start | bytes 12292
  26.4 1.6 %collective-permute-start.1 = (bf16[128,1024]{1,0:T(8,128)(2,1)S(1)}, bf16[128,1024]{1,0:T(8,128)(2,1)S(1)}, u32[]{:S(2)}, u32[]{:S(2)}) collective-permute-start(bf16[128,1024]{1,0:T(8,128)(2,1)S(1)} %bitcast.63), channel_id=1, source_target_pairs={{0,1},{1,0},{2,3},{3,2},{4,5},{5,4},{6,7},{7,6},{8,9},{9,8},{10,11... | collective-permute-start | bytes 786440 | tf_op jit(solution)/shard_map/ppermute | solution.py:583
  26.5 1.9 %collective-permute-start.2 = (bf16[128,1024]{1,0:T(8,128)(2,1)S(1)}, bf16[128,1024]{1,0:T(8,128)(2,1)S(1)}, u32[]{:S(2)}, u32[]{:S(2)}) collective-permute-start(bf16[128,1024]{1,0:T(8,128)(2,1)S(1)} %bitcast.62), channel_id=1, source_target_pairs={{0,1},{1,0},{2,3},{3,2},{4,5},{5,4},{6,7},{7,6},{8,9},{9,8},{10,11... | collective-permute-start | bytes 786440 | tf_op jit(solution)/shard_map/ppermute | solution.py:583
  28.5 13.2 %collective-permute-start.7 = (bf16[256,1024]{1,0:T(8,128)(2,1)S(1)}, bf16[256,1024]{1,0:T(8,128)(2,1)S(1)}, u32[]{:S(2)}, u32[]{:S(2)}) collective-permute-start(bf16[256,1024]{1,0:T(8,128)(2,1)S(1)} %sum_pass.2.refs_12_), channel_id=1, source_target_pairs={{0,30},{2,28},{4,26},{6,24},{24,6},{26,4},{28,2},{30,0},{1,31},{3,... | collective-permute-start | bytes 1572872 | tf_op jit(solution)/shard_map/ppermute | solution.py:577
  29.2 47.1 %collective-permute-start.8 = (bf16[256,1024]{1,0:T(8,128)(2,1)S(1)}, bf16[256,1024]{1,0:T(8,128)(2,1)S(1)}, u32[]{:S(2)}, u32[]{:S(2)}) collective-permute-start(bf16[256,1024]{1,0:T(8,128)(2,1)S(1)} %sum_pass.2.refs_12_), channel_id=1, source_target_pairs={{8,22},{10,20},{12,18},{14,16},{16,14},{18,12},{20,10},{22,8},{9,2... | collective-permute-start | bytes 1572872 | tf_op jit(solution)/shard_map/ppermute | solution.py:577
  32.2 5.0 %copy-start.13 = (bf16[256,1024]{1,0:T(8,128)(2,1)S(1)}, bf16[256,1024]{1,0:T(8,128)(2,1)}, u32[]{:S(2)}) copy-start(bf16[256,1024]{1,0:T(8,128)(2,1)} %get-tuple-element.42.refs_0_) | copy-start | bytes 1572868
  32.2 5.0 %copy-start.16 = (bf16[256,768]{1,0:T(8,128)(2,1)S(1)}, bf16[256,768]{1,0:T(8,128)(2,1)}, u32[]{:S(2)}) copy-start(bf16[256,768]{1,0:T(8,128)(2,1)} %get-tuple-element.43.refs_1_) | copy-start | bytes 1179652
  32.2 6.9 %copy-start.3 = (bf16[1,2,256,1024]{3,2,1,0:T(8,128)(2,1)S(1)}, bf16[1,2,256,1024]{3,2,1,0:T(8,128)(2,1)}, u32[]{:S(2)}) copy-start(bf16[1,2,256,1024]{3,2,1,0:T(8,128)(2,1)} %param.14) | copy-start | bytes 3145732
  37.1 2.0 %copy-start.1 = (bf16[1,1024,768]{2,1,0:T(8,128)(2,1)S(1)}, bf16[1,1024,768]{2,1,0:T(8,128)(2,1)}, u32[]{:S(2)}) copy-start(bf16[1,1024,768]{2,1,0:T(8,128)(2,1)} %param.21) | copy-start | bytes 4718596
  37.1 2.0 %copy-start.20 = (f32[1,1024]{1,0:T(1,128)S(1)}, f32[1,1024]{1,0:T(1,128)}, u32[]{:S(2)}) copy-start(f32[1,1024]{1,0:T(1,128)} %refs_4_.7) | copy-start | bytes 12292
  38.5 3.3 %collective-permute-start.5 = (bf16[176,768]{1,0:T(8,128)(2,1)S(1)}, bf16[176,768]{1,0:T(8,128)(2,1)S(1)}, u32[]{:S(2)}, u32[]{:S(2)}) collective-permute-start(bf16[176,768]{1,0:T(8,128)(2,1)S(1)} %bitcast.61), channel_id=1, source_target_pairs={{0,1},{1,0},{2,3},{3,2},{4,5},{5,4},{6,7},{7,6},{8,9},{9,8},{10,11... | collective-permute-start | bytes 811016 | tf_op jit(solution)/shard_map/ppermute | solution.py:583
  38.5 3.2 %collective-permute-start.4 = (bf16[176,768]{1,0:T(8,128)(2,1)S(1)}, bf16[176,768]{1,0:T(8,128)(2,1)S(1)}, u32[]{:S(2)}, u32[]{:S(2)}) collective-permute-start(bf16[176,768]{1,0:T(8,128)(2,1)S(1)} %bitcast.60), channel_id=1, source_target_pairs={{0,1},{1,0},{2,3},{3,2},{4,5},{5,4},{6,7},{7,6},{8,9},{9,8},{10,11... | collective-permute-start | bytes 811016 | tf_op jit(solution)/shard_map/ppermute | solution.py:583
  39.0 2.7 %collective-permute-start.6 = (bf16[176,768]{1,0:T(8,128)(2,1)S(1)}, bf16[176,768]{1,0:T(8,128)(2,1)S(1)}, u32[]{:S(2)}, u32[]{:S(2)}) collective-permute-start(bf16[176,768]{1,0:T(8,128)(2,1)S(1)} %bitcast.59), channel_id=1, source_target_pairs={{0,1},{1,0},{2,3},{3,2},{4,5},{5,4},{6,7},{7,6},{8,9},{9,8},{10,11... | collective-permute-start | bytes 811016 | tf_op jit(solution)/shard_map/ppermute | solution.py:583
  41.8 34.6 %copy-start.5 = (bf16[1,512,1024]{2,1,0:T(8,128)(2,1)S(1)}, bf16[1,512,1024]{2,1,0:T(8,128)(2,1)}, u32[]{:S(2)}) copy-start(bf16[1,512,1024]{2,1,0:T(8,128)(2,1)} %param.22) | copy-start | bytes 3145732
  41.8 34.6 %copy-start.14 = (bf16[256,1024]{1,0:T(8,128)(2,1)S(1)}, bf16[256,1024]{1,0:T(8,128)(2,1)}, u32[]{:S(2)}) copy-start(bf16[256,1024]{1,0:T(8,128)(2,1)} %refs_5_.3) | copy-start | bytes 1572868
  41.8 34.6 %copy-start.15 = (bf16[256,1024]{1,0:T(8,128)(2,1)S(1)}, bf16[256,1024]{1,0:T(8,128)(2,1)}, u32[]{:S(2)}) copy-start(bf16[256,1024]{1,0:T(8,128)(2,1)} %get-tuple-element.57.refs_11_) | copy-start | bytes 1572868
  41.8 34.6 %copy-start.24 = (f32[1,1024]{1,0:T(1,128)S(1)}, f32[1,1024]{1,0:T(1,128)}, u32[]{:S(2)}) copy-start(f32[1,1024]{1,0:T(1,128)} %get-tuple-element.62.refs_9_) | copy-start | bytes 12292
  42.0 50.9 %collective-permute-start.9 = (bf16[528,768]{1,0:T(8,128)(2,1)S(1)}, bf16[528,768]{1,0:T(8,128)(2,1)S(1)}, u32[]{:S(2)}, u32[]{:S(2)}) collective-permute-start(bf16[528,768]{1,0:T(8,128)(2,1)S(1)} %sum_pass.3.refs_13_), channel_id=1, source_target_pairs={{0,30},{2,28},{4,26},{6,24},{8,22},{10,20},{12,18},{14,16},{16,14}... | collective-permute-start | bytes 2433032 | tf_op jit(solution)/shard_map/ppermute | solution.py:577
  76.4 4.1 %copy-start.8 = (bf16[1,256,1024]{2,1,0:T(8,128)(2,1)S(1)}, bf16[1,256,1024]{2,1,0:T(8,128)(2,1)}, u32[]{:S(2)}) copy-start(bf16[1,256,1024]{2,1,0:T(8,128)(2,1)} %param.16) | copy-start | bytes 1572868
  76.4 4.1 %copy-start.10 = (bf16[256,768]{1,0:T(8,128)(2,1)S(1)}, bf16[256,768]{1,0:T(8,128)(2,1)}, u32[]{:S(2)}) copy-start(bf16[256,768]{1,0:T(8,128)(2,1)} %get-tuple-element.45.refs_5_.refs_1_) | copy-start | bytes 1179652
  76.4 4.1 %copy-start.12 = (bf16[256,1024]{1,0:T(8,128)(2,1)S(1)}, bf16[256,1024]{1,0:T(8,128)(2,1)}, u32[]{:S(2)}) copy-start(bf16[256,1024]{1,0:T(8,128)(2,1)} %get-tuple-element.68.refs_0_) | copy-start | bytes 1572868
  76.4 4.1 %copy-start.17 = (bf16[256,512]{1,0:T(8,128)(2,1)S(1)}, bf16[256,512]{1,0:T(8,128)(2,1)}, u32[]{:S(2)}) copy-start(bf16[256,512]{1,0:T(8,128)(2,1)} %get-tuple-element.69.refs_2_) | copy-start | bytes 786436
  82.5 2.2 %collective-permute-start.10 = (bf16[1296,256]{1,0:T(8,128)(2,1)S(1)}, bf16[1296,256]{1,0:T(8,128)(2,1)S(1)}, u32[]{:S(2)}, u32[]{:S(2)}) collective-permute-start(bf16[1296,256]{1,0:T(8,128)(2,1)S(1)} %bitcast.58), channel_id=1, source_target_pairs={{0,1},{1,0},{2,3},{3,2},{4,5},{5,4},{6,7},{7,6},{8,9},{9,8},{10,11... | collective-permute-start | bytes 1990664 | tf_op jit(solution)/shard_map/ppermute | solution.py:583
  82.6 3.0 %collective-permute-start.11 = (bf16[1296,256]{1,0:T(8,128)(2,1)S(1)}, bf16[1296,256]{1,0:T(8,128)(2,1)S(1)}, u32[]{:S(2)}, u32[]{:S(2)}) collective-permute-start(bf16[1296,256]{1,0:T(8,128)(2,1)S(1)} %bitcast.57), channel_id=1, source_target_pairs={{0,1},{1,0},{2,3},{3,2},{4,5},{5,4},{6,7},{7,6},{8,9},{9,8},{10,11... | collective-permute-start | bytes 1990664 | tf_op jit(solution)/shard_map/ppermute | solution.py:583

commit v4 on v3

--- a/solution.py
+++ b/solution.py
@@ -12,6 +12,7 @@
 EPSILON = 1e-05
 MASKED = -1e30
 PAD = 16
+LANES = 128
 PACKED_PAD = 32
 PIECES = 2
 PIECES_OUT = 2
@@ -492,9 +493,9 @@
     return sends, keep
 
 
-def final_kernel(keep, outer_out, inner_out, mirror_qkv, *refs, parts, pieces):
+def own_kernel(keep, outer_out, inner_out, *refs, parts, pieces):
     moved, refs = refs[: (parts - 1) * pieces], refs[(parts - 1) * pieces :]
-    gain_hbm, qkv_hbm, out_hbm, gain_ref, qkv_ref, out_ref, sems = refs
+    out_hbm, qkv_ref, gain_ref, out_ref, sem = refs
     model, width = out_ref.shape[1], qkv_ref.shape[1]
     unit, out_rows, qkv_rows, start, gain_at, rows = layout(parts, out_ref.shape[0] * parts, model, width)
     each = rows // pieces
@@ -511,59 +512,104 @@
             result = result + (taken[0] if len(taken) == 1 else jnp.concatenate(taken, axis=0))
         return result
 
-    for c in range(width // unit):
-        columns = slice(c * unit, (c + 1) * unit)
-        qkv_ref[:, columns] = total(start + c * qkv_rows, qkv_rows) + mirror_qkv[:qkv_rows, columns].astype(F32)
-    copies = [pltpu.make_async_copy(qkv_ref, qkv_hbm, sems.at[0])]
-    copies[0].start()
     for c in range(model // unit):
         columns = slice(c * unit, (c + 1) * unit)
         out_ref[:, columns] = total(c * out_rows, out_rows) + (outer_out[:, columns] + inner_out[:, columns]).astype(F32)
-    copies.append(pltpu.make_async_copy(out_ref, out_hbm, sems.at[1]))
-    copies[1].start()
+    copy = pltpu.make_async_copy(out_ref, out_hbm, sem)
+    copy.start()
+    for c in range(width // unit):
+        qkv_ref[:, c * unit : (c + 1) * unit] = total(start + c * qkv_rows, qkv_rows)
     lines = total(gain_at, PACKED_PAD)
-    other = mirror_qkv[qkv_rows:, :].astype(F32)
     for i in range(pl.cdiv(qkv_rows, unit)):
         until = min((i + 1) * unit, qkv_rows)
-        gain_ref[:, i * unit : until] = lines[i : i + 1, : until - i * unit] + other[:1, i * unit : until]
-    copies.append(pltpu.make_async_copy(gain_ref, gain_hbm, sems.at[2]))
-    copies[2].start()
+        gain_ref[:, i * unit : until] = lines[i : i + 1, : until - i * unit]
+    copy.wait()
+
+
+def own_pass(keep, outer_out, inner_out, moved, parts, query_width, model, width):
+    hbm, vmem = pltpu.HBM, pltpu.VMEM
+    out_shape = (query_width // parts, model)
+    return call(
+        functools.partial(own_kernel, parts=parts, pieces=len(moved[0])),
+        "own_pass",
+        [(keep, vmem), (outer_out, vmem), (inner_out, vmem)] + [(m, vmem) for per in moved for m in per],
+        [
+            (out_shape, F32, hbm),
+            ((model // parts, width), F32, vmem),
+            ((1, model // parts), F32, vmem),
+        ],
+        [pltpu.VMEM(out_shape, F32), pltpu.SemaphoreType.DMA(())],
+    )
+
+
+def final_kernel(own_qkv, own_gain, mirror_qkv, mirror_gains, gain_hbm, qkv_hbm, gain_ref, qkv_ref, sems):
+    rows, width = qkv_ref.shape
+    half = rows // 2
+    lanes = mirror_gains.shape[1]
+    lines = mirror_gains[...].astype(F32)
+    for i in range(gain_ref.shape[1] // lanes):
+        at = slice(i * lanes, (i + 1) * lanes)
+        gain_ref[:, at] = own_gain[:, at] + lines[i : i + 1, :]
+    copies = [pltpu.make_async_copy(gain_ref, gain_hbm, sems.at[0])]
+    copies[0].start()
+    for i in range(2):
+        at = slice(i * half, (i + 1) * half)
+        qkv_ref[at, :] = own_qkv[at, :] + mirror_qkv[at, :].astype(F32)
+        copies.append(pltpu.make_async_copy(qkv_ref.at[at], qkv_hbm.at[at], sems.at[1 + i]))
+        copies[-1].start()
     for copy in copies:
         copy.wait()
 
 
-def final_pass(keep, outer_out, inner_out, mirror_qkv, moved, parts, query_width, model, width):
+def final_pass(own_qkv, own_gain, mirror_qkv, mirror_gains):
     hbm, vmem = pltpu.HBM, pltpu.VMEM
-    shapes = ((1, model // parts), (model // parts, width), (query_width // parts, model))
     return call(
-        functools.partial(final_kernel, parts=parts, pieces=len(moved[0])),
+        final_kernel,
         "final_pass",
-        [(keep, vmem), (outer_out, vmem), (inner_out, vmem), (mirror_qkv, vmem)] + [(m, vmem) for per in moved for m in per],
-        [(shape, F32, hbm) for shape in shapes],
-        [pltpu.VMEM(shape, F32) for shape in shapes] + [pltpu.SemaphoreType.DMA((3,))],
-    )
-
-
-def sum_kernel(keep, *refs):
-    *moved, sum_ref = refs
-    pieces = len(moved)
-    at = 0
-    for p in range(pieces):
-        rows = moved[p].shape[1]
-        total = keep[at : at + rows, :].astype(F32)
-        for k in range(moved[p].shape[0]):
-            total = total + moved[p][k].astype(F32)
-        sum_ref[at : at + rows, :] = total.astype(BF16)
-        at += rows
-
-
-def sum_pass(keep, moved, after=()):
+        [(own_qkv, vmem), (own_gain, vmem), (mirror_qkv, vmem), (mirror_gains, vmem)],
+        [(own_gain.shape, F32, hbm), (own_qkv.shape, F32, hbm)],
+        [pltpu.VMEM(own_gain.shape, F32), pltpu.VMEM(own_qkv.shape, F32), pltpu.SemaphoreType.DMA((3,))],
+    )
+
+
+def summed(keep, moved, at, rows):
+    total = keep[at : at + rows, :].astype(F32)
+    first, taken = 0, []
+    for part in moved:
+        low, high = max(at, first), min(at + rows, first + part.shape[1])
+        if low < high:
+            piece = part[0, low - first : high - first, :].astype(F32)
+            for k in range(1, part.shape[0]):
+                piece = piece + part[k, low - first : high - first, :].astype(F32)
+            taken.append(piece)
+        first += part.shape[1]
+    return total + (taken[0] if len(taken) == 1 else jnp.concatenate(taken, axis=0))
+
+
+def sum_kernel(keep, *refs, gains):
+    moved, outs = refs[: -1 - bool(gains)], refs[-1 - bool(gains) :]
+    rows = outs[0].shape[0]
+    outs[0][...] = summed(keep, moved, 0, rows).astype(BF16)
+    if gains:
+        line = summed(keep, moved, rows, PAD)[:1, :gains]
+        lanes = outs[1].shape[1]
+        row = lax.broadcasted_iota(jnp.int32, outs[1].shape, 0)
+        block = jnp.zeros(outs[1].shape, F32)
+        for i in range(gains // lanes):
+            block = jnp.where(row == i, line[:, i * lanes : (i + 1) * lanes], block)
+        outs[1][...] = block.astype(BF16)
+
+
+def sum_pass(keep, moved, gains=0, after=()):
     vmem = pltpu.VMEM
     pieces = [jnp.stack([per[p] for per in moved]) if len(moved) > 1 else moved[0][p][None] for p in range(len(moved[0]))]
-    (total,) = call(
-        sum_kernel, "sum_pass", [(keep, vmem)] + [(p, vmem) for p in pieces], [(keep.shape, BF16, vmem)], [], after
-    )
-    return total
+    outputs = [((keep.shape[0] - (PAD if gains else 0), keep.shape[1]), BF16, vmem)]
+    if gains:
+        outputs += [((16 * pl.cdiv(gains, 16 * LANES), LANES), BF16, vmem)]
+    return call(
+        functools.partial(sum_kernel, gains=gains),
+        "sum_pass", [(keep, vmem)] + [(p, vmem) for p in pieces], outputs, [], after,
+    )
 
 
 def shifted(value, axis, steps):
@@ -605,9 +651,9 @@
     up_moved = shifted(up_one[0], "section", 1)
     down_one = first_pass(0, ints, act_down[0], *down, grad_down[0], limit=60 * 1024 * 1024, after=(up_one[4],))
     down_moved = shifted(down_one[0], "section", -1)
-    up_forward = forward_pass(1, ints, act_up[0], gain_up, qkv_up[0], query_width, after=(down_one[3],))
+    up_forward = forward_pass(1, ints, act_up[0], gain_up, qkv_up[0], query_width)
     sends, keep = outproj_pass(1, up_one[2], up_forward[2], grad_up[0], up_moved, seed_up, parts)
-    up_out = sum_pass(keep, exchanged(sends, "dp"))
+    (up_out,) = sum_pass(keep, exchanged(sends, "dp"))
     outer_out = mirrored(up_out, "section", outer)
     inner_out = mirrored(up_out, "section", inner)
     up_two = backward_pass(
@@ -615,7 +661,10 @@
     )
     sends, keep = qkv_pass(up_one[1], up_one[3], up_forward[0], up_two[1], up_two[2], parts, after=(down_moved,))
     down_forward = forward_pass(0, ints, act_down[0], gain_down, qkv_down[0], query_width, after=(keep,))
-    up_qkv = sum_pass(keep, exchanged(sends, "dp"), after=(outer_out, down_forward[2]))
+    up_qkv, up_gains = sum_pass(
+        keep, exchanged(sends, "dp"), model // parts, after=(outer_out, down_forward[2])
+    )
+    mirror_gains = mirrored(up_gains, "section")
     mirror_qkv = mirrored(up_qkv, "section")
     down_two = backward_pass(
         0, slot_order, act_down[0], *down, seed_down, down_forward, down_one[4], down_moved, down_one[0],
@@ -625,9 +674,10 @@
         down_one[1], down_one[3], down_one[2], grad_down[0],
         down_forward[0], down_two[1], down_forward[2], down_two[0], down_two[2], parts,
     )
-    grad_gain, grad_qkv, grad_outproj = final_pass(
-        keep, outer_out, inner_out, mirror_qkv, exchanged(sends, "dp"), parts, query_width, model, width
-    )
+    grad_outproj, own_qkv, own_gain = own_pass(
+        keep, outer_out, inner_out, exchanged(sends, "dp"), parts, query_width, model, width
+    )
+    grad_gain, grad_qkv = final_pass(own_qkv, own_gain, mirror_qkv, mirror_gains)
     return (down_two[3][:, None], grad_gain, grad_qkv[None], grad_outproj[None])
 
 

time: 95.2 us -> 93.3 us (0.980)
  waiting for transfers between devices: 42.6 us -> 39.4 us
  starting transfers between devices: 16.1 us -> 17.6 us
  local copies, waits for them, and re-layouts: 1.13 us -> 0.14 us
    ppermute x3 -> x4, waiting for transfers between devices: 38.7 us -> 36.6 us  [mirrored(): lax.ppermute(value, axis, [(i, count - 1 - i) for i in (range(count) if s...]
    ppermute x7, waiting for transfers between devices: 3.95 us -> 2.35 us  [exchanged(): lax.ppermute(send[k], axis, [(i, (i + 1 + k) % parts) for i in range(part...]
    ppermute x3 -> x4, starting transfers between devices: 6.5 us -> 8.09 us  [mirrored(): lax.ppermute(value, axis, [(i, count - 1 - i) for i in (range(count) if s...]
    unnamed x50 -> x48, local copies, waits for them, and re-layouts: 1.13 us -> 0.14 us
    pallas_call x12 -> x13, Pallas kernels: 33.7 us -> 34.4 us  [call(): pl.pallas_call(ordered, out_shape=tuple((jax.ShapeDtypeStruct(shape, dtyp...]
  transfers between devices with their start and end apart: 12 -> 13, of which waited for: 6 -> 6; matrix products, arithmetic and copies ran while one was open for 0% -> 0% of each run, Pallas kernels for 27% -> 29%
where the time goes in v4:
time: 93.3 us; the launch traced here: 92.9 us
  waiting for transfers between devices  39.4 us (42%)
  Pallas kernels  34.4 us (37%)
  starting transfers between devices  17.6 us (19%)
  between operations  1.29 us (1%)
    ppermute x4, waiting for transfers between devices, mirrored(): lax.ppermute(value, axis, [(i, count - 1 - i) for i in (range(count) if s...  36.6 us
    pallas_call x13, Pallas kernels, call(): pl.pallas_call(ordered, out_shape=tuple((jax.ShapeDtypeStruct(shape, dtyp...  34.4 us
    ppermute x4, starting transfers between devices, mirrored(): lax.ppermute(value, axis, [(i, count - 1 - i) for i in (range(count) if s...  8.09 us
    ppermute x2, starting transfers between devices, shifted(): lax.ppermute(value, axis, [(source, source + steps) for source in range(f...  7.77 us
    ppermute x7, waiting for transfers between devices, exchanged(): lax.ppermute(send[k], axis, [(i, (i + 1 + k) % parts) for i in range(part...  2.35 us
  transfers between devices with their start and end apart: 13, of which 6 were waited for; matrix products, arithmetic and copies ran while one was open for 0% of the time, Pallas kernels for 29%

profile of v4, /device:TPU:16, one launch (start us, length us, event | category | flops | bytes accessed | tf_op | source)
XLA Modules:
  0.0 92.9 jit_solution(9561572225518601665)
XLA Ops:
  0.6 6.5 %first_pass.2 = (bf16[256,1024]{1,0:T(8,128)(2,1)}, bf16[256,1024]{1,0:T(8,128)(2,1)}, bf16[256,512]{1,0:T(8,128)(2,1)}, bf16[256,768]{1,0:T(8,128)(2,1)}, f32[1,1024]{1,0:T(1,128)}) custom-call(s32[2,1,2]{2,1,0:T(1,128)} %refs_0_.11, s32[2,1,2]{2,1,0:T(1,128)} %bitcast.53, bf16[2,256,1024]{2,1,0:T(8,128)(2,1)} %bitcast.34, bf16[1024,768]{1,0:T(8,128)(2,1)} %bitcast.28, ...), custom_call_target="tpu_custom_call" | custom-call | flops 1 | bytes 1 | tf_op jit(solution)/shard_map/first_pass/pallas_call | solution.py:155
  7.2 3.4 %collective-permute-start = (bf16[256,1024]{1,0:T(8,128)(2,1)}, bf16[256,1024]{1,0:T(8,128)(2,1)S(1)}, u32[]{:S(2)}, u32[]{:S(2)}) collective-permute-start(bf16[256,1024]{1,0:T(8,128)(2,1)} %get-tuple-element.53.refs_11_), channel_id=1, source_target_pairs={{0,2},{2,4},{4,6},{6,8},{8,10},{10,12},{12,14},{14,16},{16,18},{18... | collective-permute-start | bytes 1572872 | tf_op jit(solution)/shard_map/ppermute | solution.py:618
  10.6 0.0 copy-start
  10.6 0.0 copy-start.2
  10.6 0.0 copy-start.18
  10.6 0.0 copy-start.20
  10.6 0.0 copy-start.22
  10.6 6.7 %first_pass.3 = (bf16[256,1024]{1,0:T(8,128)(2,1)}, bf16[256,1024]{1,0:T(8,128)(2,1)}, bf16[256,512]{1,0:T(8,128)(2,1)}, bf16[256,768]{1,0:T(8,128)(2,1)}, f32[1,1024]{1,0:T(1,128)}) custom-call(s32[2,1,2]{2,1,0:T(1,128)} %refs_0_.11, s32[2,1,2]{2,1,0:T(1,128)} %bitcast.54, bf16[2,256,1024]{2,1,0:T(8,128)(2,1)} %bitcast.37, bf16[1024,768]{1,0:T(8,128)(2,1)} %bitcast.31, ...), custom_call_target="tpu_custom_call" | custom-call | flops 1 | bytes 1 | tf_op jit(solution)/shard_map/first_pass/pallas_call | solution.py:155
  17.3 0.0 copy-start.6
  17.4 0.0 copy-start.7
  17.4 0.0 copy-start.17
  17.4 4.4 %collective-permute-start.3 = (bf16[256,1024]{1,0:T(8,128)(2,1)}, bf16[256,1024]{1,0:T(8,128)(2,1)S(1)}, u32[]{:S(2)}, u32[]{:S(2)}) collective-permute-start(bf16[256,1024]{1,0:T(8,128)(2,1)} %get-tuple-element.60.refs_11_), channel_id=1, source_target_pairs={{2,0},{4,2},{6,4},{8,6},{10,8},{12,10},{14,12},{16,14},{18,16},{20... | collective-permute-start | bytes 1572872 | tf_op jit(solution)/shard_map/ppermute | solution.py:618
  21.8 2.6 %forward_pass.2 = (bf16[256,1024]{1,0:T(8,128)(2,1)S(1)}, bf16[256,768]{1,0:T(8,128)(2,1)S(1)}, bf16[256,512]{1,0:T(8,128)(2,1)S(1)}, bf16[4,256,512]{2,1,0:T(8,128)(2,1)S(1)}) custom-call(s32[2,1,2]{2,1,0:T(1,128)S(1)} %copy-done.20, s32[2,1,2]{2,1,0:T(1,128)S(1)} %bitcast.55, bf16[2,256,1024]{2,1,0:T(8,128)(2,1)S(1)} %bitcast.35, ...), custom_call_target="tpu_custom_call" | custom-call | flops 1 | bytes 1 | tf_op jit(solution)/shard_map/forward_pass/pallas_call | solution.py:155
  24.4 0.4 collective-permute-done.refs_4_.refs_10_
  24.9 0.0 copy-start.4
  24.9 0.0 copy-start.11
  24.9 0.9 %outproj_pass.1 = (bf16[1,128,1024]{2,1,0:T(8,128)(2,1)S(1)}, bf16[1,128,1024]{2,1,0:T(8,128)(2,1)S(1)}, bf16[256,1024]{1,0:T(8,128)(2,1)S(1)}) custom-call(bf16[256,1024]{1,0:T(8,128)(2,1)S(1)} %bitcast.45, bf16[256,1024]{1,0:T(8,128)(2,1)S(1)} %copy-done.7, bf16[256,512]{1,0:T(8,128)(2,1)S(1)} %copy-done.17, ...), custom_call_target="tpu_custom_call" | custom-call | flops 1 | bytes 1 | tf_op jit(solution)/shard_map/outproj_pass/pallas_call | solution.py:155
  25.8 0.1 collective-permute-start.1
  25.9 0.5 collective-permute-start.2
  26.4 1.0 %collective-permute-done.1 = bf16[128,1024]{1,0:T(8,128)(2,1)S(1)} collective-permute-done((bf16[128,1024]{1,0:T(8,128)(2,1)S(1)}, bf16[128,1024]{1,0:T(8,128)(2,1)S(1)}, u32[]{:S(2)}, u32[]{:S(2)}) %collective-permute-start.1) | collective-permute-done | bytes 262176 | tf_op jit(solution)/shard_map/ppermute | solution.py:629
  27.4 0.4 collective-permute-done.2
  27.8 0.1 sum_pass.2.refs_12_
  27.9 0.7 collective-permute-start.7
  28.6 3.5 %collective-permute-start.8 = (bf16[256,1024]{1,0:T(8,128)(2,1)S(1)}, bf16[256,1024]{1,0:T(8,128)(2,1)S(1)}, u32[]{:S(2)}, u32[]{:S(2)}) collective-permute-start(bf16[256,1024]{1,0:T(8,128)(2,1)S(1)} %sum_pass.2.refs_12_), channel_id=1, source_target_pairs={{8,22},{10,20},{12,18},{14,16},{16,14},{18,12},{20,10},{22,8},{9,2... | collective-permute-start | bytes 1572872 | tf_op jit(solution)/shard_map/ppermute | solution.py:623
  32.2 0.0 copy-start.13
  32.2 0.0 copy-start.3
  32.2 4.9 %backward_pass.2 = (bf16[256,1024]{1,0:T(8,128)(2,1)}, bf16[256,768]{1,0:T(8,128)(2,1)S(1)}, f32[1,1024]{1,0:T(1,128)S(1)}, bf16[2,2,256,1024]{3,2,1,0:T(8,128)(2,1)}) custom-call(s32[2,1,2]{2,1,0:T(1,128)S(1)} %copy-done.20, bf16[2,256,1024]{2,1,0:T(8,128)(2,1)S(1)} %bitcast.36, bf16[1024,768]{1,0:T(8,128)(2,1)S(1)} %bitcast.30, ...), custom_call_target="tpu_custom_call" | custom-call | flops 1 | bytes 1 | tf_op jit(solution)/shard_map/backward_pass/pallas_call | solution.py:155
  37.2 0.0 copy-start.19
  37.2 1.3 %qkv_pass.1 = (bf16[1,176,768]{2,1,0:T(8,128)(2,1)S(1)}, bf16[1,176,768]{2,1,0:T(8,128)(2,1)S(1)}, bf16[1,176,768]{2,1,0:T(8,128)(2,1)S(1)}, bf16[528,768]{1,0:T(8,128)(2,1)S(1)}) custom-call(bf16[256,1024]{1,0:T(8,128)(2,1)S(1)} %copy-done.13, bf16[256,768]{1,0:T(8,128)(2,1)S(1)} %copy-done.14, bf16[256,1024]{1,0:T(8,128)(2,1)S(1)} %get-tuple-element.48.refs_2_, ...), custom_call_target="tpu_custom_call" | custom-call | flops 1 | bytes 1 | tf_op jit(solution)/shard_map/qkv_pass/pallas_call | solution.py:155
  38.5 0.1 collective-permute-start.5
  38.5 0.5 collective-permute-start.4
  39.0 0.1 collective-permute-start.6
  39.1 2.6 %forward_pass.3 = (bf16[256,1024]{1,0:T(8,128)(2,1)S(1)}, bf16[256,768]{1,0:T(8,128)(2,1)S(1)}, bf16[256,512]{1,0:T(8,128)(2,1)S(1)}, bf16[4,256,512]{2,1,0:T(8,128)(2,1)S(1)}) custom-call(s32[2,1,2]{2,1,0:T(1,128)S(1)} %copy-done.20, s32[2,1,2]{2,1,0:T(1,128)S(1)} %bitcast.56, bf16[2,256,1024]{2,1,0:T(8,128)(2,1)S(1)} %bitcast.38, ...), custom_call_target="tpu_custom_call" | custom-call | flops 1 | bytes 1 | tf_op jit(solution)/shard_map/forward_pass/pallas_call | solution.py:155
  41.7 0.0 copy-start.5
  41.7 0.0 copy-start.9
  41.8 0.2 sum_pass.3
  42.0 2.3 %collective-permute-start.11 = (bf16[512,768]{1,0:T(8,128)(2,1)S(1)}, bf16[512,768]{1,0:T(8,128)(2,1)S(1)}, u32[]{:S(2)}, u32[]{:S(2)}) collective-permute-start(bf16[512,768]{1,0:T(8,128)(2,1)S(1)} %get-tuple-element.70.refs_13_), channel_id=1, source_target_pairs={{0,30},{2,28},{4,26},{6,24},{8,22},{10,20},{12,18},{14,16},{16,14}... | collective-permute-start | bytes 2359304 | tf_op jit(solution)/shard_map/ppermute | solution.py:623
  44.3 31.0 %collective-permute-done.8.refs_14_.refs_2_ = bf16[256,1024]{1,0:T(8,128)(2,1)S(1)} collective-permute-done((bf16[256,1024]{1,0:T(8,128)(2,1)S(1)}, bf16[256,1024]{1,0:T(8,128)(2,1)S(1)}, u32[]{:S(2)}, u32[]{:S(2)}) %collective-permute-start.8) | collective-permute-done | bytes 524320 | tf_op jit(solution)/shard_map/ppermute | solution.py:623
  75.3 0.0 copy-start.8
  75.4 4.0 %backward_pass.3 = (bf16[256,1024]{1,0:T(8,128)(2,1)S(1)}, bf16[256,768]{1,0:T(8,128)(2,1)S(1)}, f32[1,1024]{1,0:T(1,128)S(1)}, bf16[2,2,256,1024]{3,2,1,0:T(8,128)(2,1)}) custom-call(s32[2,1,2]{2,1,0:T(1,128)S(1)} %copy-done.20, bf16[2,256,1024]{2,1,0:T(8,128)(2,1)S(1)} %bitcast.39, ...), custom_call_target="tpu_custom_call", output_to_operand_aliasing={{3}: (12, {})} | custom-call | flops 1 | bytes 1 | tf_op jit(solution)/shard_map/backward_pass/pallas_call | solution.py:155
  79.5 2.0 %packed_pass.1 = (bf16[1,1296,256]{2,1,0:T(8,128)(2,1)S(1)}, bf16[1,1296,256]{2,1,0:T(8,128)(2,1)S(1)}, bf16[2592,256]{1,0:T(8,128)(2,1)S(1)}) custom-call(bf16[256,1024]{1,0:T(8,128)(2,1)S(1)} %copy-done.12, bf16[256,768]{1,0:T(8,128)(2,1)S(1)} %copy-done.15, bf16[256,512]{1,0:T(8,128)(2,1)S(1)} %copy-done.16, bf16[256,1024]{1,0:T(8,128)(2,1)S(1)} %bitcast.47, ...), custom_call_target="tpu_custom_call" | custom-call | flops 1 | bytes 1 | tf_op jit(solution)/shard_map/packed_pass/pallas_call | solution.py:155
  81.5 0.1 collective-permute-start.9
  81.6 0.5 collective-permute-start.10
  82.1 1.6 %collective-permute-start.12 = (bf16[16,128]{1,0:T(8,128)(2,1)S(1)}, bf16[16,128]{1,0:T(8,128)(2,1)S(1)}, u32[]{:S(2)}, u32[]{:S(2)}) collective-permute-start(bf16[16,128]{1,0:T(8,128)(2,1)S(1)} %get-tuple-element.84), channel_id=1, source_target_pairs={{0,30},{2,28},{4,26},{6,24},{8,22},{10,20},{12,18},{14,16},{16,14}... | collective-permute-start | bytes 12296 | tf_op jit(solution)/shard_map/ppermute | solution.py:623
  83.7 0.9 %collective-permute-done.10.refs_4_ = bf16[1296,256]{1,0:T(8,128)(2,1)S(1)} collective-permute-done((bf16[1296,256]{1,0:T(8,128)(2,1)S(1)}, bf16[1296,256]{1,0:T(8,128)(2,1)S(1)}, u32[]{:S(2)}, u32[]{:S(2)}) %collective-permute-start.10) | collective-permute-done | bytes 663584 | tf_op jit(solution)/shard_map/ppermute | solution.py:629
  84.7 1.2 %own_pass.1 = (f32[256,1024]{1,0:T(8,128)}, f32[512,768]{1,0:T(8,128)S(1)}, f32[1,512]{1,0:T(1,128)S(1)}) custom-call(bf16[2592,256]{1,0:T(8,128)(2,1)S(1)} %get-tuple-element.79.refs_0_, bf16[256,1024]{1,0:T(8,128)(2,1)S(1)} %collective-permute-done.7.refs_4_.refs_1_, bf16[256,1024]{1,0:T(8,128)(2,1)S(1)} %collective-permute-done.8.refs_14_.refs_2_, ...), custom_call_target="tpu_custom_call" | custom-call | flops 1 | bytes 1 | tf_op jit(solution)/shard_map/own_pass/pallas_call | solution.py:155
  85.8 5.6 %collective-permute-done.12.refs_3_ = bf16[16,128]{1,0:T(8,128)(2,1)S(1)} collective-permute-done((bf16[16,128]{1,0:T(8,128)(2,1)S(1)}, bf16[16,128]{1,0:T(8,128)(2,1)S(1)}, u32[]{:S(2)}, u32[]{:S(2)}) %collective-permute-start.12) | collective-permute-done | bytes 4128 | tf_op jit(solution)/shard_map/ppermute | solution.py:623
  91.5 1.2 %final_pass.1 = (f32[1,512]{1,0:T(1,128)}, f32[512,768]{1,0:T(8,128)}) custom-call(f32[512,768]{1,0:T(8,128)S(1)} %get-tuple-element.82.refs_0_, f32[1,512]{1,0:T(1,128)S(1)} %get-tuple-element.83.refs_1_, bf16[512,768]{1,0:T(8,128)(2,1)S(1)} %collective-permute-done.11.refs_2_, bf16[16,128]{1,0:T(8,128)(2,1)S(1)} %collective-permute-done.12.refs_3_), custom_call_target="tpu_custom_call" | custom-call | flops 1 | bytes 1 | tf_op jit(solution)/shard_map/final_pass/pallas_call | solution.py:155
  (39 shorter events, 0.1 us)
Async XLA Ops:
  7.2 17.7 %collective-permute-start = (bf16[256,1024]{1,0:T(8,128)(2,1)}, bf16[256,1024]{1,0:T(8,128)(2,1)S(1)}, u32[]{:S(2)}, u32[]{:S(2)}) collective-permute-start(bf16[256,1024]{1,0:T(8,128)(2,1)} %get-tuple-element.53.refs_11_), channel_id=1, source_target_pairs={{0,2},{2,4},{4,6},{6,8},{8,10},{10,12},{12,14},{14,16},{16,18},{18... | collective-permute-start | bytes 1572872 | tf_op jit(solution)/shard_map/ppermute | solution.py:618
  10.6 11.2 %copy-start = (bf16[1,1024,768]{2,1,0:T(8,128)(2,1)S(1)}, bf16[1,1024,768]{2,1,0:T(8,128)(2,1)}, u32[]{:S(2)}) copy-start(bf16[1,1024,768]{2,1,0:T(8,128)(2,1)} %param.24) | copy-start | bytes 4718596
  10.6 11.2 %copy-start.2 = (bf16[1,2,256,1024]{3,2,1,0:T(8,128)(2,1)S(1)}, bf16[1,2,256,1024]{3,2,1,0:T(8,128)(2,1)}, u32[]{:S(2)}) copy-start(bf16[1,2,256,1024]{3,2,1,0:T(8,128)(2,1)} %param.15) | copy-start | bytes 3145732
  10.6 11.2 %copy-start.18 = (f32[1,1024]{1,0:T(1,128)S(1)}, f32[1,1024]{1,0:T(1,128)}, u32[]{:S(2)}) copy-start(f32[1,1024]{1,0:T(1,128)} %refs_4_.5) | copy-start | bytes 12292
  10.6 11.2 %copy-start.20 = (s32[2,1,2]{2,1,0:T(1,128)S(1)}, s32[2,1,2]{2,1,0:T(1,128)}, u32[]{:S(2)}) copy-start(s32[2,1,2]{2,1,0:T(1,128)} %refs_0_.11) | copy-start | bytes 52
  10.6 11.2 %copy-start.22 = (s32[2,1,2,1]{2,3,1,0:T(1,128)S(1)}, s32[2,1,2,1]{2,3,1,0:T(1,128)}, u32[]{:S(2)}) copy-start(s32[2,1,2,1]{2,3,1,0:T(1,128)} %param.26) | copy-start | bytes 52
  17.3 7.5 %copy-start.6 = (bf16[1,256,1024]{2,1,0:T(8,128)(2,1)S(1)}, bf16[1,256,1024]{2,1,0:T(8,128)(2,1)}, u32[]{:S(2)}) copy-start(bf16[1,256,1024]{2,1,0:T(8,128)(2,1)} %param.17) | copy-start | bytes 1572868
  17.4 7.5 %copy-start.7 = (bf16[256,1024]{1,0:T(8,128)(2,1)S(1)}, bf16[256,1024]{1,0:T(8,128)(2,1)}, u32[]{:S(2)}) copy-start(bf16[256,1024]{1,0:T(8,128)(2,1)} %refs_5_.2) | copy-start | bytes 1572868
  17.4 7.5 %copy-start.17 = (bf16[256,512]{1,0:T(8,128)(2,1)S(1)}, bf16[256,512]{1,0:T(8,128)(2,1)}, u32[]{:S(2)}) copy-start(bf16[256,512]{1,0:T(8,128)(2,1)} %get-tuple-element.54.refs_2_) | copy-start | bytes 786436
  17.4 19.8 %collective-permute-start.3 = (bf16[256,1024]{1,0:T(8,128)(2,1)}, bf16[256,1024]{1,0:T(8,128)(2,1)S(1)}, u32[]{:S(2)}, u32[]{:S(2)}) collective-permute-start(bf16[256,1024]{1,0:T(8,128)(2,1)} %get-tuple-element.60.refs_11_), channel_id=1, source_target_pairs={{2,0},{4,2},{6,4},{8,6},{10,8},{12,10},{14,12},{16,14},{18,16},{20... | collective-permute-start | bytes 1572872 | tf_op jit(solution)/shard_map/ppermute | solution.py:618
  24.9 7.3 %copy-start.4 = (bf16[1,512,1024]{2,1,0:T(8,128)(2,1)S(1)}, bf16[1,512,1024]{2,1,0:T(8,128)(2,1)}, u32[]{:S(2)}) copy-start(bf16[1,512,1024]{2,1,0:T(8,128)(2,1)} %param.25) | copy-start | bytes 3145732
  24.9 7.3 %copy-start.11 = (bf16[256,1024]{1,0:T(8,128)(2,1)S(1)}, bf16[256,1024]{1,0:T(8,128)(2,1)}, u32[]{:S(2)}) copy-start(bf16[256,1024]{1,0:T(8,128)(2,1)} %get-tuple-element.53.refs_11_) | copy-start | bytes 1572868
  24.9 7.3 %copy-start.21 = (f32[1,1024]{1,0:T(1,128)S(1)}, f32[1,1024]{1,0:T(1,128)}, u32[]{:S(2)}) copy-start(f32[1,1024]{1,0:T(1,128)} %get-tuple-element.52.refs_9_.refs_7_) | copy-start | bytes 12292
  25.8 1.6 %collective-permute-start.1 = (bf16[128,1024]{1,0:T(8,128)(2,1)S(1)}, bf16[128,1024]{1,0:T(8,128)(2,1)S(1)}, u32[]{:S(2)}, u32[]{:S(2)}) collective-permute-start(bf16[128,1024]{1,0:T(8,128)(2,1)S(1)} %bitcast.63), channel_id=1, source_target_pairs={{0,1},{1,0},{2,3},{3,2},{4,5},{5,4},{6,7},{7,6},{8,9},{9,8},{10,11... | collective-permute-start | bytes 786440 | tf_op jit(solution)/shard_map/ppermute | solution.py:629
  25.9 1.9 %collective-permute-start.2 = (bf16[128,1024]{1,0:T(8,128)(2,1)S(1)}, bf16[128,1024]{1,0:T(8,128)(2,1)S(1)}, u32[]{:S(2)}, u32[]{:S(2)}) collective-permute-start(bf16[128,1024]{1,0:T(8,128)(2,1)S(1)} %bitcast.62), channel_id=1, source_target_pairs={{0,1},{1,0},{2,3},{3,2},{4,5},{5,4},{6,7},{7,6},{8,9},{9,8},{10,11... | collective-permute-start | bytes 786440 | tf_op jit(solution)/shard_map/ppermute | solution.py:629
  27.9 13.9 %collective-permute-start.7 = (bf16[256,1024]{1,0:T(8,128)(2,1)S(1)}, bf16[256,1024]{1,0:T(8,128)(2,1)S(1)}, u32[]{:S(2)}, u32[]{:S(2)}) collective-permute-start(bf16[256,1024]{1,0:T(8,128)(2,1)S(1)} %sum_pass.2.refs_12_), channel_id=1, source_target_pairs={{0,30},{2,28},{4,26},{6,24},{24,6},{26,4},{28,2},{30,0},{1,31},{3,... | collective-permute-start | bytes 1572872 | tf_op jit(solution)/shard_map/ppermute | solution.py:623
  28.6 46.7 %collective-permute-start.8 = (bf16[256,1024]{1,0:T(8,128)(2,1)S(1)}, bf16[256,1024]{1,0:T(8,128)(2,1)S(1)}, u32[]{:S(2)}, u32[]{:S(2)}) collective-permute-start(bf16[256,1024]{1,0:T(8,128)(2,1)S(1)} %sum_pass.2.refs_12_), channel_id=1, source_target_pairs={{8,22},{10,20},{12,18},{14,16},{16,14},{18,12},{20,10},{22,8},{9,2... | collective-permute-start | bytes 1572872 | tf_op jit(solution)/shard_map/ppermute | solution.py:623
  32.2 5.0 %copy-start.13 = (bf16[256,1024]{1,0:T(8,128)(2,1)S(1)}, bf16[256,1024]{1,0:T(8,128)(2,1)}, u32[]{:S(2)}) copy-start(bf16[256,1024]{1,0:T(8,128)(2,1)} %get-tuple-element.46.refs_0_) | copy-start | bytes 1572868
  32.2 5.0 %copy-start.14 = (bf16[256,768]{1,0:T(8,128)(2,1)S(1)}, bf16[256,768]{1,0:T(8,128)(2,1)}, u32[]{:S(2)}) copy-start(bf16[256,768]{1,0:T(8,128)(2,1)} %get-tuple-element.47.refs_1_) | copy-start | bytes 1179652
  32.2 6.9 %copy-start.3 = (bf16[1,2,256,1024]{3,2,1,0:T(8,128)(2,1)S(1)}, bf16[1,2,256,1024]{3,2,1,0:T(8,128)(2,1)}, u32[]{:S(2)}) copy-start(bf16[1,2,256,1024]{3,2,1,0:T(8,128)(2,1)} %param.14) | copy-start | bytes 3145732
  37.2 2.0 %copy-start.1 = (bf16[1,1024,768]{2,1,0:T(8,128)(2,1)S(1)}, bf16[1,1024,768]{2,1,0:T(8,128)(2,1)}, u32[]{:S(2)}) copy-start(bf16[1,1024,768]{2,1,0:T(8,128)(2,1)} %param.21) | copy-start | bytes 4718596
  37.2 2.0 %copy-start.19 = (f32[1,1024]{1,0:T(1,128)S(1)}, f32[1,1024]{1,0:T(1,128)}, u32[]{:S(2)}) copy-start(f32[1,1024]{1,0:T(1,128)} %refs_4_.7) | copy-start | bytes 12292
  38.5 3.3 %collective-permute-start.5 = (bf16[176,768]{1,0:T(8,128)(2,1)S(1)}, bf16[176,768]{1,0:T(8,128)(2,1)S(1)}, u32[]{:S(2)}, u32[]{:S(2)}) collective-permute-start(bf16[176,768]{1,0:T(8,128)(2,1)S(1)} %bitcast.61), channel_id=1, source_target_pairs={{0,1},{1,0},{2,3},{3,2},{4,5},{5,4},{6,7},{7,6},{8,9},{9,8},{10,11... | collective-permute-start | bytes 811016 | tf_op jit(solution)/shard_map/ppermute | solution.py:629
  38.5 3.2 %collective-permute-start.4 = (bf16[176,768]{1,0:T(8,128)(2,1)S(1)}, bf16[176,768]{1,0:T(8,128)(2,1)S(1)}, u32[]{:S(2)}, u32[]{:S(2)}) collective-permute-start(bf16[176,768]{1,0:T(8,128)(2,1)S(1)} %bitcast.60), channel_id=1, source_target_pairs={{0,1},{1,0},{2,3},{3,2},{4,5},{5,4},{6,7},{7,6},{8,9},{9,8},{10,11... | collective-permute-start | bytes 811016 | tf_op jit(solution)/shard_map/ppermute | solution.py:629
  39.0 2.8 %collective-permute-start.6 = (bf16[176,768]{1,0:T(8,128)(2,1)S(1)}, bf16[176,768]{1,0:T(8,128)(2,1)S(1)}, u32[]{:S(2)}, u32[]{:S(2)}) collective-permute-start(bf16[176,768]{1,0:T(8,128)(2,1)S(1)} %bitcast.59), channel_id=1, source_target_pairs={{0,1},{1,0},{2,3},{3,2},{4,5},{5,4},{6,7},{7,6},{8,9},{9,8},{10,11... | collective-permute-start | bytes 811016 | tf_op jit(solution)/shard_map/ppermute | solution.py:629
  41.7 33.6 %copy-start.5 = (bf16[1,512,1024]{2,1,0:T(8,128)(2,1)S(1)}, bf16[1,512,1024]{2,1,0:T(8,128)(2,1)}, u32[]{:S(2)}) copy-start(bf16[1,512,1024]{2,1,0:T(8,128)(2,1)} %param.22) | copy-start | bytes 3145732
  41.7 33.6 %copy-start.9 = (bf16[256,1024]{1,0:T(8,128)(2,1)S(1)}, bf16[256,1024]{1,0:T(8,128)(2,1)}, u32[]{:S(2)}) copy-start(bf16[256,1024]{1,0:T(8,128)(2,1)} %refs_5_.3) | copy-start | bytes 1572868
  41.8 33.6 %copy-start.10 = (bf16[256,1024]{1,0:T(8,128)(2,1)S(1)}, bf16[256,1024]{1,0:T(8,128)(2,1)}, u32[]{:S(2)}) copy-start(bf16[256,1024]{1,0:T(8,128)(2,1)} %get-tuple-element.60.refs_11_) | copy-start | bytes 1572868
  41.8 33.6 %copy-start.23 = (f32[1,1024]{1,0:T(1,128)S(1)}, f32[1,1024]{1,0:T(1,128)}, u32[]{:S(2)}) copy-start(f32[1,1024]{1,0:T(1,128)} %get-tuple-element.65.refs_9_) | copy-start | bytes 12292
  42.0 49.4 %collective-permute-start.11 = (bf16[512,768]{1,0:T(8,128)(2,1)S(1)}, bf16[512,768]{1,0:T(8,128)(2,1)S(1)}, u32[]{:S(2)}, u32[]{:S(2)}) collective-permute-start(bf16[512,768]{1,0:T(8,128)(2,1)S(1)} %get-tuple-element.70.refs_13_), channel_id=1, source_target_pairs={{0,30},{2,28},{4,26},{6,24},{8,22},{10,20},{12,18},{14,16},{16,14}... | collective-permute-start | bytes 2359304 | tf_op jit(solution)/shard_map/ppermute | solution.py:623
  75.3 4.1 %copy-start.8 = (bf16[1,256,1024]{2,1,0:T(8,128)(2,1)S(1)}, bf16[1,256,1024]{2,1,0:T(8,128)(2,1)}, u32[]{:S(2)}) copy-start(bf16[1,256,1024]{2,1,0:T(8,128)(2,1)} %param.16) | copy-start | bytes 1572868
  75.4 4.1 %copy-start.12 = (bf16[256,1024]{1,0:T(8,128)(2,1)S(1)}, bf16[256,1024]{1,0:T(8,128)(2,1)}, u32[]{:S(2)}) copy-start(bf16[256,1024]{1,0:T(8,128)(2,1)} %get-tuple-element.72.refs_0_) | copy-start | bytes 1572868
  75.4 4.1 %copy-start.15 = (bf16[256,768]{1,0:T(8,128)(2,1)S(1)}, bf16[256,768]{1,0:T(8,128)(2,1)}, u32[]{:S(2)}) copy-start(bf16[256,768]{1,0:T(8,128)(2,1)} %get-tuple-element.73.refs_1_) | copy-start | bytes 1179652
  75.4 4.1 %copy-start.16 = (bf16[256,512]{1,0:T(8,128)(2,1)S(1)}, bf16[256,512]{1,0:T(8,128)(2,1)}, u32[]{:S(2)}) copy-start(bf16[256,512]{1,0:T(8,128)(2,1)} %get-tuple-element.74.refs_2_) | copy-start | bytes 786436
  81.5 2.2 %collective-permute-start.9 = (bf16[1296,256]{1,0:T(8,128)(2,1)S(1)}, bf16[1296,256]{1,0:T(8,128)(2,1)S(1)}, u32[]{:S(2)}, u32[]{:S(2)}) collective-permute-start(bf16[1296,256]{1,0:T(8,128)(2,1)S(1)} %bitcast.58), channel_id=1, source_target_pairs={{0,1},{1,0},{2,3},{3,2},{4,5},{5,4},{6,7},{7,6},{8,9},{9,8},{10,11... | collective-permute-start | bytes 1990664 | tf_op jit(solution)/shard_map/ppermute | solution.py:629
  81.6 3.0 %collective-permute-start.10 = (bf16[1296,256]{1,0:T(8,128)(2,1)S(1)}, bf16[1296,256]{1,0:T(8,128)(2,1)S(1)}, u32[]{:S(2)}, u32[]{:S(2)}) collective-permute-start(bf16[1296,256]{1,0:T(8,128)(2,1)S(1)} %bitcast.57), channel_id=1, source_target_pairs={{0,1},{1,0},{2,3},{3,2},{4,5},{5,4},{6,7},{7,6},{8,9},{9,8},{10,11... | collective-permute-start | bytes 1990664 | tf_op jit(solution)/shard_map/ppermute | solution.py:629
  82.1 9.4 %collective-permute-start.12 = (bf16[16,128]{1,0:T(8,128)(2,1)S(1)}, bf16[16,128]{1,0:T(8,128)(2,1)S(1)}, u32[]{:S(2)}, u32[]{:S(2)}) collective-permute-start(bf16[16,128]{1,0:T(8,128)(2,1)S(1)} %get-tuple-element.84), channel_id=1, source_target_pairs={{0,30},{2,28},{4,26},{6,24},{8,22},{10,20},{12,18},{14,16},{16,14}... | collective-permute-start | bytes 12296 | tf_op jit(solution)/shard_map/ppermute | solution.py:623

commit v5 on v4

--- a/solution.py
+++ b/solution.py
@@ -654,15 +654,15 @@
     up_forward = forward_pass(1, ints, act_up[0], gain_up, qkv_up[0], query_width)
     sends, keep = outproj_pass(1, up_one[2], up_forward[2], grad_up[0], up_moved, seed_up, parts)
     (up_out,) = sum_pass(keep, exchanged(sends, "dp"))
-    outer_out = mirrored(up_out, "section", outer)
-    inner_out = mirrored(up_out, "section", inner)
+    outer_out = mirrored(up_out, "section", range(edge))
+    inner_out = mirrored(up_out, "section", range(edge, sections))
     up_two = backward_pass(
         1, slot_order, act_up[0], *up, seed_up, up_forward, up_one[4], up_moved, up_one[0], after=(up_out,)
     )
     sends, keep = qkv_pass(up_one[1], up_one[3], up_forward[0], up_two[1], up_two[2], parts, after=(down_moved,))
     down_forward = forward_pass(0, ints, act_down[0], gain_down, qkv_down[0], query_width, after=(keep,))
     up_qkv, up_gains = sum_pass(
-        keep, exchanged(sends, "dp"), model // parts, after=(outer_out, down_forward[2])
+        keep, exchanged(sends, "dp"), model // parts, after=(outer_out,)
     )
     mirror_gains = mirrored(up_gains, "section")
     mirror_qkv = mirrored(up_qkv, "section")

time: 93.3 us -> 93.2 us (level)
  waiting for transfers between devices: 39.4 us -> 36.8 us
  starting transfers between devices: 17.6 us -> 20.2 us
    ppermute x4, waiting for transfers between devices: 36.6 us -> 32.3 us  [mirrored(): lax.ppermute(value, axis, [(i, count - 1 - i) for i in (range(count) if s...]
    ppermute x4, starting transfers between devices: 8.09 us -> 10.7 us  [mirrored(): lax.ppermute(value, axis, [(i, count - 1 - i) for i in (range(count) if s...]
    ppermute x7, waiting for transfers between devices: 2.35 us -> 4.07 us  [exchanged(): lax.ppermute(send[k], axis, [(i, (i + 1 + k) % parts) for i in range(part...]
  transfers between devices with their start and end apart: 13 -> 13, of which waited for: 6 -> 9; matrix products, arithmetic and copies ran while one was open for 0% -> 0% of each run, Pallas kernels for 29% -> 29%
where the time goes in v5:
time: 93.2 us; the launch traced here: 92.9 us
  waiting for transfers between devices  36.8 us (39%)
  Pallas kernels  34.4 us (37%)
  starting transfers between devices  20.2 us (22%)
  between operations  1.26 us (1%)
    pallas_call x13, Pallas kernels, call(): pl.pallas_call(ordered, out_shape=tuple((jax.ShapeDtypeStruct(shape, dtyp...  34.4 us
    ppermute x4, waiting for transfers between devices, mirrored(): lax.ppermute(value, axis, [(i, count - 1 - i) for i in (range(count) if s...  32.3 us
    ppermute x4, starting transfers between devices, mirrored(): lax.ppermute(value, axis, [(i, count - 1 - i) for i in (range(count) if s...  10.7 us
    ppermute x2, starting transfers between devices, shifted(): lax.ppermute(value, axis, [(source, source + steps) for source in range(f...  7.77 us
    ppermute x7, waiting for transfers between devices, exchanged(): lax.ppermute(send[k], axis, [(i, (i + 1 + k) % parts) for i in range(part...  4.07 us
  transfers between devices with their start and end apart: 13, of which 9 were waited for; matrix products, arithmetic and copies ran while one was open for 0% of the time, Pallas kernels for 29%

profile of v5, /device:TPU:16, one launch (start us, length us, event | category | flops | bytes accessed | tf_op | source)
XLA Modules:
  0.0 92.9 jit_solution(16843115430883372813)
XLA Ops:
  0.6 6.5 %first_pass.2 = (bf16[256,1024]{1,0:T(8,128)(2,1)}, bf16[256,1024]{1,0:T(8,128)(2,1)}, bf16[256,512]{1,0:T(8,128)(2,1)}, bf16[256,768]{1,0:T(8,128)(2,1)}, f32[1,1024]{1,0:T(1,128)}) custom-call(s32[2,1,2]{2,1,0:T(1,128)} %refs_0_.11, s32[2,1,2]{2,1,0:T(1,128)} %bitcast.53, bf16[2,256,1024]{2,1,0:T(8,128)(2,1)} %bitcast.34, bf16[1024,768]{1,0:T(8,128)(2,1)} %bitcast.28, ...), custom_call_target="tpu_custom_call" | custom-call | flops 1 | bytes 1 | tf_op jit(solution)/shard_map/first_pass/pallas_call | solution.py:155
  7.2 3.4 %collective-permute-start = (bf16[256,1024]{1,0:T(8,128)(2,1)}, bf16[256,1024]{1,0:T(8,128)(2,1)S(1)}, u32[]{:S(2)}, u32[]{:S(2)}) collective-permute-start(bf16[256,1024]{1,0:T(8,128)(2,1)} %get-tuple-element.53.refs_11_), channel_id=1, source_target_pairs={{0,2},{2,4},{4,6},{6,8},{8,10},{10,12},{12,14},{14,16},{16,18},{18... | collective-permute-start | bytes 1572872 | tf_op jit(solution)/shard_map/ppermute | solution.py:618
  10.6 0.0 copy-start
  10.6 0.0 copy-start.2
  10.6 0.0 copy-start.18
  10.6 0.0 copy-start.20
  10.6 0.0 copy-start.22
  10.6 6.7 %first_pass.3 = (bf16[256,1024]{1,0:T(8,128)(2,1)}, bf16[256,1024]{1,0:T(8,128)(2,1)}, bf16[256,512]{1,0:T(8,128)(2,1)}, bf16[256,768]{1,0:T(8,128)(2,1)}, f32[1,1024]{1,0:T(1,128)}) custom-call(s32[2,1,2]{2,1,0:T(1,128)} %refs_0_.11, s32[2,1,2]{2,1,0:T(1,128)} %bitcast.54, bf16[2,256,1024]{2,1,0:T(8,128)(2,1)} %bitcast.37, bf16[1024,768]{1,0:T(8,128)(2,1)} %bitcast.31, ...), custom_call_target="tpu_custom_call" | custom-call | flops 1 | bytes 1 | tf_op jit(solution)/shard_map/first_pass/pallas_call | solution.py:155
  17.3 0.0 copy-start.6
  17.4 0.0 copy-start.7
  17.4 0.0 copy-start.17
  17.4 4.4 %collective-permute-start.3 = (bf16[256,1024]{1,0:T(8,128)(2,1)}, bf16[256,1024]{1,0:T(8,128)(2,1)S(1)}, u32[]{:S(2)}, u32[]{:S(2)}) collective-permute-start(bf16[256,1024]{1,0:T(8,128)(2,1)} %get-tuple-element.60.refs_11_), channel_id=1, source_target_pairs={{2,0},{4,2},{6,4},{8,6},{10,8},{12,10},{14,12},{16,14},{18,16},{20... | collective-permute-start | bytes 1572872 | tf_op jit(solution)/shard_map/ppermute | solution.py:618
  21.8 2.6 %forward_pass.2 = (bf16[256,1024]{1,0:T(8,128)(2,1)S(1)}, bf16[256,768]{1,0:T(8,128)(2,1)S(1)}, bf16[256,512]{1,0:T(8,128)(2,1)S(1)}, bf16[4,256,512]{2,1,0:T(8,128)(2,1)S(1)}) custom-call(s32[2,1,2]{2,1,0:T(1,128)S(1)} %copy-done.20, s32[2,1,2]{2,1,0:T(1,128)S(1)} %bitcast.55, bf16[2,256,1024]{2,1,0:T(8,128)(2,1)S(1)} %bitcast.35, ...), custom_call_target="tpu_custom_call" | custom-call | flops 1 | bytes 1 | tf_op jit(solution)/shard_map/forward_pass/pallas_call | solution.py:155
  24.4 0.4 collective-permute-done.refs_4_.refs_10_
  24.9 0.0 copy-start.4
  24.9 0.0 copy-start.11
  24.9 0.9 %outproj_pass.1 = (bf16[1,128,1024]{2,1,0:T(8,128)(2,1)S(1)}, bf16[1,128,1024]{2,1,0:T(8,128)(2,1)S(1)}, bf16[256,1024]{1,0:T(8,128)(2,1)S(1)}) custom-call(bf16[256,1024]{1,0:T(8,128)(2,1)S(1)} %bitcast.45, bf16[256,1024]{1,0:T(8,128)(2,1)S(1)} %copy-done.7, bf16[256,512]{1,0:T(8,128)(2,1)S(1)} %copy-done.17, ...), custom_call_target="tpu_custom_call" | custom-call | flops 1 | bytes 1 | tf_op jit(solution)/shard_map/outproj_pass/pallas_call | solution.py:155
  25.8 0.1 collective-permute-start.1
  25.9 0.5 collective-permute-start.2
  26.4 1.0 %collective-permute-done.1 = bf16[128,1024]{1,0:T(8,128)(2,1)S(1)} collective-permute-done((bf16[128,1024]{1,0:T(8,128)(2,1)S(1)}, bf16[128,1024]{1,0:T(8,128)(2,1)S(1)}, u32[]{:S(2)}, u32[]{:S(2)}) %collective-permute-start.1) | collective-permute-done | bytes 262176 | tf_op jit(solution)/shard_map/ppermute | solution.py:629
  27.4 0.4 collective-permute-done.2
  27.8 0.1 sum_pass.2.refs_12_
  27.9 0.7 collective-permute-start.7
  28.6 3.5 %collective-permute-start.8 = (bf16[256,1024]{1,0:T(8,128)(2,1)S(1)}, bf16[256,1024]{1,0:T(8,128)(2,1)S(1)}, u32[]{:S(2)}, u32[]{:S(2)}) collective-permute-start(bf16[256,1024]{1,0:T(8,128)(2,1)S(1)} %sum_pass.2.refs_12_), channel_id=1, source_target_pairs={{8,22},{10,20},{12,18},{14,16},{16,14},{18,12},{20,10},{22,8},{24,... | collective-permute-start | bytes 1572872 | tf_op jit(solution)/shard_map/ppermute | solution.py:623
  32.2 0.0 copy-start.13
  32.2 5.0 %backward_pass.2 = (bf16[256,1024]{1,0:T(8,128)(2,1)}, bf16[256,768]{1,0:T(8,128)(2,1)S(1)}, f32[1,1024]{1,0:T(1,128)S(1)}, bf16[2,2,256,1024]{3,2,1,0:T(8,128)(2,1)}) custom-call(s32[2,1,2]{2,1,0:T(1,128)S(1)} %copy-done.20, bf16[2,256,1024]{2,1,0:T(8,128)(2,1)S(1)} %bitcast.36, bf16[1024,768]{1,0:T(8,128)(2,1)S(1)} %bitcast.30, ...), custom_call_target="tpu_custom_call" | custom-call | flops 1 | bytes 1 | tf_op jit(solution)/shard_map/backward_pass/pallas_call | solution.py:155
  37.2 1.3 %qkv_pass.1 = (bf16[1,176,768]{2,1,0:T(8,128)(2,1)S(1)}, bf16[1,176,768]{2,1,0:T(8,128)(2,1)S(1)}, bf16[1,176,768]{2,1,0:T(8,128)(2,1)S(1)}, bf16[528,768]{1,0:T(8,128)(2,1)S(1)}) custom-call(bf16[256,1024]{1,0:T(8,128)(2,1)S(1)} %copy-done.13, bf16[256,768]{1,0:T(8,128)(2,1)S(1)} %copy-done.14, bf16[256,1024]{1,0:T(8,128)(2,1)S(1)} %get-tuple-element.48.refs_2_, ...), custom_call_target="tpu_custom_call" | custom-call | flops 1 | bytes 1 | tf_op jit(solution)/shard_map/qkv_pass/pallas_call | solution.py:155
  38.5 0.0 copy-start.19
  38.5 0.1 collective-permute-start.4
  38.6 0.5 collective-permute-start.5
  39.1 0.1 collective-permute-start.6
  39.2 1.0 %collective-permute-done.4 = bf16[176,768]{1,0:T(8,128)(2,1)S(1)} collective-permute-done((bf16[176,768]{1,0:T(8,128)(2,1)S(1)}, bf16[176,768]{1,0:T(8,128)(2,1)S(1)}, u32[]{:S(2)}, u32[]{:S(2)}) %collective-permute-start.4) | collective-permute-done | bytes 270368 | tf_op jit(solution)/shard_map/ppermute | solution.py:629
  40.1 0.4 collective-permute-done.5
  40.5 0.4 collective-permute-done.6
  40.9 0.2 sum_pass.3
  41.1 4.9 %collective-permute-start.11 = (bf16[512,768]{1,0:T(8,128)(2,1)S(1)}, bf16[512,768]{1,0:T(8,128)(2,1)S(1)}, u32[]{:S(2)}, u32[]{:S(2)}) collective-permute-start(bf16[512,768]{1,0:T(8,128)(2,1)S(1)} %get-tuple-element.70.refs_13_), channel_id=1, source_target_pairs={{0,30},{2,28},{4,26},{6,24},{8,22},{10,20},{12,18},{14,16},{16,14}... | collective-permute-start | bytes 2359304 | tf_op jit(solution)/shard_map/ppermute | solution.py:623
  46.1 2.6 %forward_pass.3 = (bf16[256,1024]{1,0:T(8,128)(2,1)S(1)}, bf16[256,768]{1,0:T(8,128)(2,1)S(1)}, bf16[256,512]{1,0:T(8,128)(2,1)S(1)}, bf16[4,256,512]{2,1,0:T(8,128)(2,1)S(1)}) custom-call(s32[2,1,2]{2,1,0:T(1,128)S(1)} %copy-done.20, s32[2,1,2]{2,1,0:T(1,128)S(1)} %bitcast.56, bf16[2,256,1024]{2,1,0:T(8,128)(2,1)S(1)} %bitcast.38, ...), custom_call_target="tpu_custom_call" | custom-call | flops 1 | bytes 1 | tf_op jit(solution)/shard_map/forward_pass/pallas_call | solution.py:155
  48.7 26.7 %collective-permute-done.8.refs_14_.refs_2_ = bf16[256,1024]{1,0:T(8,128)(2,1)S(1)} collective-permute-done((bf16[256,1024]{1,0:T(8,128)(2,1)S(1)}, bf16[256,1024]{1,0:T(8,128)(2,1)S(1)}, u32[]{:S(2)}, u32[]{:S(2)}) %collective-permute-start.8) | collective-permute-done | bytes 524320 | tf_op jit(solution)/shard_map/ppermute | solution.py:623
  75.3 0.0 copy-start.8
  75.4 4.0 %backward_pass.3 = (bf16[256,1024]{1,0:T(8,128)(2,1)S(1)}, bf16[256,768]{1,0:T(8,128)(2,1)S(1)}, f32[1,1024]{1,0:T(1,128)S(1)}, bf16[2,2,256,1024]{3,2,1,0:T(8,128)(2,1)}) custom-call(s32[2,1,2]{2,1,0:T(1,128)S(1)} %copy-done.20, bf16[2,256,1024]{2,1,0:T(8,128)(2,1)S(1)} %bitcast.39, ...), custom_call_target="tpu_custom_call", output_to_operand_aliasing={{3}: (12, {})} | custom-call | flops 1 | bytes 1 | tf_op jit(solution)/shard_map/backward_pass/pallas_call | solution.py:155
  79.5 2.1 %packed_pass.1 = (bf16[1,1296,256]{2,1,0:T(8,128)(2,1)S(1)}, bf16[1,1296,256]{2,1,0:T(8,128)(2,1)S(1)}, bf16[2592,256]{1,0:T(8,128)(2,1)S(1)}) custom-call(bf16[256,1024]{1,0:T(8,128)(2,1)S(1)} %copy-done.12, bf16[256,768]{1,0:T(8,128)(2,1)S(1)} %copy-done.15, bf16[256,512]{1,0:T(8,128)(2,1)S(1)} %copy-done.16, bf16[256,1024]{1,0:T(8,128)(2,1)S(1)} %bitcast.47, ...), custom_call_target="tpu_custom_call" | custom-call | flops 1 | bytes 1 | tf_op jit(solution)/shard_map/packed_pass/pallas_call | solution.py:155
  81.5 0.1 collective-permute-start.10
  81.6 0.5 collective-permute-start.9
  82.1 1.6 %collective-permute-start.12 = (bf16[16,128]{1,0:T(8,128)(2,1)S(1)}, bf16[16,128]{1,0:T(8,128)(2,1)S(1)}, u32[]{:S(2)}, u32[]{:S(2)}) collective-permute-start(bf16[16,128]{1,0:T(8,128)(2,1)S(1)} %get-tuple-element.84), channel_id=1, source_target_pairs={{0,30},{2,28},{4,26},{6,24},{8,22},{10,20},{12,18},{14,16},{16,14}... | collective-permute-start | bytes 12296 | tf_op jit(solution)/shard_map/ppermute | solution.py:623
  83.7 0.9 %collective-permute-done.9.refs_3_ = bf16[1296,256]{1,0:T(8,128)(2,1)S(1)} collective-permute-done((bf16[1296,256]{1,0:T(8,128)(2,1)S(1)}, bf16[1296,256]{1,0:T(8,128)(2,1)S(1)}, u32[]{:S(2)}, u32[]{:S(2)}) %collective-permute-start.9) | collective-permute-done | bytes 663584 | tf_op jit(solution)/shard_map/ppermute | solution.py:629
  84.6 1.2 %own_pass.1 = (f32[256,1024]{1,0:T(8,128)}, f32[512,768]{1,0:T(8,128)S(1)}, f32[1,512]{1,0:T(1,128)S(1)}) custom-call(bf16[2592,256]{1,0:T(8,128)(2,1)S(1)} %get-tuple-element.79.refs_0_, bf16[256,1024]{1,0:T(8,128)(2,1)S(1)} %collective-permute-done.7.refs_4_.refs_1_, bf16[256,1024]{1,0:T(8,128)(2,1)S(1)} %collective-permute-done.8.refs_14_.refs_2_, ...), custom_call_target="tpu_custom_call" | custom-call | flops 1 | bytes 1 | tf_op jit(solution)/shard_map/own_pass/pallas_call | solution.py:155
  85.8 5.6 %collective-permute-done.12.refs_3_ = bf16[16,128]{1,0:T(8,128)(2,1)S(1)} collective-permute-done((bf16[16,128]{1,0:T(8,128)(2,1)S(1)}, bf16[16,128]{1,0:T(8,128)(2,1)S(1)}, u32[]{:S(2)}, u32[]{:S(2)}) %collective-permute-start.12) | collective-permute-done | bytes 4128 | tf_op jit(solution)/shard_map/ppermute | solution.py:623
  91.5 1.2 %final_pass.1 = (f32[1,512]{1,0:T(1,128)}, f32[512,768]{1,0:T(8,128)}) custom-call(f32[512,768]{1,0:T(8,128)S(1)} %get-tuple-element.82.refs_0_, f32[1,512]{1,0:T(1,128)S(1)} %get-tuple-element.83.refs_1_, bf16[512,768]{1,0:T(8,128)(2,1)S(1)} %collective-permute-done.11.refs_2_, bf16[16,128]{1,0:T(8,128)(2,1)S(1)} %collective-permute-done.12.refs_3_), custom_call_target="tpu_custom_call" | custom-call | flops 1 | bytes 1 | tf_op jit(solution)/shard_map/final_pass/pallas_call | solution.py:155
  (39 shorter events, 0.1 us)
Async XLA Ops:
  7.2 17.7 %collective-permute-start = (bf16[256,1024]{1,0:T(8,128)(2,1)}, bf16[256,1024]{1,0:T(8,128)(2,1)S(1)}, u32[]{:S(2)}, u32[]{:S(2)}) collective-permute-start(bf16[256,1024]{1,0:T(8,128)(2,1)} %get-tuple-element.53.refs_11_), channel_id=1, source_target_pairs={{0,2},{2,4},{4,6},{6,8},{8,10},{10,12},{12,14},{14,16},{16,18},{18... | collective-permute-start | bytes 1572872 | tf_op jit(solution)/shard_map/ppermute | solution.py:618
  10.6 11.2 %copy-start = (bf16[1,1024,768]{2,1,0:T(8,128)(2,1)S(1)}, bf16[1,1024,768]{2,1,0:T(8,128)(2,1)}, u32[]{:S(2)}) copy-start(bf16[1,1024,768]{2,1,0:T(8,128)(2,1)} %param.24) | copy-start | bytes 4718596
  10.6 11.2 %copy-start.2 = (bf16[1,2,256,1024]{3,2,1,0:T(8,128)(2,1)S(1)}, bf16[1,2,256,1024]{3,2,1,0:T(8,128)(2,1)}, u32[]{:S(2)}) copy-start(bf16[1,2,256,1024]{3,2,1,0:T(8,128)(2,1)} %param.15) | copy-start | bytes 3145732
  10.6 11.2 %copy-start.18 = (f32[1,1024]{1,0:T(1,128)S(1)}, f32[1,1024]{1,0:T(1,128)}, u32[]{:S(2)}) copy-start(f32[1,1024]{1,0:T(1,128)} %refs_4_.5) | copy-start | bytes 12292
  10.6 11.2 %copy-start.20 = (s32[2,1,2]{2,1,0:T(1,128)S(1)}, s32[2,1,2]{2,1,0:T(1,128)}, u32[]{:S(2)}) copy-start(s32[2,1,2]{2,1,0:T(1,128)} %refs_0_.11) | copy-start | bytes 52
  10.6 11.2 %copy-start.22 = (s32[2,1,2,1]{2,3,1,0:T(1,128)S(1)}, s32[2,1,2,1]{2,3,1,0:T(1,128)}, u32[]{:S(2)}) copy-start(s32[2,1,2,1]{2,3,1,0:T(1,128)} %param.26) | copy-start | bytes 52
  17.3 7.5 %copy-start.6 = (bf16[1,256,1024]{2,1,0:T(8,128)(2,1)S(1)}, bf16[1,256,1024]{2,1,0:T(8,128)(2,1)}, u32[]{:S(2)}) copy-start(bf16[1,256,1024]{2,1,0:T(8,128)(2,1)} %param.17) | copy-start | bytes 1572868
  17.4 7.5 %copy-start.7 = (bf16[256,1024]{1,0:T(8,128)(2,1)S(1)}, bf16[256,1024]{1,0:T(8,128)(2,1)}, u32[]{:S(2)}) copy-start(bf16[256,1024]{1,0:T(8,128)(2,1)} %refs_5_.2) | copy-start | bytes 1572868
  17.4 7.5 %copy-start.17 = (bf16[256,512]{1,0:T(8,128)(2,1)S(1)}, bf16[256,512]{1,0:T(8,128)(2,1)}, u32[]{:S(2)}) copy-start(bf16[256,512]{1,0:T(8,128)(2,1)} %get-tuple-element.54.refs_2_) | copy-start | bytes 786436
  17.4 19.8 %collective-permute-start.3 = (bf16[256,1024]{1,0:T(8,128)(2,1)}, bf16[256,1024]{1,0:T(8,128)(2,1)S(1)}, u32[]{:S(2)}, u32[]{:S(2)}) collective-permute-start(bf16[256,1024]{1,0:T(8,128)(2,1)} %get-tuple-element.60.refs_11_), channel_id=1, source_target_pairs={{2,0},{4,2},{6,4},{8,6},{10,8},{12,10},{14,12},{16,14},{18,16},{20... | collective-permute-start | bytes 1572872 | tf_op jit(solution)/shard_map/ppermute | solution.py:618
  24.9 7.3 %copy-start.4 = (bf16[1,512,1024]{2,1,0:T(8,128)(2,1)S(1)}, bf16[1,512,1024]{2,1,0:T(8,128)(2,1)}, u32[]{:S(2)}) copy-start(bf16[1,512,1024]{2,1,0:T(8,128)(2,1)} %param.25) | copy-start | bytes 3145732
  24.9 7.3 %copy-start.11 = (bf16[256,1024]{1,0:T(8,128)(2,1)S(1)}, bf16[256,1024]{1,0:T(8,128)(2,1)}, u32[]{:S(2)}) copy-start(bf16[256,1024]{1,0:T(8,128)(2,1)} %get-tuple-element.53.refs_11_) | copy-start | bytes 1572868
  24.9 7.3 %copy-start.21 = (f32[1,1024]{1,0:T(1,128)S(1)}, f32[1,1024]{1,0:T(1,128)}, u32[]{:S(2)}) copy-start(f32[1,1024]{1,0:T(1,128)} %get-tuple-element.52.refs_9_.refs_7_) | copy-start | bytes 12292
  25.8 1.6 %collective-permute-start.1 = (bf16[128,1024]{1,0:T(8,128)(2,1)S(1)}, bf16[128,1024]{1,0:T(8,128)(2,1)S(1)}, u32[]{:S(2)}, u32[]{:S(2)}) collective-permute-start(bf16[128,1024]{1,0:T(8,128)(2,1)S(1)} %bitcast.63), channel_id=1, source_target_pairs={{0,1},{1,0},{2,3},{3,2},{4,5},{5,4},{6,7},{7,6},{8,9},{9,8},{10,11... | collective-permute-start | bytes 786440 | tf_op jit(solution)/shard_map/ppermute | solution.py:629
  25.9 1.9 %collective-permute-start.2 = (bf16[128,1024]{1,0:T(8,128)(2,1)S(1)}, bf16[128,1024]{1,0:T(8,128)(2,1)S(1)}, u32[]{:S(2)}, u32[]{:S(2)}) collective-permute-start(bf16[128,1024]{1,0:T(8,128)(2,1)S(1)} %bitcast.62), channel_id=1, source_target_pairs={{0,1},{1,0},{2,3},{3,2},{4,5},{5,4},{6,7},{7,6},{8,9},{9,8},{10,11... | collective-permute-start | bytes 786440 | tf_op jit(solution)/shard_map/ppermute | solution.py:629
  27.9 13.0 %collective-permute-start.7 = (bf16[256,1024]{1,0:T(8,128)(2,1)S(1)}, bf16[256,1024]{1,0:T(8,128)(2,1)S(1)}, u32[]{:S(2)}, u32[]{:S(2)}) collective-permute-start(bf16[256,1024]{1,0:T(8,128)(2,1)S(1)} %sum_pass.2.refs_12_), channel_id=1, source_target_pairs={{0,30},{2,28},{4,26},{6,24},{1,31},{3,29},{5,27},{7,25}} | collective-permute-start | bytes 1572872 | tf_op jit(solution)/shard_map/ppermute | solution.py:623
  28.6 46.7 %collective-permute-start.8 = (bf16[256,1024]{1,0:T(8,128)(2,1)S(1)}, bf16[256,1024]{1,0:T(8,128)(2,1)S(1)}, u32[]{:S(2)}, u32[]{:S(2)}) collective-permute-start(bf16[256,1024]{1,0:T(8,128)(2,1)S(1)} %sum_pass.2.refs_12_), channel_id=1, source_target_pairs={{8,22},{10,20},{12,18},{14,16},{16,14},{18,12},{20,10},{22,8},{24,... | collective-permute-start | bytes 1572872 | tf_op jit(solution)/shard_map/ppermute | solution.py:623
  32.2 5.0 %copy-start.13 = (bf16[256,1024]{1,0:T(8,128)(2,1)S(1)}, bf16[256,1024]{1,0:T(8,128)(2,1)}, u32[]{:S(2)}) copy-start(bf16[256,1024]{1,0:T(8,128)(2,1)} %get-tuple-element.46.refs_0_) | copy-start | bytes 1572868
  32.2 5.0 %copy-start.14 = (bf16[256,768]{1,0:T(8,128)(2,1)S(1)}, bf16[256,768]{1,0:T(8,128)(2,1)}, u32[]{:S(2)}) copy-start(bf16[256,768]{1,0:T(8,128)(2,1)} %get-tuple-element.47.refs_1_) | copy-start | bytes 1179652
  37.2 8.8 %copy-start.3 = (bf16[1,2,256,1024]{3,2,1,0:T(8,128)(2,1)S(1)}, bf16[1,2,256,1024]{3,2,1,0:T(8,128)(2,1)}, u32[]{:S(2)}) copy-start(bf16[1,2,256,1024]{3,2,1,0:T(8,128)(2,1)} %param.14) | copy-start | bytes 3145732
  38.5 7.6 %copy-start.1 = (bf16[1,1024,768]{2,1,0:T(8,128)(2,1)S(1)}, bf16[1,1024,768]{2,1,0:T(8,128)(2,1)}, u32[]{:S(2)}) copy-start(bf16[1,1024,768]{2,1,0:T(8,128)(2,1)} %param.21) | copy-start | bytes 4718596
  38.5 7.5 %copy-start.19 = (f32[1,1024]{1,0:T(1,128)S(1)}, f32[1,1024]{1,0:T(1,128)}, u32[]{:S(2)}) copy-start(f32[1,1024]{1,0:T(1,128)} %refs_4_.7) | copy-start | bytes 12292
  38.5 1.6 %collective-permute-start.4 = (bf16[176,768]{1,0:T(8,128)(2,1)S(1)}, bf16[176,768]{1,0:T(8,128)(2,1)S(1)}, u32[]{:S(2)}, u32[]{:S(2)}) collective-permute-start(bf16[176,768]{1,0:T(8,128)(2,1)S(1)} %bitcast.61), channel_id=1, source_target_pairs={{0,1},{1,0},{2,3},{3,2},{4,5},{5,4},{6,7},{7,6},{8,9},{9,8},{10,11... | collective-permute-start | bytes 811016 | tf_op jit(solution)/shard_map/ppermute | solution.py:629
  38.6 1.9 %collective-permute-start.5 = (bf16[176,768]{1,0:T(8,128)(2,1)S(1)}, bf16[176,768]{1,0:T(8,128)(2,1)S(1)}, u32[]{:S(2)}, u32[]{:S(2)}) collective-permute-start(bf16[176,768]{1,0:T(8,128)(2,1)S(1)} %bitcast.60), channel_id=1, source_target_pairs={{0,1},{1,0},{2,3},{3,2},{4,5},{5,4},{6,7},{7,6},{8,9},{9,8},{10,11... | collective-permute-start | bytes 811016 | tf_op jit(solution)/shard_map/ppermute | solution.py:629
  39.1 1.8 %collective-permute-start.6 = (bf16[176,768]{1,0:T(8,128)(2,1)S(1)}, bf16[176,768]{1,0:T(8,128)(2,1)S(1)}, u32[]{:S(2)}, u32[]{:S(2)}) collective-permute-start(bf16[176,768]{1,0:T(8,128)(2,1)S(1)} %bitcast.59), channel_id=1, source_target_pairs={{0,1},{1,0},{2,3},{3,2},{4,5},{5,4},{6,7},{7,6},{8,9},{9,8},{10,11... | collective-permute-start | bytes 811016 | tf_op jit(solution)/shard_map/ppermute | solution.py:629
  41.1 34.2 %copy-start.5 = (bf16[1,512,1024]{2,1,0:T(8,128)(2,1)S(1)}, bf16[1,512,1024]{2,1,0:T(8,128)(2,1)}, u32[]{:S(2)}) copy-start(bf16[1,512,1024]{2,1,0:T(8,128)(2,1)} %param.22) | copy-start | bytes 3145732
  41.1 34.2 %copy-start.9 = (bf16[256,1024]{1,0:T(8,128)(2,1)S(1)}, bf16[256,1024]{1,0:T(8,128)(2,1)}, u32[]{:S(2)}) copy-start(bf16[256,1024]{1,0:T(8,128)(2,1)} %refs_5_.3) | copy-start | bytes 1572868
  41.1 34.2 %copy-start.10 = (bf16[256,1024]{1,0:T(8,128)(2,1)S(1)}, bf16[256,1024]{1,0:T(8,128)(2,1)}, u32[]{:S(2)}) copy-start(bf16[256,1024]{1,0:T(8,128)(2,1)} %get-tuple-element.60.refs_11_) | copy-start | bytes 1572868
  41.1 34.2 %copy-start.23 = (f32[1,1024]{1,0:T(1,128)S(1)}, f32[1,1024]{1,0:T(1,128)}, u32[]{:S(2)}) copy-start(f32[1,1024]{1,0:T(1,128)} %get-tuple-element.65.refs_9_) | copy-start | bytes 12292
  41.1 50.3 %collective-permute-start.11 = (bf16[512,768]{1,0:T(8,128)(2,1)S(1)}, bf16[512,768]{1,0:T(8,128)(2,1)S(1)}, u32[]{:S(2)}, u32[]{:S(2)}) collective-permute-start(bf16[512,768]{1,0:T(8,128)(2,1)S(1)} %get-tuple-element.70.refs_13_), channel_id=1, source_target_pairs={{0,30},{2,28},{4,26},{6,24},{8,22},{10,20},{12,18},{14,16},{16,14}... | collective-permute-start | bytes 2359304 | tf_op jit(solution)/shard_map/ppermute | solution.py:623
  75.3 4.1 %copy-start.8 = (bf16[1,256,1024]{2,1,0:T(8,128)(2,1)S(1)}, bf16[1,256,1024]{2,1,0:T(8,128)(2,1)}, u32[]{:S(2)}) copy-start(bf16[1,256,1024]{2,1,0:T(8,128)(2,1)} %param.16) | copy-start | bytes 1572868
  75.4 4.1 %copy-start.12 = (bf16[256,1024]{1,0:T(8,128)(2,1)S(1)}, bf16[256,1024]{1,0:T(8,128)(2,1)}, u32[]{:S(2)}) copy-start(bf16[256,1024]{1,0:T(8,128)(2,1)} %get-tuple-element.72.refs_0_) | copy-start | bytes 1572868
  75.4 4.1 %copy-start.15 = (bf16[256,768]{1,0:T(8,128)(2,1)S(1)}, bf16[256,768]{1,0:T(8,128)(2,1)}, u32[]{:S(2)}) copy-start(bf16[256,768]{1,0:T(8,128)(2,1)} %get-tuple-element.73.refs_1_) | copy-start | bytes 1179652
  75.4 4.1 %copy-start.16 = (bf16[256,512]{1,0:T(8,128)(2,1)S(1)}, bf16[256,512]{1,0:T(8,128)(2,1)}, u32[]{:S(2)}) copy-start(bf16[256,512]{1,0:T(8,128)(2,1)} %get-tuple-element.74.refs_2_) | copy-start | bytes 786436
  81.5 2.2 %collective-permute-start.10 = (bf16[1296,256]{1,0:T(8,128)(2,1)S(1)}, bf16[1296,256]{1,0:T(8,128)(2,1)S(1)}, u32[]{:S(2)}, u32[]{:S(2)}) collective-permute-start(bf16[1296,256]{1,0:T(8,128)(2,1)S(1)} %bitcast.58), channel_id=1, source_target_pairs={{0,1},{1,0},{2,3},{3,2},{4,5},{5,4},{6,7},{7,6},{8,9},{9,8},{10,11... | collective-permute-start | bytes 1990664 | tf_op jit(solution)/shard_map/ppermute | solution.py:629
  81.6 3.0 %collective-permute-start.9 = (bf16[1296,256]{1,0:T(8,128)(2,1)S(1)}, bf16[1296,256]{1,0:T(8,128)(2,1)S(1)}, u32[]{:S(2)}, u32[]{:S(2)}) collective-permute-start(bf16[1296,256]{1,0:T(8,128)(2,1)S(1)} %bitcast.57), channel_id=1, source_target_pairs={{0,1},{1,0},{2,3},{3,2},{4,5},{5,4},{6,7},{7,6},{8,9},{9,8},{10,11... | collective-permute-start | bytes 1990664 | tf_op jit(solution)/shard_map/ppermute | solution.py:629
  82.1 9.4 %collective-permute-start.12 = (bf16[16,128]{1,0:T(8,128)(2,1)S(1)}, bf16[16,128]{1,0:T(8,128)(2,1)S(1)}, u32[]{:S(2)}, u32[]{:S(2)}) collective-permute-start(bf16[16,128]{1,0:T(8,128)(2,1)S(1)} %get-tuple-element.84), channel_id=1, source_target_pairs={{0,30},{2,28},{4,26},{6,24},{8,22},{10,20},{12,18},{14,16},{16,14}... | collective-permute-start | bytes 12296 | tf_op jit(solution)/shard_map/ppermute | solution.py:623
